TPU v7x, 32 devices: a whole 2x2x4 slice. The times are simulated.
32 devices in a mesh: row: 8 (over y, x, core), col: 4 (over z).
Axes of the slice: x: 2, y: 2, z: 4, core: 2. Of those that a mesh axis runs over, the one named last changes fastest.
Arguments:
- top_inverse: bfloat16 [8, 4, 8, 4, 128, 128], P('row', None, None, 'col'), as said below
- upper_panel: bfloat16 [3, 8, 4, 128, 128], P(None, 'row', 'col'), may hold values from -0.25 to 0.25
- upper_pattern: int32 [3, 8, 4], P(None, 'row', 'col'), may hold values from 0 to 1
- upper_diagonal: float32 [3, 128, 128], replicated, may hold values from -6 to 6
- lower_panel: bfloat16 [8, 8, 4, 128, 128], P(None, 'row', 'col'), may hold values from -0.25 to 0.25
- lower_pattern: int32 [8, 8, 4], P(None, 'row', 'col'), may hold values from 0 to 1, as said below
- parents: int32 [8], replicated, may hold values from 0 to 2, as said below
- parent_panel: bfloat16 [8, 128, 128], replicated, may hold values from -0.5 to 0.5
- lower_diagonal: float32 [8, 128, 128], replicated, may hold values from -6 to 6
Outputs:
- upper_columns: bfloat16 [3, 8, 4, 128, 128], P(None, 'row', 'col')
- upper_blocks: float32 [3, 128, 128], replicated
- lower_columns: bfloat16 [8, 8, 4, 128, 128], P(None, 'row', 'col')
- lower_cross: float32 [8, 128, 128], replicated
- lower_blocks: float32 [8, 128, 128], replicated
Inputs may be any that keep to these rules, and one draw needn't show every extreme that they name: top_inverse is symmetric: block (I, J) is the transpose of block (J, I). `lower_pattern`: A second-level pattern is zero wherever the pattern of its parent is zero. `parents`: every first-level supernode is the parent of some second-level supernode.
All inputs are finite; a program needn't handle non-finite values.
Results may differ from a plain program's by a relative error of at most 0.0041.
Values may be sent and summed in bfloat16 or wider, within the bound.
No kernel may reach another device: no remote copies, remote signals or barrier semaphores. Data moves between devices by JAX's collectives and lax.ppermute only.
A program may use at most 128 MiB of HBM per device.

v0:
```python
import jax
import jax.numpy as jnp
from jax import lax
from jax.sharding import PartitionSpec as P

HIGH = lax.Precision.HIGHEST


def by_cols(top_inverse, panel):
    partial_value = jnp.einsum(
        "aibjxy,kaixz->bjkyz",
        top_inverse,
        lax.all_gather(panel, "col", axis=2, tiled=True),
        preferred_element_type=jnp.float32,
    )
    reduced = lax.psum_scatter(partial_value, "row", scatter_dimension=0, tiled=True)
    return jnp.transpose(reduced, (2, 0, 1, 3, 4))


def upper_part(upper_product, upper_mask, upper_masked, lower_masked, parents):
    upper_columns = (-upper_product * upper_mask).astype(jnp.bfloat16)
    selected = jnp.take(upper_columns, parents, axis=0)
    local_upper = jnp.einsum(
        "ktsxy,ktsxz->kyz", upper_masked, upper_columns, preferred_element_type=jnp.float32
    )
    local_cross = jnp.einsum(
        "mtsxy,mtsxz->myz", selected, lower_masked, preferred_element_type=jnp.float32
    )
    return (upper_columns, selected, local_upper, local_cross)


def lower_part(lower_product, selected, parent_panel, lower_mask, lower_masked):
    extension = jnp.einsum(
        "mtsxy,myz->mtsxz", selected, parent_panel, preferred_element_type=jnp.float32
    )
    lower_columns = (-(lower_product + extension) * lower_mask).astype(jnp.bfloat16)
    local_lower = jnp.einsum(
        "mtsxy,mtsxz->myz", lower_masked, lower_columns, preferred_element_type=jnp.float32
    )
    return (lower_columns, local_lower)


def per_device(
    top_inverse,
    upper_panel,
    upper_pattern,
    upper_diagonal,
    lower_panel,
    lower_pattern,
    parents,
    parent_panel,
    lower_diagonal,
):
    upper_mask = upper_pattern.astype(jnp.float32)[:, :, :, None, None]
    upper_masked = upper_panel * upper_mask.astype(jnp.bfloat16)
    lower_mask = lower_pattern.astype(jnp.float32)[:, :, :, None, None]
    lower_masked = lower_panel * lower_mask.astype(jnp.bfloat16)
    upper_product = by_cols(top_inverse, upper_masked)
    upper_columns, selected, local_upper, local_cross = upper_part(
        upper_product, upper_mask, upper_masked, lower_masked, parents
    )
    summed_upper, summed_cross = lax.psum((local_upper, local_cross), ("row", "col"))
    lower_product = by_cols(top_inverse, lower_masked)
    lower_columns, local_lower = lower_part(
        lower_product, selected, parent_panel, lower_mask, lower_masked
    )
    summed_lower = lax.psum(local_lower, ("row", "col"))
    upper_blocks = upper_diagonal - summed_upper
    panel_wide = parent_panel.astype(jnp.float32)
    parent_blocks = jnp.take(upper_blocks, parents, axis=0)
    lower_cross = -summed_cross - jnp.einsum(
        "mxy,myz->mxz", parent_blocks, panel_wide, precision=HIGH
    )
    lower_blocks = (
        lower_diagonal
        - summed_lower
        - jnp.einsum("myx,myz->mxz", panel_wide, lower_cross, precision=HIGH)
    )
    return (upper_columns, upper_blocks, lower_columns, lower_cross, lower_blocks)


def solution(mesh):
    return jax.shard_map(
        per_device,
        mesh=mesh,
        in_specs=(
            P("row", None, None, "col", None, None),
            P(None, "row", "col", None, None),
            P(None, "row", "col"),
            P(),
            P(None, "row", "col", None, None),
            P(None, "row", "col"),
            P(),
            P(),
            P(),
        ),
        out_specs=(
            P(None, "row", "col", None, None),
            P(),
            P(None, "row", "col", None, None),
            P(),
            P(),
        ),
        check_vma=False,
    )
```

profile of v0, /device:TPU:0, one launch (start us, length us, event | category | flops | bytes accessed | tf_op | source)
XLA Modules:
  0.0 298.5 jit_solution(9543165021093269581)
XLA Ops:
  7.2 0.0 copy-start
  7.2 0.0 all-gather.2.cloned.1.call-start
  7.2 1.2 copy.58
  8.4 0.7 convert_bitcast_fusion
  9.1 0.8 broadcast_multiply_fusion
  9.9 0.0 all-gather.2.cloned.1.call-update
  9.9 0.0 all-reduce.9.cloned.1.call-start
  10.0 1.0 copy.55
  11.0 0.7 fusion.23
  11.6 0.1 broadcast_multiply_fusion.1
  11.7 19.5 %all_gather.6 = bf16[3,1,4,128,128]{3,4,2,0,1:T(8,128)(2,1)S(1)} all-gather(bf16[3,1,1,128,128]{3,4,2,0,1:T(8,128)(2,1)S(1)} %broadcast_multiply_fusion.1), channel_id=1, replica_groups=mesh['row'=8,'col'=4] {'col'}, dimensions={2}, use_global_device_ids=true | all-gather | bytes 491520 | tf_op jit(solution)/shard_map/all_gather | solution.py:13
  31.2 0.0 copy-done
  31.2 1.8 convolution_bitcast_fusion.1
  33.0 10.4 %all-gather.2.cloned.1.call-done = bf16[8,1,4,128,128]{3,4,2,0,1:T(8,128)(2,1)} async-done(((bf16[8,1,1,128,128]{3,4,2,0,1:T(8,128)(2,1)}), bf16[8,1,4,128,128]{3,4,2,0,1:T(8,128)(2,1)}) %all-gather.2.cloned.1.call-update) | async-done | bytes 1048592 | tf_op jit(solution)/shard_map/all_gather | solution.py:13
  43.4 4.4 %convolution_bitcast_fusion = f32[8,1,8,128,128]{3,4,0,2,1:T(8,128)} fusion(bf16[8,1,4,128,128]{3,4,2,0,1:T(8,128)(2,1)} %all-gather.2.cloned.1.call-done, bf16[1,4,8,1,128,128]{5,4,3,2,1,0:T(8,128)(2,1)S(1)} %copy-done), kind=kOutput, calls=%fused_computation.2 | convolution fusion | flops 1073741824 | bytes 6291456 | tf_op jit(solution)/shard_map/aibjxy,kaixz->bjkyz/dot_general | solution.py:10
  47.8 0.0 copy-start.9
  47.8 0.0 copy-start.8
  47.8 0.0 copy-start.1
  47.8 0.0 copy-start.3
  47.8 0.0 all-reduce.9.cloned.1.call-update
  47.9 0.0 all-reduce.7.cloned.1.call-start
  47.9 0.6 copy-done.9
  48.5 0.6 dynamic-slice
  49.1 0.0 copy-done.8
  49.1 97.1 %all-reduce.9.cloned.1.call-done = (f32[8,1,3,128,128]{3,4,0,2,1:T(8,128)}, f32[8,1,8,128,128]{3,4,0,2,1:T(8,128)}) async-done(((f32[8,1,3,128,128]{3,4,0,2,1:T(8,128)}, f32[8,1,8,128,128]{3,4,0,2,1:T(8,128)}), (f32[8,1,3,128,128]{3,4,0,2,1:T(8,128)}, f32[8,1,8,128,128]{3,4,0,2,1:T(8,128)})) %all-reduce.9.cloned.1.call-update) | async-done | bytes 5767184
  146.2 1.6 constant_dynamic-slice_fusion.1
  147.8 0.0 copy-start.7
  147.8 0.1 copy.57
  147.9 0.7 fusion.29
  148.7 0.9 fusion.19
  149.6 1.7 constant_dynamic-slice_fusion
  151.3 0.2 copy.60
  151.5 0.6 gather_fusion
  152.1 0.0 copy-done.1
  152.1 0.0 copy-start.6
  152.2 1.2 fusion.13
  153.4 0.0 copy-done.3
  153.4 0.3 fusion.3
  153.7 0.0 copy-start.5
  153.7 1.0 fusion.11
  154.7 0.0 all-reduce.7.cloned.1.call-update
  154.7 131.7 %all-reduce.7.cloned.1.call-done = (f32[3,128,128]{2,1,0:T(8,128)}, f32[8,128,128]{2,1,0:T(8,128)}, f32[8,128,128]{2,1,0:T(8,128)}) async-done(((f32[3,128,128]{2,1,0:T(8,128)}, f32[8,128,128]{2,1,0:T(8,128)}, f32[8,128,128]{2,1,0:T(8,128)}), (f32[3,128,128]{2,1,0:T(8,128)}, f32[8,128,128]{2,1,0:T(8,128)}, f32[8,128,128]{2,1,0:T(8,128)})) %all-reduce.7.cloned.1.call-update) | async-done | bytes 1245200 | tf_op jit(solution)/shard_map/psum | solution.py:62
  286.4 0.0 copy-done.7
  286.4 0.9 sub.12
  287.4 0.0 copy-start.2
  287.4 0.6 gather_fusion.1
  288.0 1.5 convolution_subtract_fusion
  289.5 0.0 copy-start.4
  289.5 0.0 copy-done.6
  289.5 2.5 fusion.2
  292.0 0.0 copy-done.5
  292.0 0.0 copy-done.2
  292.0 0.0 copy-done.4
  (3 shorter events, 0.0 us)
Async XLA Ops:
  7.2 24.0 %copy-start = (bf16[1,4,8,1,128,128]{5,4,3,2,1,0:T(8,128)(2,1)S(1)}, bf16[1,4,8,1,128,128]{5,4,3,2,1,0:T(8,128)(2,1)}, u32[]{:S(2)}) copy-start(bf16[1,4,8,1,128,128]{5,4,3,2,1,0:T(8,128)(2,1)} %param.9) | copy-start | bytes 3145732
  7.2 36.2 %all-gather.2.cloned.1.call-start = ((), (), s32[]{:S(2)}) async-start(), calls=%async_computation | async-start | bytes 1310720 | tf_op jit(solution)/shard_map/all_gather | solution.py:13
  9.9 136.3 %all-reduce.9.cloned.1.call-start = ((), (), s32[]{:S(2)}) async-start(), calls=%async_computation.2 | async-start | bytes 11534336
  47.8 0.7 copy-start.9
  47.8 1.2 copy-start.8
  47.8 104.3 %copy-start.1 = (bf16[8,1,1,128,128]{3,4,2,0,1:T(8,128)(2,1)S(1)}, bf16[8,1,1,128,128]{3,4,2,0,1:T(8,128)(2,1)}, u32[]{:S(2)}) copy-start(bf16[8,1,1,128,128]{3,4,2,0,1:T(8,128)(2,1)} %broadcast_multiply_fusion) | copy-start | bytes 786436
  47.8 105.6 %copy-start.3 = (bf16[8,128,128]{2,1,0:T(8,128)(2,1)S(1)}, bf16[8,128,128]{2,1,0:T(8,128)(2,1)}, u32[]{:S(2)}) copy-start(bf16[8,128,128]{2,1,0:T(8,128)(2,1)} %param.16) | copy-start | bytes 786436
  47.9 238.5 %all-reduce.7.cloned.1.call-start = ((), (), s32[]{:S(2)}) async-start(), calls=%async_computation.1 | async-start | bytes 2490368 | tf_op jit(solution)/shard_map/psum | solution.py:62
  147.8 138.6 %copy-start.7 = (f32[3,128,128]{2,1,0:T(8,128)S(1)}, f32[3,128,128]{2,1,0:T(8,128)}, u32[]{:S(2)}) copy-start(f32[3,128,128]{2,1,0:T(8,128)} %param.12) | copy-start | bytes 589828
  152.1 137.3 %copy-start.6 = (f32[8,128,128]{2,1,0:T(8,128)S(1)}, f32[8,128,128]{2,1,0:T(8,128)}, u32[]{:S(2)}) copy-start(f32[8,128,128]{2,1,0:T(8,128)} %param.17) | copy-start | bytes 1572868
  153.7 138.3 %copy-start.5 = (bf16[8,128,128]{2,1,0:T(8,128)(2,1)}, bf16[8,128,128]{2,1,0:T(8,128)(2,1)S(1)}, u32[]{:S(2)}) copy-start(bf16[8,128,128]{2,1,0:T(8,128)(2,1)S(1)} %fusion.3) | copy-start | bytes 786436
  287.4 4.6 %copy-start.2 = (f32[3,128,128]{2,1,0:T(8,128)}, f32[3,128,128]{2,1,0:T(8,128)S(1)}, u32[]{:S(2)}) copy-start(f32[3,128,128]{2,1,0:T(8,128)S(1)} %sub.12) | copy-start | bytes 589828
  289.5 2.5 copy-start.4
Sparse Core Ops, SparseCore 0:
  10.2 33.1 all-gather.1
  48.0 98.1 all-reduce.8
  154.8 131.5 all-reduce.6
where the time goes:
time: 299 us
  waiting for transfers between devices  239 us (80%)
  blocking collectives  19.5 us (7%)
  between operations  13.9 us (5%)
  matrix products  13.7 us (5%)
  local copies, waits for them, and re-layouts  8.23 us (3%)
  other arithmetic  3.91 us (1%)
    psum x1, waiting for transfers between devices, per_device(): lax.psum((local_upper, local_cross), ('row', 'col'))  132 us
    unnamed x4, waiting for transfers between devices  97.2 us
    all_gather x1, blocking collectives, by_cols(): lax.all_gather(panel, 'col', axis=2, tiled=True)  19.5 us
    all_gather x1, waiting for transfers between devices, by_cols(): lax.all_gather(panel, 'col', axis=2, tiled=True)  10.4 us
    unnamed x25, local copies, waits for them, and re-layouts  6.73 us
    dot_general x2, matrix products, by_cols(): jnp.einsum('aibjxy,kaixz->bjkyz', top_inverse, lax.all_gather(panel, 'col...  6.22 us
  transfers between devices with their start and end apart: 3, of which 3 were waited for; matrix products, arithmetic and copies ran while one was open for 1% of the time, Pallas kernels for 0%

commit v1 on v0

v1 whole, which is shorter than its diff:
```python
import jax
import jax.numpy as jnp
from jax import lax
from jax.sharding import PartitionSpec as P

HIGH = lax.Precision.HIGHEST
ALL = ("row", "col")


def all_sum(blocks, count):
    shape = blocks.shape
    flat = blocks.reshape(-1, shape[-1])
    rows = flat.shape[0]
    chunk = -(-rows // (16 * count)) * 16
    flat = jnp.pad(flat.astype(jnp.bfloat16), ((0, chunk * count - rows), (0, 0)))
    parts = lax.all_to_all(
        flat.reshape(count, chunk, shape[-1]), ALL, split_axis=0, concat_axis=0, tiled=True
    )
    mine = jnp.sum(parts.astype(jnp.float32), axis=0).astype(jnp.bfloat16)
    spread = jnp.broadcast_to(mine[None], (count, chunk, shape[-1]))
    whole = lax.all_to_all(spread, ALL, split_axis=0, concat_axis=0, tiled=True)
    return whole.reshape(chunk * count, shape[-1])[:rows].reshape(shape).astype(jnp.float32)


def per_device(
    top_inverse,
    upper_panel,
    upper_pattern,
    upper_diagonal,
    lower_panel,
    lower_pattern,
    parents,
    parent_panel,
    lower_diagonal,
):
    count = lax.axis_size("row") * lax.axis_size("col")
    uppers = upper_panel.shape[0]
    block = upper_panel.shape[-1]
    upper_panel = upper_panel.reshape(-1, block, block)
    lower_panel = lower_panel.reshape(-1, block, block)
    upper_mask = upper_pattern.reshape(-1, 1, 1).astype(jnp.float32)
    lower_mask = lower_pattern.reshape(-1, 1, 1).astype(jnp.float32)
    masked = jnp.concatenate(
        [
            upper_panel * upper_mask.astype(jnp.bfloat16),
            lower_panel * lower_mask.astype(jnp.bfloat16),
        ]
    )
    upper_masked, lower_masked = masked[:uppers], masked[uppers:]
    gathered = lax.all_gather(masked, "col", axis=0)
    partial_value = jnp.einsum(
        "bjxy,bkxz->jkyz",
        top_inverse[0, :, :, 0],
        gathered,
        preferred_element_type=jnp.float32,
    ).astype(jnp.bfloat16)
    parts = lax.all_to_all(partial_value, "row", split_axis=0, concat_axis=0, tiled=True)
    product = jnp.sum(parts.astype(jnp.float32), axis=0)

    upper_columns = (-product[:uppers] * upper_mask).astype(jnp.bfloat16)
    selected = jnp.take(upper_columns, parents, axis=0)
    local_upper = jnp.einsum(
        "kxy,kxz->kyz", upper_masked, upper_columns, preferred_element_type=jnp.float32
    )
    local_cross = jnp.einsum(
        "mxy,mxz->myz", selected, lower_masked, preferred_element_type=jnp.float32
    )
    extension = jnp.einsum(
        "mxy,myz->mxz", selected, parent_panel, preferred_element_type=jnp.float32
    )
    lower_columns = (-(product[uppers:] + extension) * lower_mask).astype(jnp.bfloat16)
    local_lower = jnp.einsum(
        "mxy,mxz->myz", lower_masked, lower_columns, preferred_element_type=jnp.float32
    )
    sums = all_sum(jnp.concatenate([local_upper, local_cross, local_lower]), count)
    lowers = lower_panel.shape[0]
    summed_upper = sums[:uppers]
    summed_cross = sums[uppers : uppers + lowers]
    summed_lower = sums[uppers + lowers :]
    upper_blocks = upper_diagonal - summed_upper
    panel_wide = parent_panel.astype(jnp.float32)
    parent_blocks = jnp.take(upper_blocks, parents, axis=0)
    lower_cross = -summed_cross - jnp.einsum(
        "mxy,myz->mxz", parent_blocks, panel_wide, precision=HIGH
    )
    lower_blocks = (
        lower_diagonal
        - summed_lower
        - jnp.einsum("myx,myz->mxz", panel_wide, lower_cross, precision=HIGH)
    )
    return (
        upper_columns[:, None, None],
        upper_blocks,
        lower_columns[:, None, None],
        lower_cross,
        lower_blocks,
    )


def solution(mesh):
    return jax.shard_map(
        per_device,
        mesh=mesh,
        in_specs=(
            P("row", None, None, "col", None, None),
            P(None, "row", "col", None, None),
            P(None, "row", "col"),
            P(),
            P(None, "row", "col", None, None),
            P(None, "row", "col"),
            P(),
            P(),
            P(),
        ),
        out_specs=(
            P(None, "row", "col", None, None),
            P(),
            P(None, "row", "col", None, None),
            P(),
            P(),
        ),
        check_vma=False,
    )
```

time: 299 us -> 155 us (0.52)
  waiting for transfers between devices: 239 us -> 88.8 us
  starting transfers between devices: 0.12 us -> 8.86 us
  matrix products: 13.7 us -> 6.42 us
  other arithmetic: 3.91 us -> 8.56 us
    psum x1 -> x0, waiting for transfers between devices: 132 us -> none  [per_device(): lax.psum((local_upper, local_cross), ('row', 'col'))]
    unnamed x4 -> x1, waiting for transfers between devices: 97.2 us -> 0.02 us
    all_to_all x0 -> x2, waiting for transfers between devices: none -> 51 us  [the longest x1 35 us: per_device(): lax.all_to_all(partial_value, 'row', split_axis=0, concat_axis=0, tiled=T...]
    all_gather x1, waiting for transfers between devices: 10.4 us -> 37.8 us  [per_device(): gathered = lax.all_gather(masked, 'col', axis=0)]
    all_gather x1 -> x0, blocking collectives: 19.5 us -> none  [by_cols(): lax.all_gather(panel, 'col', axis=2, tiled=True)]
    all_to_all x0 -> x1, blocking collectives: none -> 18.6 us  [all_sum(): lax.all_to_all(flat.reshape(count, chunk, shape[-1]), ALL, split_axis=0,...]
    all_to_all x0 -> x2, starting transfers between devices: none -> 8.82 us  [the longest x1 4.56 us: per_device(): lax.all_to_all(partial_value, 'row', split_axis=0, concat_axis=0, tiled=T...]
    dot_general x6 -> x5, matrix products: 9.65 us -> 4.18 us  [the longest x1 3.05 us: per_device(): jnp.einsum('bjxy,bkxz->jkyz', top_inverse[0, :, :, 0], gathered, preferre...]
where the time goes in v1:
time: 155 us; the launch traced here: 153 us
  waiting for transfers between devices  88.8 us (57%)
  blocking collectives  18.6 us (12%)
  between operations  14.3 us (9%)
  starting transfers between devices  8.86 us (6%)
  other arithmetic  8.56 us (6%)
  local copies, waits for them, and re-layouts  7.67 us (5%)
  matrix products  6.42 us (4%)
    all_gather x1, waiting for transfers between devices, per_device(): gathered = lax.all_gather(masked, 'col', axis=0)  37.8 us
    all_to_all x1, waiting for transfers between devices, per_device(): lax.all_to_all(partial_value, 'row', split_axis=0, concat_axis=0, tiled=T...  35 us
    all_to_all x1, blocking collectives, all_sum(): lax.all_to_all(flat.reshape(count, chunk, shape[-1]), ALL, split_axis=0,...  18.6 us
    all_to_all x1, waiting for transfers between devices, all_sum(): whole = lax.all_to_all(spread, ALL, split_axis=0, concat_axis=0, tiled=True)  16 us
    all_to_all x1, starting transfers between devices, per_device(): lax.all_to_all(partial_value, 'row', split_axis=0, concat_axis=0, tiled=T...  4.56 us
    all_to_all x1, starting transfers between devices, all_sum(): whole = lax.all_to_all(spread, ALL, split_axis=0, concat_axis=0, tiled=True)  4.27 us
  transfers between devices with their start and end apart: 3, of which 3 were waited for; matrix products, arithmetic and copies ran while one was open for 1% of the time, Pallas kernels for 0%

profile of v1, /device:TPU:0, one launch (start us, length us, event | category | flops | bytes accessed | tf_op | source)
XLA Modules:
  0.0 153.2 jit_solution(11540445407967752212)
XLA Ops:
  7.2 0.0 copy-start
  7.2 0.0 all-gather.3.cloned.1.call-start
  7.2 0.7 convert_bitcast_fusion.3
  8.0 0.7 convert_bitcast_fusion.1
  8.6 1.0 bitcast_multiply_fusion
  9.7 1.0 bitcast_multiply_fusion.1
  10.6 0.8 pad_maximum_fusion.1
  11.4 0.0 all-gather.3.cloned.1.call-update
  11.4 37.8 %all-gather.3.cloned.1.call-done = bf16[44,128,128]{2,1,0:T(8,128)(2,1)} async-done(((bf16[11,128,128]{2,1,0:T(8,128)(2,1)}), bf16[44,128,128]{2,1,0:T(8,128)(2,1)}) %all-gather.3.cloned.1.call-update) | async-done | bytes 1441808 | tf_op jit(solution)/shard_map/all_gather | solution.py:50
  49.2 0.0 copy-done
  49.2 3.0 %fusion = bf16[8,11,128,128]{2,3,0,1:T(8,128)(2,1)S(1)} fusion(bf16[4,11,128,128,1]{3,2,1,0,4:T(8,128)(2,1)} %bitcast.62, bf16[1,4,8,1,128,128]{5,4,3,2,1,0:T(8,128)(2,1)S(1)} %copy-done), kind=kOutput, calls=%fused_computation.4 | convolution fusion | flops 1477836800 | bytes 5373952 | tf_op jit(solution)/shard_map/bjxy,bkxz->jkyz/dot_general | solution.py:51
  52.3 1.8 %copy.67 = bf16[8,11,128,128]{2,3,1,0:T(8,128)(2,1)} copy(bf16[8,11,128,128]{2,3,0,1:T(8,128)(2,1)S(1)} %fusion) | data formatting | bytes 5767168 | tf_op jit(solution)/shard_map/convert_element_type | solution.py:56
  54.1 0.0 copy-start.7
  54.1 4.6 %all-to-all-start = ((bf16[8,11,128,128]{2,3,1,0:T(8,128)(2,1)}), bf16[8,11,128,128]{2,3,1,0:T(8,128)(2,1)}, u32[]{:S(2)}, u32[]{:S(2)}) async-start(bf16[8,11,128,128]{2,3,1,0:T(8,128)(2,1)} %copy.67), calls=%async_computation | async-start | bytes 5767168 | tf_op jit(solution)/shard_map/all_to_all | solution.py:57
  58.7 0.0 copy-done.7
  58.7 35.0 %all-to-all-done = bf16[8,11,128,128]{2,3,1,0:T(8,128)(2,1)} async-done(((bf16[8,11,128,128]{2,3,1,0:T(8,128)(2,1)}), bf16[8,11,128,128]{2,3,1,0:T(8,128)(2,1)}, u32[]{:S(2)}, u32[]{:S(2)}) %all-to-all-start) | async-done | bytes 2883616 | tf_op jit(solution)/shard_map/all_to_all | solution.py:57
  93.7 2.4 %convert_reduce_fusion = f32[11,128,128]{1,2,0:T(8,128)S(1)} fusion(bf16[8,11,128,128]{2,3,1,0:T(8,128)(2,1)} %all-to-all-done), kind=kLoop, calls=%fused_computation.3 | loop fusion | flops 2703360 | bytes 3604480 | tf_op jit(solution)/shard_map/reduce_sum | solution.py:58
  96.2 0.1 copy.89
  96.4 0.0 copy-start.2
  96.4 0.2 copy.90
  96.6 0.1 multiply_convert_fusion
  96.7 0.2 convolution_convert_fusion.2
  96.9 0.6 gather_fusion
  97.5 0.4 convolution_convert_fusion.1
  97.9 0.0 copy-done.2
  97.9 0.3 fusion.5
  98.2 0.0 copy-start.4
  98.2 0.3 convolution_convert_fusion
  98.5 0.1 pad_maximum_fusion
  98.6 0.3 copy-done.4
  98.9 18.6 %all_to_all.15 = bf16[32,80,128]{2,1,0:T(8,128)(2,1)S(1)} all-to-all(bf16[32,80,128]{2,1,0:T(8,128)(2,1)S(1)} %bitcast.55), channel_id=1, replica_groups=mesh['row'=8,'col'=4] {'row','col'}, dimensions={0} | all-to-all | bytes 1310720 | tf_op jit(solution)/shard_map/all_to_all | solution.py:16
  117.5 0.0 copy-start.5
  117.5 0.1 reduce_sum.22
  117.6 0.9 broadcast_in_dim.36
  118.5 4.3 %all-to-all-start.2 = ((bf16[32,80,128]{2,1,0:T(8,128)(2,1)}), bf16[32,80,128]{2,1,0:T(8,128)(2,1)S(1)}, u32[]{:S(2)}, u32[]{:S(2)}) async-start(bf16[32,80,128]{2,1,0:T(8,128)(2,1)} %broadcast_in_dim.36), calls=%async_computation.2 | async-start | bytes 1310720 | tf_op jit(solution)/shard_map/all_to_all | solution.py:21
  122.8 0.0 copy-done.5
  122.8 0.2 copy.74
  123.0 0.7 fusion.24
  123.7 16.0 %all-to-all-done.2 = bf16[32,80,128]{2,1,0:T(8,128)(2,1)S(1)} async-done(((bf16[32,80,128]{2,1,0:T(8,128)(2,1)}), bf16[32,80,128]{2,1,0:T(8,128)(2,1)S(1)}, u32[]{:S(2)}, u32[]{:S(2)}) %all-to-all-start.2) | async-done | bytes 655392 | tf_op jit(solution)/shard_map/all_to_all | solution.py:21
  139.7 0.1 slice_convert_fusion
  139.8 0.0 copy-start.6
  139.8 0.9 fusion.14
  140.7 0.0 copy-done.6
  140.8 0.0 copy-start.1
  140.8 1.4 gather_fusion.1
  142.1 0.2 copy.75
  142.4 1.6 %convolution_subtract_fusion = f32[8,128,128]{2,1,0:T(8,128)S(1)} fusion(f32[8,128,128]{2,1,0:T(8,128)} %bitcast.59, bf16[8,128,128]{2,1,0:T(8,128)(2,1)S(1)} %copy-done.2, f32[8,128,128]{2,1,0:T(8,128)} %gather_fusion.1, pred[8]{0:T(512)(128)(4,1)S(1)} %compare_and_fusion), kind=kOutput, calls=%fused_computation.11 | convolution fusion | flops 201588736 | bytes 1835016 | tf_op jit(solution)/shard_map/mxy,myz->mxz/dot_general | solution.py:83
  144.0 0.0 copy-done.1
  144.0 0.0 copy-start.3
  144.0 0.8 copy-done.3
  144.8 0.6 fusion.4
  145.4 1.0 copy.79
  (8 shorter events, 0.2 us)
Async XLA Ops:
  7.2 42.1 %copy-start = (bf16[1,4,8,1,128,128]{5,4,3,2,1,0:T(8,128)(2,1)S(1)}, bf16[1,4,8,1,128,128]{5,4,3,2,1,0:T(8,128)(2,1)}, u32[]{:S(2)}) copy-start(bf16[1,4,8,1,128,128]{5,4,3,2,1,0:T(8,128)(2,1)} %param.9) | copy-start | bytes 3145732
  7.2 42.0 %all-gather.3.cloned.1.call-start = ((), (), s32[]{:S(2)}) async-start(), calls=%async_computation.3 | async-start | bytes 1802240 | tf_op jit(solution)/shard_map/all_gather | solution.py:50
  54.1 4.6 %copy-start.7 = (s32[8]{0:T(128)S(1)}, s32[8]{0:T(128)}, u32[]{:S(2)}) copy-start(s32[8]{0:T(128)} %param.15) | copy-start | bytes 100
  54.1 39.6 %all-to-all-start = ((bf16[8,11,128,128]{2,3,1,0:T(8,128)(2,1)}), bf16[8,11,128,128]{2,3,1,0:T(8,128)(2,1)}, u32[]{:S(2)}, u32[]{:S(2)}) async-start(bf16[8,11,128,128]{2,3,1,0:T(8,128)(2,1)} %copy.67), calls=%async_computation | async-start | bytes 5767168 | tf_op jit(solution)/shard_map/all_to_all | solution.py:57
  96.4 1.5 copy-start.2
  98.2 0.7 copy-start.4
  117.5 5.3 %copy-start.5 = (f32[8,128,128]{2,1,0:T(8,128)S(1)}, f32[8,128,128]{2,1,0:T(8,128)}, u32[]{:S(2)}) copy-start(f32[8,128,128]{2,1,0:T(8,128)} %param.17) | copy-start | bytes 1572868
  118.5 21.2 %all-to-all-start.2 = ((bf16[32,80,128]{2,1,0:T(8,128)(2,1)}), bf16[32,80,128]{2,1,0:T(8,128)(2,1)S(1)}, u32[]{:S(2)}, u32[]{:S(2)}) async-start(bf16[32,80,128]{2,1,0:T(8,128)(2,1)} %broadcast_in_dim.36), calls=%async_computation.2 | async-start | bytes 1310720 | tf_op jit(solution)/shard_map/all_to_all | solution.py:21
  139.8 0.9 copy-start.6
  140.8 3.2 %copy-start.1 = (f32[3,128,128]{2,1,0:T(8,128)}, f32[3,128,128]{2,1,0:T(8,128)S(1)}, u32[]{:S(2)}) copy-start(f32[3,128,128]{2,1,0:T(8,128)S(1)} %sub.12) | copy-start | bytes 589828
  144.0 0.8 copy-start.3
Sparse Core Ops, SparseCore 0:
  11.6 37.6 all-gather.2

commit v2 on v1

v2 whole, which is shorter than its diff:
```python
import jax
import jax.numpy as jnp
from jax import lax
from jax.sharding import PartitionSpec as P

HIGH = lax.Precision.HIGHEST
WIRE = jnp.bfloat16


def bits_of(axis):
    return lax.axis_size(axis).bit_length() - 1


def flip(value, axis, bit):
    size = lax.axis_size(axis)
    return lax.ppermute(value, axis, [(i, i ^ (1 << bit)) for i in range(size)])


def shift(value, axis, step):
    size = lax.axis_size(axis)
    return lax.ppermute(value, axis, [(i, (i + step) % size) for i in range(size)])


def gather_shifts(value, axis):
    size = lax.axis_size(axis)
    me = lax.axis_index(axis)
    pieces = jnp.stack([value] + [shift(value, axis, s) for s in range(1, size)])
    return jnp.take(pieces, (me - jnp.arange(size)) % size, axis=0)


def scatter_shifts(parts, axis):
    size = lax.axis_size(axis)
    me = lax.axis_index(axis)
    total = lax.dynamic_index_in_dim(parts, me, 0, keepdims=False)
    for s in range(1, size):
        piece = lax.dynamic_index_in_dim(parts, (me + s) % size, 0, keepdims=False)
        total = total + shift(piece, axis, s)
    return total


def scatter_halves(parts, axis, order):
    me = lax.axis_index(axis)
    left = sorted(order, reverse=True)
    value = parts.reshape((2,) * len(left) + parts.shape[1:])
    for bit in order:
        place = left.index(bit)
        mine = (me >> bit) & 1
        away = lax.dynamic_index_in_dim(value, 1 - mine, place, keepdims=False)
        keep = lax.dynamic_index_in_dim(value, mine, place, keepdims=False)
        kind = jnp.float32 if bit == 0 else WIRE
        value = keep.astype(jnp.float32) + flip(away.astype(kind), axis, bit).astype(jnp.float32)
        left.remove(bit)
    return value


def gather_doubles(value, axis, order):
    me = lax.axis_index(axis)
    done = []
    for bit in order:
        done = sorted(done + [bit], reverse=True)
        place = done.index(bit)
        other = flip(value, axis, bit)
        mine = (me >> bit) & 1
        value = jnp.stack(
            [jnp.where(mine == 0, value, other), jnp.where(mine == 0, other, value)], axis=place
        )
    return value


def all_sum(blocks):
    shape = blocks.shape
    rows_n, cols_n = lax.axis_size("row"), lax.axis_size("col")
    count = rows_n * cols_n
    flat = blocks.reshape(-1, shape[-1])
    rows = flat.shape[0]
    chunk = -(-rows // (16 * count)) * 16
    flat = jnp.pad(flat, ((0, chunk * count - rows), (0, 0)))
    parts = flat.reshape(rows_n, cols_n * chunk, shape[-1])
    order = list(range(bits_of("row")))
    part = scatter_halves(parts, "row", order)
    part = scatter_shifts(part.reshape(cols_n, chunk, shape[-1]), "col")
    part = gather_shifts(part.astype(WIRE), "col").reshape(cols_n * chunk, shape[-1])
    whole = gather_doubles(part, "row", order[::-1])
    return whole.reshape(chunk * count, shape[-1])[:rows].reshape(shape).astype(jnp.float32)


def product_parts(top, gathered):
    return jnp.einsum("bjxy,bkxz->jkyz", top, gathered, preferred_element_type=jnp.float32)


def per_device(
    top_inverse,
    upper_panel,
    upper_pattern,
    upper_diagonal,
    lower_panel,
    lower_pattern,
    parents,
    parent_panel,
    lower_diagonal,
):
    uppers, block = upper_panel.shape[0], upper_panel.shape[-1]
    lowers = lower_panel.shape[0]
    top = top_inverse[0, :, :, 0]
    upper_mask = upper_pattern.reshape(-1, 1, 1).astype(jnp.float32)
    lower_mask = lower_pattern.reshape(-1, 1, 1).astype(jnp.float32)
    upper_masked = upper_panel.reshape(-1, block, block) * upper_mask.astype(jnp.bfloat16)
    lower_masked = lower_panel.reshape(-1, block, block) * lower_mask.astype(jnp.bfloat16)
    order = list(range(bits_of("row")))
    turned = order[:1] + order[1:][::-1]

    upper_parts = product_parts(top, gather_shifts(upper_masked, "col"))
    upper_product = scatter_halves(upper_parts, "row", order)
    upper_columns = (-upper_product * upper_mask).astype(jnp.bfloat16)
    selected = jnp.take(upper_columns, parents, axis=0)
    local_upper = jnp.einsum(
        "kxy,kxz->kyz", upper_masked, upper_columns, preferred_element_type=jnp.float32
    )
    local_cross = jnp.einsum(
        "mxy,mxz->myz", selected, lower_masked, preferred_element_type=jnp.float32
    )
    first = all_sum(jnp.concatenate([local_upper, local_cross]))

    lower_parts = product_parts(top, gather_shifts(lower_masked, "col"))
    half = lowers // 2
    lower_product = jnp.concatenate(
        [
            scatter_halves(lower_parts[:, :half], "row", order),
            scatter_halves(lower_parts[:, half:], "row", turned),
        ]
    )
    extension = jnp.einsum(
        "mxy,myz->mxz", selected, parent_panel, preferred_element_type=jnp.float32
    )
    lower_columns = (-(lower_product + extension) * lower_mask).astype(jnp.bfloat16)
    local_lower = jnp.einsum(
        "mxy,mxz->myz", lower_masked, lower_columns, preferred_element_type=jnp.float32
    )
    summed_lower = all_sum(local_lower)

    upper_blocks = upper_diagonal - first[:uppers]
    panel_wide = parent_panel.astype(jnp.float32)
    parent_blocks = jnp.take(upper_blocks, parents, axis=0)
    lower_cross = -first[uppers:] - jnp.einsum(
        "mxy,myz->mxz", parent_blocks, panel_wide, precision=HIGH
    )
    lower_blocks = (
        lower_diagonal
        - summed_lower
        - jnp.einsum("myx,myz->mxz", panel_wide, lower_cross, precision=HIGH)
    )
    return (
        upper_columns[:, None, None],
        upper_blocks,
        lower_columns[:, None, None],
        lower_cross,
        lower_blocks,
    )


def solution(mesh):
    return jax.shard_map(
        per_device,
        mesh=mesh,
        in_specs=(
            P("row", None, None, "col", None, None),
            P(None, "row", "col", None, None),
            P(None, "row", "col"),
            P(),
            P(None, "row", "col", None, None),
            P(None, "row", "col"),
            P(),
            P(),
            P(),
        ),
        out_specs=(
            P(None, "row", "col", None, None),
            P(),
            P(None, "row", "col", None, None),
            P(),
            P(),
        ),
        check_vma=False,
    )
```

time: 155 us -> 145 us (0.935)
  starting transfers between devices: 8.86 us -> 45.6 us
  waiting for transfers between devices: 88.8 us -> 52.6 us
  blocking collectives: 18.6 us -> 0 us
  between operations: 14.3 us -> 1.38 us
  local copies, waits for them, and re-layouts: 7.67 us -> 20.2 us
  other arithmetic: 8.56 us -> 16.1 us
  matrix products: 6.42 us -> 7.99 us
    ppermute x0 -> x39, waiting for transfers between devices: none -> 52.6 us  [the longest x18 29.4 us: shift(): lax.ppermute(value, axis, [(i, (i + step) % size) for i in range(size)])]
    all_to_all x2 -> x0, waiting for transfers between devices: 51 us -> none  [the longest x1 35 us: per_device(): lax.all_to_all(partial_value, 'row', split_axis=0, concat_axis=0, tiled=T...]
    ppermute x0 -> x39, starting transfers between devices: none -> 45.6 us  [the longest x18 29.6 us: shift(): lax.ppermute(value, axis, [(i, (i + step) % size) for i in range(size)])]
    all_gather x1 -> x0, waiting for transfers between devices: 37.8 us -> none  [per_device(): gathered = lax.all_gather(masked, 'col', axis=0)]
    all_to_all x1 -> x0, blocking collectives: 18.6 us -> none  [all_sum(): lax.all_to_all(flat.reshape(count, chunk, shape[-1]), ALL, split_axis=0,...]
    dynamic_slice x0 -> x8, local copies, waits for them, and re-layouts: none -> 9.98 us  [the longest x5 6.15 us: scatter_halves(): keep = lax.dynamic_index_in_dim(value, mine, place, keepdims=False)]
    all_to_all x2 -> x0, starting transfers between devices: 8.82 us -> none  [the longest x1 4.56 us: per_device(): lax.all_to_all(partial_value, 'row', split_axis=0, concat_axis=0, tiled=T...]
    add x0 -> x14, other arithmetic: none -> 5.32 us  [scatter_halves(): keep.astype(jnp.float32)]
  transfers between devices with their start and end apart: 3 -> 39, of which waited for: 3 -> 23; matrix products, arithmetic and copies ran while one was open for 1% -> 26% of each run, Pallas kernels for 0% -> 0%
where the time goes in v2:
time: 145 us; the launch traced here: 144 us
  waiting for transfers between devices  52.6 us (36%)
  starting transfers between devices  45.6 us (31%)
  local copies, waits for them, and re-layouts  20.2 us (14%)
  other arithmetic  16.1 us (11%)
  matrix products  7.99 us (6%)
    ppermute x18, starting transfers between devices, shift(): lax.ppermute(value, axis, [(i, (i + step) % size) for i in range(size)])  29.6 us
    ppermute x18, waiting for transfers between devices, shift(): lax.ppermute(value, axis, [(i, (i + step) % size) for i in range(size)])  29.4 us
    ppermute x21, waiting for transfers between devices, flip(): return lax.ppermute(value, axis, [(i, i ^ 1 << bit) for i in range(size)])  23.1 us
    ppermute x21, starting transfers between devices, flip(): return lax.ppermute(value, axis, [(i, i ^ 1 << bit) for i in range(size)])  16 us
    dynamic_slice x5, local copies, waits for them, and re-layouts, scatter_halves(): keep = lax.dynamic_index_in_dim(value, mine, place, keepdims=False)  6.15 us
    add x14, other arithmetic, scatter_halves(): keep.astype(jnp.float32)  5.32 us
    dynamic_slice x3, local copies, waits for them, and re-layouts, scatter_halves(): away = lax.dynamic_index_in_dim(value, 1 - mine, place, keepdims=False)  3.83 us
    unnamed x32, local copies, waits for them, and re-layouts  3.74 us
  transfers between devices with their start and end apart: 39, of which 23 were waited for; matrix products, arithmetic and copies ran while one was open for 26% of the time, Pallas kernels for 0%

profile of v2, /device:TPU:0, one launch (start us, length us, event | category | flops | bytes accessed | tf_op | source)
XLA Modules:
  0.0 143.8 jit_solution(17696267214575377734)
XLA Ops:
  1.4 1.0 bitcast_multiply_fusion.1
  2.4 3.1 %collective-permute-start.18 = (bf16[8,128,128]{2,1,0:T(8,128)(2,1)S(1)}, bf16[8,128,128]{2,1,0:T(8,128)(2,1)S(1)}, u32[]{:S(2)}, u32[]{:S(2)}) collective-permute-start(bf16[8,128,128]{2,1,0:T(8,128)(2,1)S(1)} %bitcast_multiply_fusion.1), channel_id=1, source_target_pairs={{0,1},{1,2},{2,3},{3,0},{4,5},{5,6},{6,7},{7,4},{8,9},{9,10},{10,1... | collective-permute-start | bytes 786440 | tf_op jit(solution)/shard_map/ppermute | solution.py:21
  5.5 2.6 %collective-permute-start.19 = (bf16[8,128,128]{2,1,0:T(8,128)(2,1)S(1)}, bf16[8,128,128]{2,1,0:T(8,128)(2,1)S(1)}, u32[]{:S(2)}, u32[]{:S(2)}) collective-permute-start(bf16[8,128,128]{2,1,0:T(8,128)(2,1)S(1)} %bitcast_multiply_fusion.1), channel_id=1, source_target_pairs={{0,2},{1,3},{2,0},{3,1},{4,6},{5,7},{6,4},{7,5},{8,10},{9,11},{10,... | collective-permute-start | bytes 786440 | tf_op jit(solution)/shard_map/ppermute | solution.py:21
  8.8 1.0 bitcast_multiply_fusion.2
  9.9 1.8 %collective-permute-start.1 = (bf16[3,128,128]{2,1,0:T(8,128)(2,1)S(1)}, bf16[3,128,128]{2,1,0:T(8,128)(2,1)S(1)}, u32[]{:S(2)}, u32[]{:S(2)}) collective-permute-start(bf16[3,128,128]{2,1,0:T(8,128)(2,1)S(1)} %bitcast_multiply_fusion.2), channel_id=1, source_target_pairs={{0,2},{1,3},{2,0},{3,1},{4,6},{5,7},{6,4},{7,5},{8,10},{9,11},{10,... | collective-permute-start | bytes 294920 | tf_op jit(solution)/shard_map/ppermute | solution.py:21
  11.7 1.9 %collective-permute-start.2 = (bf16[3,128,128]{2,1,0:T(8,128)(2,1)S(1)}, bf16[3,128,128]{2,1,0:T(8,128)(2,1)S(1)}, u32[]{:S(2)}, u32[]{:S(2)}) collective-permute-start(bf16[3,128,128]{2,1,0:T(8,128)(2,1)S(1)} %bitcast_multiply_fusion.2), channel_id=1, source_target_pairs={{0,3},{1,0},{2,1},{3,2},{4,7},{5,4},{6,5},{7,6},{8,11},{9,8},{10,9... | collective-permute-start | bytes 294920 | tf_op jit(solution)/shard_map/ppermute | solution.py:21
  13.6 1.7 %bitcast_multiply_fusion = bf16[1,8,128,128]{3,2,1,0:T(8,128)(2,1)} fusion(bf16[8,1,1,128,128]{4,3,2,1,0:T(8,128)(2,1)} %param.13, bf16[8]{0:T(256)(128)(2,1)S(1)} %get-tuple-element.42), kind=kLoop, calls=%fused_computation.48 | loop fusion | flops 131072 | bytes 524304 | tf_op jit(solution)/shard_map/mul | solution.py:108
  15.4 1.0 bitcast_multiply_fusion.3
  17.9 2.0 %copy.51 = f32[8,128,128]{1,2,0:T(8,128)} copy(f32[8,128,128]{2,1,0:T(8,128)} %param.17) | data formatting | bytes 1048576 | tf_op args[8]
  20.1 2.4 %collective-permute-done = bf16[3,128,128]{2,1,0:T(8,128)(2,1)S(1)} collective-permute-done((bf16[3,128,128]{2,1,0:T(8,128)(2,1)S(1)}, bf16[3,128,128]{2,1,0:T(8,128)(2,1)S(1)}, u32[]{:S(2)}, u32[]{:S(2)}) %collective-permute-start) | collective-permute-done | bytes 98336 | tf_op jit(solution)/shard_map/ppermute | solution.py:21
  22.5 9.0 %collective-permute-done.1 = bf16[3,128,128]{2,1,0:T(8,128)(2,1)S(1)} collective-permute-done((bf16[3,128,128]{2,1,0:T(8,128)(2,1)S(1)}, bf16[3,128,128]{2,1,0:T(8,128)(2,1)S(1)}, u32[]{:S(2)}, u32[]{:S(2)}) %collective-permute-start.1) | collective-permute-done | bytes 98336 | tf_op jit(solution)/shard_map/ppermute | solution.py:21
  33.0 1.2 copy.38
  34.2 1.1 copy.37
  35.4 6.0 %collective-permute-done.20 = bf16[8,128,128]{2,1,0:T(8,128)(2,1)} collective-permute-done((bf16[8,128,128]{2,1,0:T(8,128)(2,1)S(1)}, bf16[8,128,128]{2,1,0:T(8,128)(2,1)}, u32[]{:S(2)}, u32[]{:S(2)}) %collective-permute-start.20) | collective-permute-done | bytes 262176 | tf_op jit(solution)/shard_map/ppermute | solution.py:21
  41.4 1.3 pad_maximum_fusion
  43.4 1.4 convolution_bitcast_fusion
  45.9 1.2 bitcast_add_fusion.2
  47.9 1.5 %collective-permute-start.4 = (bf16[2,3,128,128]{3,2,1,0:T(8,128)(2,1)}, bf16[2,3,128,128]{3,2,1,0:T(8,128)(2,1)}, u32[]{:S(2)}, u32[]{:S(2)}) collective-permute-start(bf16[2,3,128,128]{3,2,1,0:T(8,128)(2,1)} %fusion.16), channel_id=1, source_target_pairs={{0,8},{4,12},{8,0},{12,4},{16,24},{20,28},{24,16},{28,20},{1,9},{5... | collective-permute-start | bytes 589832 | tf_op jit(solution)/shard_map/ppermute | solution.py:16
  49.4 1.7 %constant_dynamic-slice_fusion.1 = (f32[2,2,1,4,128,128]{4,5,2,1,0,3:T(8,128)}, f32[2,2,1,4,128,128]{4,5,2,1,0,3:T(8,128)S(1)}, f32[2,2,1,4,128,128]{4,5,2,1,0,3:T(8,128)S(1)}, f32[2,2,1,4,128,128]{4,5,2,1,0,3:T(8,128)}) fusion(f32[2,2,2,4,128,128]{4,5,2,1,0,3:T(8,128)S(1)} %bitcast.221, s32[]{:T(128)S(6)} %select_n.249, s32[]{:T(128)S(6)} %select_n.250, ...), kind=kLoop, calls=%fused_computation.116 | loop fusion | bytes 8388616 | tf_op jit(solution)/shard_map/jit(dynamic_index_in_dim)/dynamic_slice | solution.py:49
  51.2 1.4 copy.46
  52.5 1.4 collective-permute-done.4
  53.9 1.1 bitcast_add_fusion.6
  55.1 1.6 %collective-permute-start.5 = (bf16[3,128,128]{2,1,0:T(8,128)(2,1)S(1)}, bf16[3,128,128]{2,1,0:T(8,128)(2,1)}, u32[]{:S(2)}, u32[]{:S(2)}) collective-permute-start(bf16[3,128,128]{2,1,0:T(8,128)(2,1)S(1)} %fusion.24), channel_id=1, source_target_pairs={{0,16},{4,20},{8,24},{12,28},{16,0},{20,4},{24,8},{28,12},{1,17},{... | collective-permute-start | bytes 294920 | tf_op jit(solution)/shard_map/ppermute | solution.py:16
  56.7 1.6 %copy.45 = f32[2,2,1,4,128,128]{5,4,3,0,1,2:T(8,128)S(1)} copy(f32[2,2,1,4,128,128]{4,5,2,1,0,3:T(8,128)} %get-tuple-element.46) | data formatting | bytes 2097152 | tf_op jit(solution)/shard_map/jit(dynamic_index_in_dim)/dynamic_slice | solution.py:49
  58.3 1.3 copy.48
  59.6 1.6 %copy.47 = f32[2,2,1,4,128,128]{5,4,3,1,0,2:T(8,128)S(1)} copy(f32[2,2,1,4,128,128]{4,5,2,1,0,3:T(8,128)} %get-tuple-element.19) | data formatting | bytes 2097152 | tf_op jit(solution)/shard_map/jit(dynamic_index_in_dim)/dynamic_slice | solution.py:49
  61.2 1.1 fusion.19
  62.2 1.3 gather_fusion.1
  63.5 1.1 fusion.42
  64.7 1.3 fusion.23
  66.7 1.3 bitcast_add_fusion.1
  68.1 1.6 %collective-permute-start.22 = (bf16[2,4,128,128]{3,2,1,0:T(8,128)(2,1)S(1)}, bf16[2,4,128,128]{3,2,1,0:T(8,128)(2,1)S(1)}, u32[]{:S(2)}, u32[]{:S(2)}) collective-permute-start(bf16[2,4,128,128]{3,2,1,0:T(8,128)(2,1)S(1)} %fusion.12), channel_id=1, source_target_pairs={{0,8},{4,12},{8,0},{12,4},{16,24},{20,28},{24,16},{28,20},{1,9},{5... | collective-permute-start | bytes 786440 | tf_op jit(solution)/shard_map/ppermute | solution.py:16
  69.7 1.3 bitcast_add_fusion
  71.7 4.6 %collective-permute-done.22 = bf16[2,4,128,128]{3,2,1,0:T(8,128)(2,1)S(1)} collective-permute-done((bf16[2,4,128,128]{3,2,1,0:T(8,128)(2,1)S(1)}, bf16[2,4,128,128]{3,2,1,0:T(8,128)(2,1)S(1)}, u32[]{:S(2)}, u32[]{:S(2)}) %collective-permute-start.22) | collective-permute-done | bytes 262176 | tf_op jit(solution)/shard_map/ppermute | solution.py:16
  77.3 1.6 %collective-permute-start.7 = (bf16[2,192,128]{2,1,0:T(8,128)(2,1)S(1)}, bf16[2,192,128]{2,1,0:T(8,128)(2,1)S(1)}, u32[]{:S(2)}, u32[]{:S(2)}) collective-permute-start(bf16[2,192,128]{2,1,0:T(8,128)(2,1)S(1)} %fusion.25), channel_id=1, source_target_pairs={{0,8},{4,12},{8,0},{12,4},{16,24},{20,28},{24,16},{28,20},{1,9},{5... | collective-permute-start | bytes 294920 | tf_op jit(solution)/shard_map/ppermute | solution.py:16
  79.9 3.1 %collective-permute-done.7 = bf16[2,192,128]{2,1,0:T(8,128)(2,1)S(1)} collective-permute-done((bf16[2,192,128]{2,1,0:T(8,128)(2,1)S(1)}, bf16[2,192,128]{2,1,0:T(8,128)(2,1)S(1)}, u32[]{:S(2)}, u32[]{:S(2)}) %collective-permute-start.7) | collective-permute-done | bytes 98336 | tf_op jit(solution)/shard_map/ppermute | solution.py:16
  83.1 1.1 collective-permute-start.8
  85.2 2.0 %collective-permute-done.8 = bf16[192,128]{1,0:T(8,128)(2,1)S(1)} collective-permute-done((bf16[192,128]{1,0:T(8,128)(2,1)S(1)}, bf16[192,128]{1,0:T(8,128)(2,1)S(1)}, u32[]{:S(2)}, u32[]{:S(2)}) %collective-permute-start.8) | collective-permute-done | bytes 49184 | tf_op jit(solution)/shard_map/ppermute | solution.py:16
  87.3 4.0 %collective-permute-start.10 = (f32[48,128]{1,0:T(8,128)S(1)}, f32[48,128]{1,0:T(8,128)S(1)}, u32[]{:S(2)}, u32[]{:S(2)}) collective-permute-start(f32[48,128]{1,0:T(8,128)S(1)} %get-tuple-element.35), channel_id=1, source_target_pairs={{0,2},{1,3},{2,0},{3,1},{4,6},{5,7},{6,4},{7,5},{8,10},{9,11},{10,... | collective-permute-start | bytes 73736 | tf_op jit(solution)/shard_map/ppermute | solution.py:21
  91.2 1.8 %collective-permute-start.11 = (f32[48,128]{1,0:T(8,128)S(1)}, f32[48,128]{1,0:T(8,128)S(1)}, u32[]{:S(2)}, u32[]{:S(2)}) collective-permute-start(f32[48,128]{1,0:T(8,128)S(1)} %get-tuple-element.34), channel_id=1, source_target_pairs={{0,3},{1,0},{2,1},{3,2},{4,7},{5,4},{6,5},{7,6},{8,11},{9,8},{10,9... | collective-permute-start | bytes 73736 | tf_op jit(solution)/shard_map/ppermute | solution.py:21
  93.9 1.5 %collective-permute-done.11 = f32[48,128]{1,0:T(8,128)S(1)} collective-permute-done((f32[48,128]{1,0:T(8,128)S(1)}, f32[48,128]{1,0:T(8,128)S(1)}, u32[]{:S(2)}, u32[]{:S(2)}) %collective-permute-start.11) | collective-permute-done | bytes 24608 | tf_op jit(solution)/shard_map/ppermute | solution.py:21
  95.4 3.4 %collective-permute-done.9 = f32[48,128]{1,0:T(8,128)S(1)} collective-permute-done((f32[48,128]{1,0:T(8,128)S(1)}, f32[48,128]{1,0:T(8,128)S(1)}, u32[]{:S(2)}, u32[]{:S(2)}) %collective-permute-start.9) | collective-permute-done | bytes 24608 | tf_op jit(solution)/shard_map/ppermute | solution.py:21
  99.4 3.2 %collective-permute-start.14 = (bf16[48,128]{1,0:T(8,128)(2,1)S(1)}, bf16[48,128]{1,0:T(8,128)(2,1)S(1)}, u32[]{:S(2)}, u32[]{:S(2)}) collective-permute-start(bf16[48,128]{1,0:T(8,128)(2,1)S(1)} %fusion.31), channel_id=1, source_target_pairs={{0,3},{1,0},{2,1},{3,2},{4,7},{5,4},{6,5},{7,6},{8,11},{9,8},{10,9... | collective-permute-start | bytes 36872 | tf_op jit(solution)/shard_map/ppermute | solution.py:21
  102.8 1.6 %collective-permute-done.12 = bf16[48,128]{1,0:T(8,128)(2,1)S(1)} collective-permute-done((bf16[48,128]{1,0:T(8,128)(2,1)S(1)}, bf16[48,128]{1,0:T(8,128)(2,1)S(1)}, u32[]{:S(2)}, u32[]{:S(2)}) %collective-permute-start.12) | collective-permute-done | bytes 12320 | tf_op jit(solution)/shard_map/ppermute | solution.py:21
  105.6 1.2 collective-permute-start.15
  106.9 1.2 collective-permute-start.28
  108.1 1.6 %collective-permute-done.15 = bf16[192,128]{1,0:T(8,128)(2,1)S(1)} collective-permute-done((bf16[192,128]{1,0:T(8,128)(2,1)S(1)}, bf16[192,128]{1,0:T(8,128)(2,1)S(1)}, u32[]{:S(2)}, u32[]{:S(2)}) %collective-permute-start.15) | collective-permute-done | bytes 49184 | tf_op jit(solution)/shard_map/ppermute | solution.py:16
  109.8 1.4 collective-permute-done.28
  112.2 1.0 collective-permute-start.16
  113.2 2.0 %collective-permute-done.29 = bf16[128,128]{1,0:T(8,128)(2,1)S(1)} collective-permute-done((bf16[128,128]{1,0:T(8,128)(2,1)S(1)}, bf16[128,128]{1,0:T(8,128)(2,1)S(1)}, u32[]{:S(2)}, u32[]{:S(2)}) %collective-permute-start.29) | collective-permute-done | bytes 32800 | tf_op jit(solution)/shard_map/ppermute | solution.py:16
  115.2 2.7 %collective-permute-start.30 = (f32[32,128]{1,0:T(8,128)S(1)}, f32[32,128]{1,0:T(8,128)S(1)}, u32[]{:S(2)}, u32[]{:S(2)}) collective-permute-start(f32[32,128]{1,0:T(8,128)S(1)} %get-tuple-element.38), channel_id=1, source_target_pairs={{0,1},{1,2},{2,3},{3,0},{4,5},{5,6},{6,7},{7,4},{8,9},{9,10},{10,1... | collective-permute-start | bytes 49160 | tf_op jit(solution)/shard_map/ppermute | solution.py:21
  117.9 1.2 collective-permute-start.31
  119.1 1.3 collective-permute-start.32
  120.8 1.8 %collective-permute-done.31 = f32[32,128]{1,0:T(8,128)S(1)} collective-permute-done((f32[32,128]{1,0:T(8,128)S(1)}, f32[32,128]{1,0:T(8,128)S(1)}, u32[]{:S(2)}, u32[]{:S(2)}) %collective-permute-start.31) | collective-permute-done | bytes 16416 | tf_op jit(solution)/shard_map/ppermute | solution.py:21
  123.5 3.1 %collective-permute-start.34 = (bf16[32,128]{1,0:T(8,128)(2,1)S(1)}, bf16[32,128]{1,0:T(8,128)(2,1)S(1)}, u32[]{:S(2)}, u32[]{:S(2)}) collective-permute-start(bf16[32,128]{1,0:T(8,128)(2,1)S(1)} %fusion.34), channel_id=1, source_target_pairs={{0,2},{1,3},{2,0},{3,1},{4,6},{5,7},{6,4},{7,5},{8,10},{9,11},{10,... | collective-permute-start | bytes 24584 | tf_op jit(solution)/shard_map/ppermute | solution.py:21
  126.5 1.0 collective-permute-start.35
  128.4 1.8 %collective-permute-done.35 = bf16[32,128]{1,0:T(8,128)(2,1)S(1)} collective-permute-done((bf16[32,128]{1,0:T(8,128)(2,1)S(1)}, bf16[32,128]{1,0:T(8,128)(2,1)S(1)}, u32[]{:S(2)}, u32[]{:S(2)}) %collective-permute-start.35) | collective-permute-done | bytes 8224 | tf_op jit(solution)/shard_map/ppermute | solution.py:21
  130.9 1.0 collective-permute-start.36
  132.0 2.8 %collective-permute-done.36 = bf16[128,128]{1,0:T(8,128)(2,1)S(1)} collective-permute-done((bf16[128,128]{1,0:T(8,128)(2,1)S(1)}, bf16[128,128]{1,0:T(8,128)(2,1)S(1)}, u32[]{:S(2)}, u32[]{:S(2)}) %collective-permute-start.36) | collective-permute-done | bytes 32800 | tf_op jit(solution)/shard_map/ppermute | solution.py:16
  135.0 1.0 collective-permute-start.37
  136.7 2.6 %collective-permute-done.37 = bf16[2,128,128]{2,1,0:T(8,128)(2,1)S(1)} collective-permute-done((bf16[2,128,128]{2,1,0:T(8,128)(2,1)S(1)}, bf16[2,128,128]{2,1,0:T(8,128)(2,1)S(1)}, u32[]{:S(2)}, u32[]{:S(2)}) %collective-permute-start.37) | collective-permute-done | bytes 65568 | tf_op jit(solution)/shard_map/ppermute | solution.py:16
  139.4 1.5 %convolution_subtract_fusion = f32[8,128,128]{2,1,0:T(8,128)S(1)} fusion(f32[8,128,128]{2,1,0:T(8,128)S(1)} %bitcast.229, bf16[8,128,128]{2,1,0:T(8,128)(2,1)} %param.16, f32[8,128,128]{2,1,0:T(8,128)S(1)} %gather_fusion.4, pred[8]{0:T(512)(128)(4,1)S(1)} %compare_and_fusion), kind=kOutput, calls=%fused_computation.9 | convolution fusion | flops 201588736 | bytes 1835016 | tf_op jit(solution)/shard_map/mxy,myz->mxz/dot_general | solution.py:144
  141.3 1.5 %fusion = f32[8,128,128]{1,2,0:T(8,128)S(1)} fusion(f32[8,128,128]{1,2,0:T(8,128)S(1)} %bitcast_subtract_fusion, f32[8,128,128]{2,1,0:T(8,128)S(1)} %convolution_subtract_fusion, bf16[8,128,128]{2,1,0:T(8,128)(2,1)} %param.16), kind=kOutput, calls=%fused_computation.8 | convolution fusion | flops 201457664 | bytes 1835008 | tf_op jit(solution)/shard_map/myx,myz->mxz/dot_general | solution.py:150
  142.8 1.0 copy.54
  (142 shorter events, 19.9 us)
Async XLA Ops:
  0.6 31.6 %copy-start = (bf16[1,4,8,1,128,128]{5,4,3,2,1,0:T(8,128)(2,1)S(1)}, bf16[1,4,8,1,128,128]{5,4,3,2,1,0:T(8,128)(2,1)}, u32[]{:S(2)}) copy-start(bf16[1,4,8,1,128,128]{5,4,3,2,1,0:T(8,128)(2,1)} %param.9) | copy-start | bytes 3145732
  2.4 32.9 %collective-permute-start.18 = (bf16[8,128,128]{2,1,0:T(8,128)(2,1)S(1)}, bf16[8,128,128]{2,1,0:T(8,128)(2,1)S(1)}, u32[]{:S(2)}, u32[]{:S(2)}) collective-permute-start(bf16[8,128,128]{2,1,0:T(8,128)(2,1)S(1)} %bitcast_multiply_fusion.1), channel_id=1, source_target_pairs={{0,1},{1,2},{2,3},{3,0},{4,5},{5,6},{6,7},{7,4},{8,9},{9,10},{10,1... | collective-permute-start | bytes 786440 | tf_op jit(solution)/shard_map/ppermute | solution.py:21
  5.5 29.8 %collective-permute-start.19 = (bf16[8,128,128]{2,1,0:T(8,128)(2,1)S(1)}, bf16[8,128,128]{2,1,0:T(8,128)(2,1)S(1)}, u32[]{:S(2)}, u32[]{:S(2)}) collective-permute-start(bf16[8,128,128]{2,1,0:T(8,128)(2,1)S(1)} %bitcast_multiply_fusion.1), channel_id=1, source_target_pairs={{0,2},{1,3},{2,0},{3,1},{4,6},{5,7},{6,4},{7,5},{8,10},{9,11},{10,... | collective-permute-start | bytes 786440 | tf_op jit(solution)/shard_map/ppermute | solution.py:21
  9.7 21.8 %copy-start.10 = (bf16[3,128,128]{2,1,0:T(8,128)(2,1)}, bf16[3,128,128]{2,1,0:T(8,128)(2,1)S(1)}, u32[]{:S(2)}) copy-start(bf16[3,128,128]{2,1,0:T(8,128)(2,1)S(1)} %bitcast_multiply_fusion.2) | copy-start | bytes 294916
  9.7 12.8 %collective-permute-start = (bf16[3,128,128]{2,1,0:T(8,128)(2,1)S(1)}, bf16[3,128,128]{2,1,0:T(8,128)(2,1)S(1)}, u32[]{:S(2)}, u32[]{:S(2)}) collective-permute-start(bf16[3,128,128]{2,1,0:T(8,128)(2,1)S(1)} %bitcast_multiply_fusion.2), channel_id=1, source_target_pairs={{0,1},{1,2},{2,3},{3,0},{4,5},{5,6},{6,7},{7,4},{8,9},{9,10},{10,1... | collective-permute-start | bytes 294920 | tf_op jit(solution)/shard_map/ppermute | solution.py:21
  9.9 21.6 %collective-permute-start.1 = (bf16[3,128,128]{2,1,0:T(8,128)(2,1)S(1)}, bf16[3,128,128]{2,1,0:T(8,128)(2,1)S(1)}, u32[]{:S(2)}, u32[]{:S(2)}) collective-permute-start(bf16[3,128,128]{2,1,0:T(8,128)(2,1)S(1)} %bitcast_multiply_fusion.2), channel_id=1, source_target_pairs={{0,2},{1,3},{2,0},{3,1},{4,6},{5,7},{6,4},{7,5},{8,10},{9,11},{10,... | collective-permute-start | bytes 294920 | tf_op jit(solution)/shard_map/ppermute | solution.py:21
  11.7 19.8 %collective-permute-start.2 = (bf16[3,128,128]{2,1,0:T(8,128)(2,1)S(1)}, bf16[3,128,128]{2,1,0:T(8,128)(2,1)S(1)}, u32[]{:S(2)}, u32[]{:S(2)}) collective-permute-start(bf16[3,128,128]{2,1,0:T(8,128)(2,1)S(1)} %bitcast_multiply_fusion.2), channel_id=1, source_target_pairs={{0,3},{1,0},{2,1},{3,2},{4,7},{5,4},{6,5},{7,6},{8,11},{9,8},{10,9... | collective-permute-start | bytes 294920 | tf_op jit(solution)/shard_map/ppermute | solution.py:21
  22.5 18.9 %collective-permute-start.20 = (bf16[8,128,128]{2,1,0:T(8,128)(2,1)S(1)}, bf16[8,128,128]{2,1,0:T(8,128)(2,1)}, u32[]{:S(2)}, u32[]{:S(2)}) collective-permute-start(bf16[8,128,128]{2,1,0:T(8,128)(2,1)S(1)} %bitcast_multiply_fusion.1), channel_id=1, source_target_pairs={{0,3},{1,0},{2,1},{3,2},{4,7},{5,4},{6,5},{7,6},{8,11},{9,8},{10,9... | collective-permute-start | bytes 786440 | tf_op jit(solution)/shard_map/ppermute | solution.py:21
  34.2 11.1 %collective-permute-start.3 = (f32[2,2,3,128,128]{4,3,2,0,1:T(8,128)}, f32[2,2,3,128,128]{4,3,2,0,1:T(8,128)}, u32[]{:S(2)}, u32[]{:S(2)}) collective-permute-start(f32[2,2,3,128,128]{4,3,2,0,1:T(8,128)} %bitcast.233), channel_id=1, source_target_pairs={{0,4},{4,0},{8,12},{12,8},{16,20},{20,16},{24,28},{28,24},{1,5},{5... | collective-permute-start | bytes 2359304 | tf_op jit(solution)/shard_map/ppermute | solution.py:16
  35.3 6.0 %copy-start.12 = (bf16[8,128,128]{2,1,0:T(8,128)(2,1)}, bf16[8,128,128]{2,1,0:T(8,128)(2,1)S(1)}, u32[]{:S(2)}) copy-start(bf16[8,128,128]{2,1,0:T(8,128)(2,1)S(1)} %collective-permute-done.18) | copy-start | bytes 786436
  35.4 6.0 %copy-start.13 = (bf16[8,128,128]{2,1,0:T(8,128)(2,1)}, bf16[8,128,128]{2,1,0:T(8,128)(2,1)S(1)}, u32[]{:S(2)}) copy-start(bf16[8,128,128]{2,1,0:T(8,128)(2,1)S(1)} %collective-permute-done.19) | copy-start | bytes 786436
  44.8 1.1 copy-start.1
  47.2 2.3 %copy-start.3 = (f32[2,2,3,128,128]{4,3,2,0,1:T(8,128)}, f32[2,2,3,128,128]{4,3,2,0,1:T(8,128)S(1)}, u32[]{:S(2)}) copy-start(f32[2,2,3,128,128]{4,3,2,0,1:T(8,128)S(1)} %bitcast_add_fusion.2) | copy-start | bytes 2359300
  47.9 6.0 %collective-permute-start.4 = (bf16[2,3,128,128]{3,2,1,0:T(8,128)(2,1)}, bf16[2,3,128,128]{3,2,1,0:T(8,128)(2,1)}, u32[]{:S(2)}, u32[]{:S(2)}) collective-permute-start(bf16[2,3,128,128]{3,2,1,0:T(8,128)(2,1)} %fusion.16), channel_id=1, source_target_pairs={{0,8},{4,12},{8,0},{12,4},{16,24},{20,28},{24,16},{28,20},{1,9},{5... | collective-permute-start | bytes 589832 | tf_op jit(solution)/shard_map/ppermute | solution.py:16
  52.5 14.2 %collective-permute-start.21 = (f32[2,2,4,128,128]{4,3,2,0,1:T(8,128)}, f32[2,2,4,128,128]{4,3,2,0,1:T(8,128)}, u32[]{:S(2)}, u32[]{:S(2)}) collective-permute-start(f32[2,2,4,128,128]{4,3,2,0,1:T(8,128)} %bitcast.231), channel_id=1, source_target_pairs={{0,4},{4,0},{8,12},{12,8},{16,20},{20,16},{24,28},{28,24},{1,5},{5... | collective-permute-start | bytes 3145736 | tf_op jit(solution)/shard_map/ppermute | solution.py:16
  55.1 1.6 %copy-start.7 = (f32[2,3,128,128]{3,2,1,0:T(8,128)}, f32[2,3,128,128]{3,2,1,0:T(8,128)S(1)}, u32[]{:S(2)}) copy-start(f32[2,3,128,128]{3,2,1,0:T(8,128)S(1)} %bitcast_add_fusion.6) | copy-start | bytes 1179652
  55.1 6.0 %collective-permute-start.5 = (bf16[3,128,128]{2,1,0:T(8,128)(2,1)S(1)}, bf16[3,128,128]{2,1,0:T(8,128)(2,1)}, u32[]{:S(2)}, u32[]{:S(2)}) collective-permute-start(bf16[3,128,128]{2,1,0:T(8,128)(2,1)S(1)} %fusion.24), channel_id=1, source_target_pairs={{0,16},{4,20},{8,24},{12,28},{16,0},{20,4},{24,8},{28,12},{1,17},{... | collective-permute-start | bytes 294920 | tf_op jit(solution)/shard_map/ppermute | solution.py:16
  59.6 10.1 %collective-permute-start.24 = (f32[2,2,4,128,128]{4,3,2,1,0:T(8,128)}, f32[2,2,4,128,128]{4,3,2,1,0:T(8,128)}, u32[]{:S(2)}, u32[]{:S(2)}) collective-permute-start(f32[2,2,4,128,128]{4,3,2,1,0:T(8,128)} %bitcast.232), channel_id=1, source_target_pairs={{0,4},{4,0},{8,12},{12,8},{16,20},{20,16},{24,28},{28,24},{1,5},{5... | collective-permute-start | bytes 3145736 | tf_op jit(solution)/shard_map/ppermute | solution.py:16
  62.2 3.8 %copy-start.4 = (bf16[3,128,128]{2,1,0:T(8,128)(2,1)}, bf16[3,128,128]{2,1,0:T(8,128)(2,1)S(1)}, u32[]{:S(2)}) copy-start(bf16[3,128,128]{2,1,0:T(8,128)(2,1)S(1)} %fusion.19) | copy-start | bytes 294916
  66.1 11.1 %collective-permute-start.6 = (f32[2,2,192,128]{3,2,1,0:T(8,128)S(1)}, f32[2,2,192,128]{3,2,1,0:T(8,128)S(1)}, u32[]{:S(2)}, u32[]{:S(2)}) collective-permute-start(f32[2,2,192,128]{3,2,1,0:T(8,128)S(1)} %dynamic-slice_bitcast_fusion), channel_id=1, source_target_pairs={{0,4},{4,0},{8,12},{12,8},{16,20},{20,16},{24,28},{28,24},{1,5},{5... | collective-permute-start | bytes 1179656 | tf_op jit(solution)/shard_map/ppermute | solution.py:16
  68.1 8.3 %collective-permute-start.22 = (bf16[2,4,128,128]{3,2,1,0:T(8,128)(2,1)S(1)}, bf16[2,4,128,128]{3,2,1,0:T(8,128)(2,1)S(1)}, u32[]{:S(2)}, u32[]{:S(2)}) collective-permute-start(bf16[2,4,128,128]{3,2,1,0:T(8,128)(2,1)S(1)} %fusion.12), channel_id=1, source_target_pairs={{0,8},{4,12},{8,0},{12,4},{16,24},{20,28},{24,16},{28,20},{1,9},{5... | collective-permute-start | bytes 786440 | tf_op jit(solution)/shard_map/ppermute | solution.py:16
  71.1 8.7 %collective-permute-start.25 = (bf16[2,4,128,128]{3,2,1,0:T(8,128)(2,1)S(1)}, bf16[2,4,128,128]{3,2,1,0:T(8,128)(2,1)S(1)}, u32[]{:S(2)}, u32[]{:S(2)}) collective-permute-start(bf16[2,4,128,128]{3,2,1,0:T(8,128)(2,1)S(1)} %fusion.13), channel_id=1, source_target_pairs={{0,16},{4,20},{8,24},{12,28},{16,0},{20,4},{24,8},{28,12},{1,17},{... | collective-permute-start | bytes 786440 | tf_op jit(solution)/shard_map/ppermute | solution.py:16
  76.5 7.7 %collective-permute-start.23 = (bf16[4,128,128]{2,1,0:T(8,128)(2,1)S(1)}, bf16[4,128,128]{2,1,0:T(8,128)(2,1)S(1)}, u32[]{:S(2)}, u32[]{:S(2)}) collective-permute-start(bf16[4,128,128]{2,1,0:T(8,128)(2,1)S(1)} %fusion.20), channel_id=1, source_target_pairs={{0,16},{4,20},{8,24},{12,28},{16,0},{20,4},{24,8},{28,12},{1,17},{... | collective-permute-start | bytes 393224 | tf_op jit(solution)/shard_map/ppermute | solution.py:16
  77.2 7.7 %copy-start.8 = (bf16[8,128,128]{2,1,0:T(8,128)(2,1)S(1)}, bf16[8,128,128]{2,1,0:T(8,128)(2,1)}, u32[]{:S(2)}) copy-start(bf16[8,128,128]{2,1,0:T(8,128)(2,1)} %param.16) | copy-start | bytes 786436
  77.2 7.7 %copy-start.9 = (bf16[8,128,128]{2,1,0:T(8,128)(2,1)S(1)}, bf16[8,128,128]{2,1,0:T(8,128)(2,1)}, u32[]{:S(2)}) copy-start(bf16[8,128,128]{2,1,0:T(8,128)(2,1)} %gather_fusion.1) | copy-start | bytes 786436
  77.3 5.7 %collective-permute-start.7 = (bf16[2,192,128]{2,1,0:T(8,128)(2,1)S(1)}, bf16[2,192,128]{2,1,0:T(8,128)(2,1)S(1)}, u32[]{:S(2)}, u32[]{:S(2)}) collective-permute-start(bf16[2,192,128]{2,1,0:T(8,128)(2,1)S(1)} %fusion.25), channel_id=1, source_target_pairs={{0,8},{4,12},{8,0},{12,4},{16,24},{20,28},{24,16},{28,20},{1,9},{5... | collective-permute-start | bytes 294920 | tf_op jit(solution)/shard_map/ppermute | solution.py:16
  79.9 5.0 %collective-permute-start.26 = (bf16[4,128,128]{2,1,0:T(8,128)(2,1)S(1)}, bf16[4,128,128]{2,1,0:T(8,128)(2,1)S(1)}, u32[]{:S(2)}, u32[]{:S(2)}) collective-permute-start(bf16[4,128,128]{2,1,0:T(8,128)(2,1)S(1)} %fusion.21), channel_id=1, source_target_pairs={{0,8},{4,12},{8,0},{12,4},{16,24},{20,28},{24,16},{28,20},{1,9},{5... | collective-permute-start | bytes 393224 | tf_op jit(solution)/shard_map/ppermute | solution.py:16
  83.1 4.2 %collective-permute-start.8 = (bf16[192,128]{1,0:T(8,128)(2,1)S(1)}, bf16[192,128]{1,0:T(8,128)(2,1)S(1)}, u32[]{:S(2)}, u32[]{:S(2)}) collective-permute-start(bf16[192,128]{1,0:T(8,128)(2,1)S(1)} %fusion.27), channel_id=1, source_target_pairs={{0,16},{4,20},{8,24},{12,28},{16,0},{20,4},{24,8},{28,12},{1,17},{... | collective-permute-start | bytes 147464 | tf_op jit(solution)/shard_map/ppermute | solution.py:16
  85.2 19.7 %copy-start.11 = (bf16[8,128,128]{2,1,0:T(8,128)(2,1)}, bf16[8,128,128]{2,1,0:T(8,128)(2,1)S(1)}, u32[]{:S(2)}) copy-start(bf16[8,128,128]{2,1,0:T(8,128)(2,1)S(1)} %fusion.9) | copy-start | bytes 786436
  87.3 6.6 %collective-permute-start.10 = (f32[48,128]{1,0:T(8,128)S(1)}, f32[48,128]{1,0:T(8,128)S(1)}, u32[]{:S(2)}, u32[]{:S(2)}) collective-permute-start(f32[48,128]{1,0:T(8,128)S(1)} %get-tuple-element.35), channel_id=1, source_target_pairs={{0,2},{1,3},{2,0},{3,1},{4,6},{5,7},{6,4},{7,5},{8,10},{9,11},{10,... | collective-permute-start | bytes 73736 | tf_op jit(solution)/shard_map/ppermute | solution.py:21
  91.2 4.1 %collective-permute-start.11 = (f32[48,128]{1,0:T(8,128)S(1)}, f32[48,128]{1,0:T(8,128)S(1)}, u32[]{:S(2)}, u32[]{:S(2)}) collective-permute-start(f32[48,128]{1,0:T(8,128)S(1)} %get-tuple-element.34), channel_id=1, source_target_pairs={{0,3},{1,0},{2,1},{3,2},{4,7},{5,4},{6,5},{7,6},{8,11},{9,8},{10,9... | collective-permute-start | bytes 73736 | tf_op jit(solution)/shard_map/ppermute | solution.py:21
  93.1 5.7 %collective-permute-start.9 = (f32[48,128]{1,0:T(8,128)S(1)}, f32[48,128]{1,0:T(8,128)S(1)}, u32[]{:S(2)}, u32[]{:S(2)}) collective-permute-start(f32[48,128]{1,0:T(8,128)S(1)} %get-tuple-element.33), channel_id=1, source_target_pairs={{0,1},{1,2},{2,3},{3,0},{4,5},{5,6},{6,7},{7,4},{8,9},{9,10},{10,1... | collective-permute-start | bytes 73736 | tf_op jit(solution)/shard_map/ppermute | solution.py:21
  98.8 5.5 %collective-permute-start.12 = (bf16[48,128]{1,0:T(8,128)(2,1)S(1)}, bf16[48,128]{1,0:T(8,128)(2,1)S(1)}, u32[]{:S(2)}, u32[]{:S(2)}) collective-permute-start(bf16[48,128]{1,0:T(8,128)(2,1)S(1)} %fusion.31), channel_id=1, source_target_pairs={{0,1},{1,2},{2,3},{3,0},{4,5},{5,6},{6,7},{7,4},{8,9},{9,10},{10,1... | collective-permute-start | bytes 36872 | tf_op jit(solution)/shard_map/ppermute | solution.py:21
  98.8 5.5 %collective-permute-start.13 = (bf16[48,128]{1,0:T(8,128)(2,1)S(1)}, bf16[48,128]{1,0:T(8,128)(2,1)S(1)}, u32[]{:S(2)}, u32[]{:S(2)}) collective-permute-start(bf16[48,128]{1,0:T(8,128)(2,1)S(1)} %fusion.31), channel_id=1, source_target_pairs={{0,2},{1,3},{2,0},{3,1},{4,6},{5,7},{6,4},{7,5},{8,10},{9,11},{10,... | collective-permute-start | bytes 36872 | tf_op jit(solution)/shard_map/ppermute | solution.py:21
  99.4 5.4 %collective-permute-start.14 = (bf16[48,128]{1,0:T(8,128)(2,1)S(1)}, bf16[48,128]{1,0:T(8,128)(2,1)S(1)}, u32[]{:S(2)}, u32[]{:S(2)}) collective-permute-start(bf16[48,128]{1,0:T(8,128)(2,1)S(1)} %fusion.31), channel_id=1, source_target_pairs={{0,3},{1,0},{2,1},{3,2},{4,7},{5,4},{6,5},{7,6},{8,11},{9,8},{10,9... | collective-permute-start | bytes 36872 | tf_op jit(solution)/shard_map/ppermute | solution.py:21
  102.7 4.1 %collective-permute-start.27 = (f32[2,2,128,128]{3,2,1,0:T(8,128)S(1)}, f32[2,2,128,128]{3,2,1,0:T(8,128)S(1)}, u32[]{:S(2)}, u32[]{:S(2)}) collective-permute-start(f32[2,2,128,128]{3,2,1,0:T(8,128)S(1)} %dynamic-slice_bitcast_fusion.1), channel_id=1, source_target_pairs={{0,4},{4,0},{8,12},{12,8},{16,20},{20,16},{24,28},{28,24},{1,5},{5... | collective-permute-start | bytes 786440 | tf_op jit(solution)/shard_map/ppermute | solution.py:16
  105.6 4.2 %collective-permute-start.15 = (bf16[192,128]{1,0:T(8,128)(2,1)S(1)}, bf16[192,128]{1,0:T(8,128)(2,1)S(1)}, u32[]{:S(2)}, u32[]{:S(2)}) collective-permute-start(bf16[192,128]{1,0:T(8,128)(2,1)S(1)} %bitcast_select_fusion), channel_id=1, source_target_pairs={{0,16},{4,20},{8,24},{12,28},{16,0},{20,4},{24,8},{28,12},{1,17},{... | collective-permute-start | bytes 147464 | tf_op jit(solution)/shard_map/ppermute | solution.py:16
  106.9 4.3 %collective-permute-start.28 = (bf16[2,128,128]{2,1,0:T(8,128)(2,1)S(1)}, bf16[2,128,128]{2,1,0:T(8,128)(2,1)S(1)}, u32[]{:S(2)}, u32[]{:S(2)}) collective-permute-start(bf16[2,128,128]{2,1,0:T(8,128)(2,1)S(1)} %fusion.26), channel_id=1, source_target_pairs={{0,8},{4,12},{8,0},{12,4},{16,24},{20,28},{24,16},{28,20},{1,9},{5... | collective-permute-start | bytes 196616 | tf_op jit(solution)/shard_map/ppermute | solution.py:16
  111.2 4.0 %collective-permute-start.29 = (bf16[128,128]{1,0:T(8,128)(2,1)S(1)}, bf16[128,128]{1,0:T(8,128)(2,1)S(1)}, u32[]{:S(2)}, u32[]{:S(2)}) collective-permute-start(bf16[128,128]{1,0:T(8,128)(2,1)S(1)} %fusion.28), channel_id=1, source_target_pairs={{0,16},{4,20},{8,24},{12,28},{16,0},{20,4},{24,8},{28,12},{1,17},{... | collective-permute-start | bytes 98312 | tf_op jit(solution)/shard_map/ppermute | solution.py:16
  112.2 8.2 %collective-permute-start.16 = (bf16[2,192,128]{2,1,0:T(8,128)(2,1)S(1)}, bf16[2,192,128]{2,1,0:T(8,128)(2,1)S(1)}, u32[]{:S(2)}, u32[]{:S(2)}) collective-permute-start(bf16[2,192,128]{2,1,0:T(8,128)(2,1)S(1)} %pad_maximum_fusion.6), channel_id=1, source_target_pairs={{0,8},{4,12},{8,0},{12,4},{16,24},{20,28},{24,16},{28,20},{1,9},{5... | collective-permute-start | bytes 294920 | tf_op jit(solution)/shard_map/ppermute | solution.py:16
  115.2 5.6 %collective-permute-start.30 = (f32[32,128]{1,0:T(8,128)S(1)}, f32[32,128]{1,0:T(8,128)S(1)}, u32[]{:S(2)}, u32[]{:S(2)}) collective-permute-start(f32[32,128]{1,0:T(8,128)S(1)} %get-tuple-element.38), channel_id=1, source_target_pairs={{0,1},{1,2},{2,3},{3,0},{4,5},{5,6},{6,7},{7,4},{8,9},{9,10},{10,1... | collective-permute-start | bytes 49160 | tf_op jit(solution)/shard_map/ppermute | solution.py:21
  117.9 4.7 %collective-permute-start.31 = (f32[32,128]{1,0:T(8,128)S(1)}, f32[32,128]{1,0:T(8,128)S(1)}, u32[]{:S(2)}, u32[]{:S(2)}) collective-permute-start(f32[32,128]{1,0:T(8,128)S(1)} %get-tuple-element.40), channel_id=1, source_target_pairs={{0,2},{1,3},{2,0},{3,1},{4,6},{5,7},{6,4},{7,5},{8,10},{9,11},{10,... | collective-permute-start | bytes 49160 | tf_op jit(solution)/shard_map/ppermute | solution.py:21
  119.1 3.7 %collective-permute-start.32 = (f32[32,128]{1,0:T(8,128)S(1)}, f32[32,128]{1,0:T(8,128)S(1)}, u32[]{:S(2)}, u32[]{:S(2)}) collective-permute-start(f32[32,128]{1,0:T(8,128)S(1)} %get-tuple-element.39), channel_id=1, source_target_pairs={{0,3},{1,0},{2,1},{3,2},{4,7},{5,4},{6,5},{7,6},{8,11},{9,8},{10,9... | collective-permute-start | bytes 49160 | tf_op jit(solution)/shard_map/ppermute | solution.py:21
  122.9 5.5 %collective-permute-start.33 = (bf16[32,128]{1,0:T(8,128)(2,1)S(1)}, bf16[32,128]{1,0:T(8,128)(2,1)S(1)}, u32[]{:S(2)}, u32[]{:S(2)}) collective-permute-start(bf16[32,128]{1,0:T(8,128)(2,1)S(1)} %fusion.34), channel_id=1, source_target_pairs={{0,1},{1,2},{2,3},{3,0},{4,5},{5,6},{6,7},{7,4},{8,9},{9,10},{10,1... | collective-permute-start | bytes 24584 | tf_op jit(solution)/shard_map/ppermute | solution.py:21
  123.5 4.9 %collective-permute-start.34 = (bf16[32,128]{1,0:T(8,128)(2,1)S(1)}, bf16[32,128]{1,0:T(8,128)(2,1)S(1)}, u32[]{:S(2)}, u32[]{:S(2)}) collective-permute-start(bf16[32,128]{1,0:T(8,128)(2,1)S(1)} %fusion.34), channel_id=1, source_target_pairs={{0,2},{1,3},{2,0},{3,1},{4,6},{5,7},{6,4},{7,5},{8,10},{9,11},{10,... | collective-permute-start | bytes 24584 | tf_op jit(solution)/shard_map/ppermute | solution.py:21
  126.5 3.7 %collective-permute-start.35 = (bf16[32,128]{1,0:T(8,128)(2,1)S(1)}, bf16[32,128]{1,0:T(8,128)(2,1)S(1)}, u32[]{:S(2)}, u32[]{:S(2)}) collective-permute-start(bf16[32,128]{1,0:T(8,128)(2,1)S(1)} %fusion.34), channel_id=1, source_target_pairs={{0,3},{1,0},{2,1},{3,2},{4,7},{5,4},{6,5},{7,6},{8,11},{9,8},{10,9... | collective-permute-start | bytes 24584 | tf_op jit(solution)/shard_map/ppermute | solution.py:21
  127.6 4.3 %collective-permute-start.17 = (bf16[2,2,192,128]{3,2,1,0:T(8,128)(2,1)S(1)}, bf16[2,2,192,128]{3,2,1,0:T(8,128)(2,1)S(1)}, u32[]{:S(2)}, u32[]{:S(2)}) collective-permute-start(bf16[2,2,192,128]{3,2,1,0:T(8,128)(2,1)S(1)} %pad_maximum_fusion.4), channel_id=1, source_target_pairs={{0,4},{4,0},{8,12},{12,8},{16,20},{20,16},{24,28},{28,24},{1,5},{5... | collective-permute-start | bytes 589832 | tf_op jit(solution)/shard_map/ppermute | solution.py:16
  130.9 5.2 %copy-start.14 = (f32[3,128,128]{2,1,0:T(8,128)S(1)}, f32[3,128,128]{2,1,0:T(8,128)}, u32[]{:S(2)}) copy-start(f32[3,128,128]{2,1,0:T(8,128)} %param.12) | copy-start | bytes 589828
  130.9 4.0 %collective-permute-start.36 = (bf16[128,128]{1,0:T(8,128)(2,1)S(1)}, bf16[128,128]{1,0:T(8,128)(2,1)S(1)}, u32[]{:S(2)}, u32[]{:S(2)}) collective-permute-start(bf16[128,128]{1,0:T(8,128)(2,1)S(1)} %bitcast_select_fusion.1), channel_id=1, source_target_pairs={{0,16},{4,20},{8,24},{12,28},{16,0},{20,4},{24,8},{28,12},{1,17},{... | collective-permute-start | bytes 98312 | tf_op jit(solution)/shard_map/ppermute | solution.py:16
  135.0 4.3 %collective-permute-start.37 = (bf16[2,128,128]{2,1,0:T(8,128)(2,1)S(1)}, bf16[2,128,128]{2,1,0:T(8,128)(2,1)S(1)}, u32[]{:S(2)}, u32[]{:S(2)}) collective-permute-start(bf16[2,128,128]{2,1,0:T(8,128)(2,1)S(1)} %pad_maximum_fusion.7), channel_id=1, source_target_pairs={{0,8},{4,12},{8,0},{12,4},{16,24},{20,28},{24,16},{28,20},{1,9},{5... | collective-permute-start | bytes 196616 | tf_op jit(solution)/shard_map/ppermute | solution.py:16
  136.1 4.9 %copy-start.2 = (f32[3,128,128]{2,1,0:T(8,128)}, f32[3,128,128]{2,1,0:T(8,128)S(1)}, u32[]{:S(2)}) copy-start(f32[3,128,128]{2,1,0:T(8,128)S(1)} %sub.65) | copy-start | bytes 589828
  139.3 1.6 %collective-permute-start.38 = (bf16[2,2,128,128]{3,2,0,1:T(8,128)(2,1)S(1)}, bf16[2,2,128,128]{3,2,0,1:T(8,128)(2,1)S(1)}, u32[]{:S(2)}, u32[]{:S(2)}) collective-permute-start(bf16[2,2,128,128]{3,2,0,1:T(8,128)(2,1)S(1)} %pad_maximum_fusion.5), channel_id=1, source_target_pairs={{0,4},{4,0},{8,12},{12,8},{16,20},{20,16},{24,28},{28,24},{1,5},{5... | collective-permute-start | bytes 393224 | tf_op jit(solution)/shard_map/ppermute | solution.py:16
  139.4 1.8 %copy-start.5 = (f32[8,128,128]{1,2,0:T(8,128)S(1)}, f32[8,128,128]{1,2,0:T(8,128)}, u32[]{:S(2)}) copy-start(f32[8,128,128]{1,2,0:T(8,128)} %copy.51) | copy-start | bytes 1572868
  140.9 1.9 %copy-start.6 = (f32[8,128,128]{2,1,0:T(8,128)}, f32[8,128,128]{2,1,0:T(8,128)S(1)}, u32[]{:S(2)}) copy-start(f32[8,128,128]{2,1,0:T(8,128)S(1)} %convolution_subtract_fusion) | copy-start | bytes 1572868

commit v3 on v0

v3 whole, which is shorter than its diff:
```python
import functools

import jax
import jax.numpy as jnp
import numpy as np
from jax import lax
from jax.experimental import pallas as pl
from jax.experimental.pallas import tpu as pltpu
from jax.sharding import PartitionSpec as P

F32 = jnp.float32
WIRE = jnp.bfloat16
VMEM = pl.BlockSpec(memory_space=pltpu.VMEM)
SMEM = pl.BlockSpec(memory_space=pltpu.SMEM)


def shape_of(dims, kind):
    return jax.ShapeDtypeStruct(dims, kind)


def flip(value, axis, mask):
    size = lax.axis_size(axis)
    return lax.ppermute(value, axis, [(i, i ^ mask) for i in range(size)])


def shift(value, axis, step):
    size = lax.axis_size(axis)
    return lax.ppermute(value, axis, [(i, (i + step) % size) for i in range(size)])


def ceil_to(value, step):
    return -(-value // step) * step


def params(refs):
    size = sum(int(np.prod(r.shape)) * np.dtype(r.dtype).itemsize for r in refs)
    return pltpu.CompilerParams(vmem_limit_bytes=ceil_to(size * 5 // 4, 1 << 20) + (4 << 20))


def call(kernel, name, scalars, arrays, outs, scratch=()):
    return pl.pallas_call(
        kernel,
        out_shape=outs,
        in_specs=[SMEM] * len(scalars) + [VMEM] * len(arrays),
        out_specs=[VMEM] * len(outs),
        scratch_shapes=[pltpu.VMEM(r.shape, r.dtype) for r in scratch],
        compiler_params=params([*arrays, *outs, *scratch]),
        name=name,
    )(*scalars, *arrays)


def mask_kernel(upper_pattern, lower_pattern, upper_panel, lower_panel, masked):
    uppers, lowers = upper_panel.shape[0], lower_panel.shape[0]
    for k in range(uppers):
        masked[k] = upper_panel[k] * upper_pattern[k].astype(F32).astype(jnp.bfloat16)
    for m in range(lowers):
        masked[uppers + m] = lower_panel[m] * lower_pattern[m].astype(F32).astype(jnp.bfloat16)


def turn_kernel(masked, turned):
    for k in range(masked.shape[0]):
        turned[k] = masked[k].T


def top_kernel(top, panel, out, panel_turned):
    depth, width, block, _ = top.shape
    row, col = lax.axis_index("row"), lax.axis_index("col")

    def step(m, carry):
        for o in range(depth):
            tile = top[lax.rem(col + o, depth), row ^ m].T
            out[pl.ds(pl.multiple_of(m * block, block), block), o * block : (o + 1) * block] = tile
        return carry

    lax.fori_loop(0, width, step, 0)
    for m in range(panel.shape[0]):
        panel_turned[m] = panel[m].T


def product_kernel(depth, width, uppers, parents, top, *refs):
    own, ups, downs = refs[0], refs[1:depth], refs[depth : 2 * depth - 1]
    near, far, keep, away, sums_keep, sums_away, both, forms = refs[2 * depth - 1 :]
    total, block = own.shape[0], own.shape[-1]
    lowers = total - uppers
    chunk = block // width
    row, col = lax.axis_index("row"), lax.axis_index("col")

    def piece(o, k):
        if o == 0:
            return own[k]
        return jnp.where(col + o < depth, downs[o - 1][k], ups[depth - o - 1][k])

    def columns(pair, carry):
        first = 2 * pair
        second = jnp.minimum(first + 1, total - 1)
        right = jnp.concatenate(
            [jnp.concatenate([piece(o, first), piece(o, second)], axis=1) for o in range(depth)],
            axis=0,
        )
        value = jnp.dot(top[...], right, preferred_element_type=F32)
        for half, k in enumerate((first, second)):
            part = value[:, half * block : (half + 1) * block]
            for m in range(width):
                tile = part[m * block : (m + 1) * block]
                (away if m & 1 else keep)[m // 2, k] = tile
            high = part.astype(jnp.bfloat16)
            both[k, :, :block] = high
            both[k, :, block:] = (part - high.astype(F32)).astype(jnp.bfloat16)
        return carry

    lax.fori_loop(0, ceil_to(total, 2) // 2, columns, 0)

    def fold(rows, k):
        value = jnp.dot(rows, both[k], preferred_element_type=F32)
        return value[:, :block] + value[:, block:]

    def row_of(k):
        return jnp.concatenate([(far if m & 1 else near)[m // 2, k] for m in range(width)], axis=1)

    def spread(slot, i):
        for m in range(width):
            start = pl.multiple_of((row ^ m) * chunk, chunk)
            (sums_away if m & 1 else sums_keep)[m // 2, i] = forms[slot, pl.ds(start, chunk)]

    def upper_step(k, carry):
        forms[0] = fold(row_of(k), k)
        spread(0, k)
        return carry

    def lower_step(m, carry):
        rows = jnp.concatenate([row_of(uppers + m), row_of(parents[m])], axis=0)
        value = fold(rows, uppers + m)
        forms[0] = value[:block]
        forms[1] = value[block:]
        spread(0, uppers + lowers + m)
        spread(1, uppers + m)
        return carry

    lax.fori_loop(0, uppers, upper_step, 0)
    lax.fori_loop(0, lowers, lower_step, 0)


def middle_kernel(
    depth, width, parents, upper_pattern, lower_pattern, panel, keep, *refs
):
    count = width // 2 - 1
    got, parts = refs[:count], refs[count : count + depth]
    upper_out, lower_out, total_out, order, product = refs[count + depth :]
    col = lax.axis_index("col")
    for o in range(depth):
        order[lax.rem(col + o, depth)] = parts[o][...].astype(F32)
    total = order[0]
    for c in range(1, depth):
        total = total + order[c]
    total_out[...] = total.astype(total_out.dtype)
    value = keep[...]
    for piece in got:
        value = value + piece[...].astype(F32)
    product[...] = value
    uppers, lowers = upper_out.shape[0], lower_out.shape[0]
    for k in range(uppers):
        upper_out[k] = (-product[k] * upper_pattern[k].astype(F32)).astype(jnp.bfloat16)
    for m in range(lowers):
        extension = jnp.dot(upper_out[parents[m]], panel[m], preferred_element_type=F32)
        value = -(product[uppers + m] + extension) * lower_pattern[m].astype(F32)
        lower_out[m] = value.astype(jnp.bfloat16)


def split(wide):
    high = wide.astype(jnp.bfloat16)
    return high, (wide - high.astype(F32)).astype(jnp.bfloat16)


def blocks_kernel(
    width,
    parents,
    near,
    far,
    upper_diagonal,
    lower_diagonal,
    panel,
    panel_turned,
    upper_out,
    cross_out,
    lower_out,
    sums,
    halves,
):
    uppers, lowers = upper_out.shape[0], lower_out.shape[0]
    block = panel.shape[-1]
    chunk = block // width
    row = lax.axis_index("row")
    for m in range(width):
        start = pl.multiple_of((row ^ m) * chunk, chunk)
        sums[:, pl.ds(start, chunk)] = (far if m & 1 else near)[m // 2].astype(F32)
    for k in range(uppers):
        value = upper_diagonal[k] + sums[k]
        upper_out[k] = value
        halves[k, :block], halves[k, block:] = split(value)
    for m in range(lowers):
        forms = sums[uppers + m]
        value = jnp.dot(halves[parents[m]], panel[m], preferred_element_type=F32)
        cross = forms - (value[:block] + value[block:])
        cross_out[m] = cross
        right = jnp.concatenate([forms.astype(jnp.bfloat16), *split(cross)], axis=1)
        value = jnp.dot(panel_turned[m], right, preferred_element_type=F32)
        back = value[:, :block].T + value[:, block : 2 * block] + value[:, 2 * block :]
        lower_out[m] = lower_diagonal[m] + sums[uppers + lowers + m] - back


def gather_shifts(value, axis):
    size = lax.axis_size(axis)
    return [value] + [shift(value, axis, -o) for o in range(1, size)]


def gather_line(value, axis):
    size = lax.axis_size(axis)
    ups, downs = [value], [value]
    for s in range(1, size):
        ups.append(lax.ppermute(ups[-1], axis, [(i, i + 1) for i in range(s - 1, size - 1)]))
        downs.append(lax.ppermute(downs[-1], axis, [(i + 1, i) for i in range(size - s)]))
    return ups[1:] + downs[1:]


def gather_near(value, axis):
    masks = range(2, lax.axis_size(axis), 2)
    return jnp.stack([value] + [flip(value, axis, m) for m in masks])


def tie(*values):
    return lax.optimization_barrier(values)


def scatter_flips(value, axis):
    masks = range(2, lax.axis_size(axis), 2)
    return [flip(value[m // 2].astype(WIRE), axis, m) for m in masks]


def per_device(
    top_inverse,
    upper_panel,
    upper_pattern,
    upper_diagonal,
    lower_panel,
    lower_pattern,
    parents,
    parent_panel,
    lower_diagonal,
):
    uppers, block = upper_panel.shape[0], upper_panel.shape[-1]
    lowers = lower_panel.shape[0]
    total = uppers + lowers
    sums_n = total + lowers
    width, depth = lax.axis_size("row"), lax.axis_size("col")
    half, chunk = width // 2, block // width
    bf16 = jnp.bfloat16
    upper_pattern, lower_pattern = upper_pattern.reshape(-1), lower_pattern.reshape(-1)

    (masked,) = call(
        mask_kernel,
        "mask",
        (upper_pattern, lower_pattern),
        (upper_panel.reshape(-1, block, block), lower_panel.reshape(-1, block, block)),
        [shape_of((total, block, block), bf16)],
    )
    pieces = gather_line(masked, "col")
    (turned,) = call(turn_kernel, "turn", (), (masked,), [shape_of(masked.shape, bf16)])
    near = gather_near(turned, "row")
    near, *pieces[depth - 3 :: depth - 1] = tie(near, *pieces[depth - 3 :: depth - 1])
    far = flip(near, "row", 1)
    top, panel_turned = call(
        top_kernel,
        "top",
        (),
        (top_inverse[0, :, :, 0], parent_panel),
        [shape_of((width * block, depth * block), bf16), shape_of(parent_panel.shape, bf16)],
    )

    keep, away, sums_keep, sums_away = call(
        functools.partial(product_kernel, depth, width, uppers),
        "product",
        (parents,),
        (top, masked, *pieces, near, far),
        [shape_of((half, total, block, block), F32)] * 2
        + [shape_of((half, sums_n, chunk, block), F32)] * 2,
        [
            shape_of((total, width * block, 2 * block), bf16),
            shape_of((2, block, block), F32),
        ],
    )

    other, away = tie(flip(sums_away, "row", 1), away)
    sums = sums_keep + other
    part = sums[0]
    for piece in scatter_flips(sums, "row"):
        part = part + piece.astype(F32)
    parts = gather_shifts(part.astype(WIRE), "col")

    product = keep + flip(away, "row", 1)
    got = scatter_flips(product, "row")
    upper_columns, lower_columns, part = call(
        functools.partial(middle_kernel, depth, width),
        "middle",
        (parents, upper_pattern, lower_pattern),
        (parent_panel, product[0], *got, *parts),
        [
            shape_of((uppers, block, block), bf16),
            shape_of((lowers, block, block), bf16),
            shape_of((sums_n, chunk, block), WIRE),
        ],
        [shape_of((depth, sums_n, chunk, block), F32), shape_of((total, block, block), F32)],
    )
    near = gather_near(part, "row")
    far = flip(near, "row", 1)

    upper_blocks, lower_cross, lower_blocks = call(
        functools.partial(blocks_kernel, width),
        "blocks",
        (parents,),
        (near, far, upper_diagonal, lower_diagonal, parent_panel, panel_turned),
        [
            shape_of((uppers, block, block), F32),
            shape_of((lowers, block, block), F32),
            shape_of((lowers, block, block), F32),
        ],
        [shape_of((sums_n, block, block), F32), shape_of((uppers, 2 * block, block), bf16)],
    )
    return (
        upper_columns[:, None, None],
        upper_blocks,
        lower_columns[:, None, None],
        lower_cross,
        lower_blocks,
    )


def solution(mesh):
    return jax.shard_map(
        per_device,
        mesh=mesh,
        in_specs=(
            P("row", None, None, "col", None, None),
            P(None, "row", "col", None, None),
            P(None, "row", "col"),
            P(),
            P(None, "row", "col", None, None),
            P(None, "row", "col"),
            P(),
            P(),
            P(),
        ),
        out_specs=(
            P(None, "row", "col", None, None),
            P(),
            P(None, "row", "col", None, None),
            P(),
            P(),
        ),
        check_vma=False,
    )
```

time: 299 us -> 92.1 us (0.31)
  waiting for transfers between devices: 239 us -> 40.2 us
  starting transfers between devices: 0.12 us -> 32.7 us
  blocking collectives: 19.5 us -> 0 us
  matrix products: 13.7 us -> 0 us
  Pallas kernels: 0 us -> 13.6 us
  between operations: 13.9 us -> 0.9 us
  local copies, waits for them, and re-layouts: 8.23 us -> 3.33 us
    psum x1 -> x0, waiting for transfers between devices: 132 us -> none  [per_device(): lax.psum((local_upper, local_cross), ('row', 'col'))]
    unnamed x4 -> x0, waiting for transfers between devices: 97.2 us -> none
    ppermute x0 -> x25, waiting for transfers between devices: none -> 40.2 us  [the longest x16 23.3 us: flip(): return lax.ppermute(value, axis, [(i, i ^ mask) for i in range(size)])]
    ppermute x0 -> x25, starting transfers between devices: none -> 32.7 us  [the longest x16 14.6 us: flip(): return lax.ppermute(value, axis, [(i, i ^ mask) for i in range(size)])]
    all_gather x1 -> x0, blocking collectives: 19.5 us -> none  [by_cols(): lax.all_gather(panel, 'col', axis=2, tiled=True)]
    dot_general x8 -> x0, matrix products: 13.7 us -> none  [the longest x2 6.22 us: by_cols(): jnp.einsum('aibjxy,kaixz->bjkyz', top_inverse, lax.all_gather(panel, 'col...]
    pallas_call x0 -> x6, Pallas kernels: none -> 13.6 us  [call(): pl.pallas_call(kernel, out_shape=outs, in_specs=[SMEM] * len(scalars) + [...]
    all_gather x1 -> x0, waiting for transfers between devices: 10.4 us -> none  [by_cols(): lax.all_gather(panel, 'col', axis=2, tiled=True)]
  transfers between devices with their start and end apart: 3 -> 25, of which waited for: 3 -> 15; matrix products, arithmetic and copies ran while one was open for 1% -> 1% of each run, Pallas kernels for 0% -> 1%
where the time goes in v3:
time: 92.1 us; the launch traced here: 91.8 us
  waiting for transfers between devices  40.2 us (44%)
  starting transfers between devices  32.7 us (36%)
  Pallas kernels  13.6 us (15%)
  local copies, waits for them, and re-layouts  3.33 us (4%)
  other arithmetic  1.12 us (1%)
    ppermute x16, waiting for transfers between devices, flip(): return lax.ppermute(value, axis, [(i, i ^ mask) for i in range(size)])  23.3 us
    ppermute x16, starting transfers between devices, flip(): return lax.ppermute(value, axis, [(i, i ^ mask) for i in range(size)])  14.6 us
    pallas_call x6, Pallas kernels, call(): pl.pallas_call(kernel, out_shape=outs, in_specs=[SMEM] * len(scalars) + [...  13.6 us
    ppermute x3, waiting for transfers between devices, gather_line(): lax.ppermute(downs[-1], axis, [(i + 1, i) for i in range(size - s)])  12.4 us
    ppermute x3, starting transfers between devices, shift(): lax.ppermute(value, axis, [(i, (i + step) % size) for i in range(size)])  7.18 us
    ppermute x3, starting transfers between devices, gather_line(): lax.ppermute(ups[-1], axis, [(i, i + 1) for i in range(s - 1, size - 1)])  6.95 us
    ppermute x3, waiting for transfers between devices, shift(): lax.ppermute(value, axis, [(i, (i + step) % size) for i in range(size)])  4.52 us
    ppermute x3, starting transfers between devices, gather_line(): lax.ppermute(downs[-1], axis, [(i + 1, i) for i in range(size - s)])  4 us
  transfers between devices with their start and end apart: 25, of which 15 were waited for; matrix products, arithmetic and copies ran while one was open for 1% of the time, Pallas kernels for 1%

profile of v3, /device:TPU:0, one launch (start us, length us, event | category | flops | bytes accessed | tf_op | source)
XLA Modules:
  0.0 91.8 jit_solution(3496620902373346663)
XLA Ops:
  0.6 0.9 %copy-done.3 = bf16[8,1,1,128,128]{4,3,2,1,0:T(8,128)(2,1)S(1)} copy-done((bf16[8,1,1,128,128]{4,3,2,1,0:T(8,128)(2,1)S(1)}, bf16[8,1,1,128,128]{4,3,2,1,0:T(8,128)(2,1)}, u32[]{:S(2)}) %copy-start.3) | copy-done | bytes 262168
  1.6 0.9 copy-done.5
  2.5 0.7 copy-done.7
  3.1 0.7 copy-done.9
  3.8 0.6 mask.1.masked.refs_0_
  4.4 1.3 %collective-permute-start.5 = (bf16[11,128,128]{2,1,0:T(8,128)(2,1)S(1)}, bf16[11,128,128]{2,1,0:T(8,128)(2,1)S(1)}, u32[]{:S(2)}, u32[]{:S(2)}) collective-permute-start(bf16[11,128,128]{2,1,0:T(8,128)(2,1)S(1)} %mask.1.masked.refs_0_), channel_id=1, source_target_pairs={{1,0},{2,1},{3,2},{5,4},{6,5},{7,6},{9,8},{10,9},{11,10},{13,12},{... | collective-permute-start | bytes 1081352 | tf_op jit(solution)/shard_map/ppermute | solution.py:221
  5.7 5.6 %collective-permute-start = (bf16[11,128,128]{2,1,0:T(8,128)(2,1)S(1)}, bf16[11,128,128]{2,1,0:T(8,128)(2,1)S(1)}, u32[]{:S(2)}, u32[]{:S(2)}) collective-permute-start(bf16[11,128,128]{2,1,0:T(8,128)(2,1)S(1)} %mask.1.masked.refs_0_), channel_id=1, source_target_pairs={{0,1},{1,2},{2,3},{4,5},{5,6},{6,7},{8,9},{9,10},{10,11},{12,13},{... | collective-permute-start | bytes 1081352 | tf_op jit(solution)/shard_map/ppermute | solution.py:220
  11.3 0.2 turn.1
  11.4 2.9 %collective-permute-start.3 = (bf16[11,128,128]{2,1,0:T(8,128)(2,1)S(1)}, bf16[11,128,128]{2,1,0:T(8,128)(2,1)S(1)}, u32[]{:S(2)}, u32[]{:S(2)}) collective-permute-start(bf16[11,128,128]{2,1,0:T(8,128)(2,1)S(1)} %turn.1), channel_id=1, source_target_pairs={{0,24},{4,28},{8,16},{12,20},{16,8},{20,12},{24,0},{28,4},{1,25},{... | collective-permute-start | bytes 1081352 | tf_op jit(solution)/shard_map/ppermute | solution.py:23
  14.4 0.5 collective-permute-start.2
  14.9 0.1 collective-permute-start.1
  15.0 2.7 %collective-permute-done.5.refs_4_ = bf16[11,128,128]{2,1,0:T(8,128)(2,1)S(1)} collective-permute-done((bf16[11,128,128]{2,1,0:T(8,128)(2,1)S(1)}, bf16[11,128,128]{2,1,0:T(8,128)(2,1)S(1)}, u32[]{:S(2)}, u32[]{:S(2)}) %collective-permute-start.5) | collective-permute-done | bytes 360480 | tf_op jit(solution)/shard_map/ppermute | solution.py:221
  17.7 1.3 %collective-permute-start.6 = (bf16[11,128,128]{2,1,0:T(8,128)(2,1)S(1)}, bf16[11,128,128]{2,1,0:T(8,128)(2,1)S(1)}, u32[]{:S(2)}, u32[]{:S(2)}) collective-permute-start(bf16[11,128,128]{2,1,0:T(8,128)(2,1)S(1)} %collective-permute-done.5.refs_4_), channel_id=1, source_target_pairs={{1,0},{2,1},{5,4},{6,5},{9,8},{10,9},{13,12},{14,13},{17,16},{18,1... | collective-permute-start | bytes 1081352 | tf_op jit(solution)/shard_map/ppermute | solution.py:221
  19.0 0.0 collective-permute-done.refs_1_
  19.0 0.7 collective-permute-start.4
  19.7 4.1 %collective-permute-done.3 = bf16[11,128,128]{2,1,0:T(8,128)(2,1)S(1)} collective-permute-done((bf16[11,128,128]{2,1,0:T(8,128)(2,1)S(1)}, bf16[11,128,128]{2,1,0:T(8,128)(2,1)S(1)}, u32[]{:S(2)}, u32[]{:S(2)}) %collective-permute-start.3) | collective-permute-done | bytes 360480 | tf_op jit(solution)/shard_map/ppermute | solution.py:23
  23.8 6.2 %collective-permute-done.2 = bf16[11,128,128]{2,1,0:T(8,128)(2,1)S(1)} collective-permute-done((bf16[11,128,128]{2,1,0:T(8,128)(2,1)S(1)}, bf16[11,128,128]{2,1,0:T(8,128)(2,1)S(1)}, u32[]{:S(2)}, u32[]{:S(2)}) %collective-permute-start.2) | collective-permute-done | bytes 360480 | tf_op jit(solution)/shard_map/ppermute | solution.py:23
  30.0 0.3 collective-permute-done.1
  30.3 0.2 pad_maximum_fusion.refs_7_
  30.4 0.0 collective-permute-done.6.refs_5_
  30.5 0.0 collective-permute-done.4.refs_2_
  30.5 0.1 collective-permute-start.9
  30.5 1.4 %collective-permute-start.8 = (bf16[11,128,128]{2,1,0:T(8,128)(2,1)S(1)}, bf16[11,128,128]{2,1,0:T(8,128)(2,1)S(1)}, u32[]{:S(2)}, u32[]{:S(2)}) collective-permute-start(bf16[11,128,128]{2,1,0:T(8,128)(2,1)S(1)} %collective-permute-done.6.refs_5_), channel_id=1, source_target_pairs={{1,0},{5,4},{9,8},{13,12},{17,16},{21,20},{25,24},{29,28}} | collective-permute-start | bytes 1081352 | tf_op jit(solution)/shard_map/ppermute | solution.py:221
  32.0 0.7 collective-permute-start.7
  32.7 0.8 top.1
  33.5 9.7 %collective-permute-done.8.refs_6_ = bf16[11,128,128]{2,1,0:T(8,128)(2,1)S(1)} collective-permute-done((bf16[11,128,128]{2,1,0:T(8,128)(2,1)S(1)}, bf16[11,128,128]{2,1,0:T(8,128)(2,1)S(1)}, u32[]{:S(2)}, u32[]{:S(2)}) %collective-permute-start.8) | collective-permute-done | bytes 360480 | tf_op jit(solution)/shard_map/ppermute | solution.py:221
  43.2 0.0 collective-permute-done.7.refs_3_
  43.3 7.1 %product.1 = (f32[4,11,128,128]{3,2,1,0:T(8,128)S(1)}, f32[4,11,128,128]{3,2,1,0:T(8,128)S(1)}, f32[4,19,16,128]{3,2,1,0:T(8,128)S(1)}, f32[4,19,16,128]{3,2,1,0:T(8,128)S(1)}) custom-call(s32[8]{0:T(128)S(1)} %copy-done.6, bf16[1024,512]{1,0:T(8,128)(2,1)S(1)} %get-tuple-element.22.top, bf16[11,128,128]{2,1,0:T(8,128)(2,1)S(1)} %mask.1.masked.refs_0_, ...), custom_call_target="tpu_custom_call" | custom-call | tf_op jit(solution)/shard_map/product/pallas_call | solution.py:41
  50.4 0.1 collective-permute-start.10
  50.5 2.0 %collective-permute-done.10 = f32[4,19,16,128]{3,2,1,0:T(8,128)S(1)} collective-permute-done((f32[4,19,16,128]{3,2,1,0:T(8,128)S(1)}, f32[4,19,16,128]{3,2,1,0:T(8,128)S(1)}, u32[]{:S(2)}, u32[]{:S(2)}) %collective-permute-start.10) | collective-permute-done | bytes 622624 | tf_op jit(solution)/shard_map/ppermute | solution.py:23
  52.5 0.1 collective-permute-start.11
  52.7 0.1 fusion.4
  52.8 1.6 %collective-permute-start.15 = (bf16[19,16,128]{2,1,0:T(8,128)(2,1)S(1)}, bf16[19,16,128]{2,1,0:T(8,128)(2,1)S(1)}, u32[]{:S(2)}, u32[]{:S(2)}) collective-permute-start(bf16[19,16,128]{2,1,0:T(8,128)(2,1)S(1)} %get-tuple-element.51), channel_id=1, source_target_pairs={{0,8},{4,12},{8,0},{12,4},{16,24},{20,28},{24,16},{28,20},{1,9},{5... | collective-permute-start | bytes 233480 | tf_op jit(solution)/shard_map/ppermute | solution.py:23
  54.4 1.4 %collective-permute-start.17 = (bf16[19,16,128]{2,1,0:T(8,128)(2,1)S(1)}, bf16[19,16,128]{2,1,0:T(8,128)(2,1)S(1)}, u32[]{:S(2)}, u32[]{:S(2)}) collective-permute-start(bf16[19,16,128]{2,1,0:T(8,128)(2,1)S(1)} %get-tuple-element.52), channel_id=1, source_target_pairs={{0,24},{4,28},{8,16},{12,20},{16,8},{20,12},{24,0},{28,4},{1,25},{... | collective-permute-start | bytes 233480 | tf_op jit(solution)/shard_map/ppermute | solution.py:23
  55.8 0.6 collective-permute-start.16
  56.4 1.5 %collective-permute-done.11 = f32[4,11,128,128]{3,2,1,0:T(8,128)S(1)} collective-permute-done((f32[4,11,128,128]{3,2,1,0:T(8,128)S(1)}, f32[4,11,128,128]{3,2,1,0:T(8,128)S(1)}, u32[]{:S(2)}, u32[]{:S(2)}) %collective-permute-start.11) | collective-permute-done | bytes 2883616 | tf_op jit(solution)/shard_map/ppermute | solution.py:23
  57.8 0.8 fusion.5
  58.6 0.1 slice_bitcast_fusion.1
  58.7 0.0 copy-start.8
  58.7 0.0 copy-start.10
  58.7 1.6 %collective-permute-start.14 = (bf16[11,128,128]{2,1,0:T(8,128)(2,1)S(1)}, bf16[11,128,128]{2,1,0:T(8,128)(2,1)S(1)}, u32[]{:S(2)}, u32[]{:S(2)}) collective-permute-start(bf16[11,128,128]{2,1,0:T(8,128)(2,1)S(1)} %get-tuple-element.48), channel_id=1, source_target_pairs={{0,24},{4,28},{8,16},{12,20},{16,8},{20,12},{24,0},{28,4},{1,25},{... | collective-permute-start | bytes 1081352 | tf_op jit(solution)/shard_map/ppermute | solution.py:23
  60.3 1.4 %collective-permute-start.13 = (bf16[11,128,128]{2,1,0:T(8,128)(2,1)S(1)}, bf16[11,128,128]{2,1,0:T(8,128)(2,1)S(1)}, u32[]{:S(2)}, u32[]{:S(2)}) collective-permute-start(bf16[11,128,128]{2,1,0:T(8,128)(2,1)S(1)} %get-tuple-element.49), channel_id=1, source_target_pairs={{0,16},{4,20},{8,24},{12,28},{16,0},{20,4},{24,8},{28,12},{1,17},{... | collective-permute-start | bytes 1081352 | tf_op jit(solution)/shard_map/ppermute | solution.py:23
  61.7 0.5 collective-permute-start.12
  62.3 0.1 collective-permute-start.20
  62.4 5.1 %collective-permute-start.19 = (bf16[19,16,128]{2,1,0:T(8,128)(2,1)S(1)}, bf16[19,16,128]{2,1,0:T(8,128)(2,1)S(1)}, u32[]{:S(2)}, u32[]{:S(2)}) collective-permute-start(bf16[19,16,128]{2,1,0:T(8,128)(2,1)S(1)} %fusion.3.refs_3_), channel_id=1, source_target_pairs={{0,2},{1,3},{2,0},{3,1},{4,6},{5,7},{6,4},{7,5},{8,10},{9,11},{10,... | collective-permute-start | bytes 233480 | tf_op jit(solution)/shard_map/ppermute | solution.py:28
  67.5 2.2 %collective-permute-done.20.refs_6_ = bf16[19,16,128]{2,1,0:T(8,128)(2,1)S(1)} collective-permute-done((bf16[19,16,128]{2,1,0:T(8,128)(2,1)S(1)}, bf16[19,16,128]{2,1,0:T(8,128)(2,1)S(1)}, u32[]{:S(2)}, u32[]{:S(2)}) %collective-permute-start.20) | collective-permute-done | bytes 77856 | tf_op jit(solution)/shard_map/ppermute | solution.py:28
  69.7 2.0 %collective-permute-start.18 = (bf16[19,16,128]{2,1,0:T(8,128)(2,1)S(1)}, bf16[19,16,128]{2,1,0:T(8,128)(2,1)S(1)}, u32[]{:S(2)}, u32[]{:S(2)}) collective-permute-start(bf16[19,16,128]{2,1,0:T(8,128)(2,1)S(1)} %fusion.3.refs_3_), channel_id=1, source_target_pairs={{0,3},{1,0},{2,1},{3,2},{4,7},{5,4},{6,5},{7,6},{8,11},{9,8},{10,9... | collective-permute-start | bytes 233480 | tf_op jit(solution)/shard_map/ppermute | solution.py:28
  71.7 0.0 copy-start.2
  71.8 0.0 copy-start.4
  71.8 0.5 collective-permute-done.19.refs_5_
  72.3 1.9 %collective-permute-done.18.refs_4_ = bf16[19,16,128]{2,1,0:T(8,128)(2,1)S(1)} collective-permute-done((bf16[19,16,128]{2,1,0:T(8,128)(2,1)S(1)}, bf16[19,16,128]{2,1,0:T(8,128)(2,1)S(1)}, u32[]{:S(2)}, u32[]{:S(2)}) %collective-permute-start.18) | collective-permute-done | bytes 77856 | tf_op jit(solution)/shard_map/ppermute | solution.py:28
  74.1 0.0 collective-permute-done.14.refs_2_
  74.1 3.7 %collective-permute-done.13.refs_1_ = bf16[11,128,128]{2,1,0:T(8,128)(2,1)S(1)} collective-permute-done((bf16[11,128,128]{2,1,0:T(8,128)(2,1)S(1)}, bf16[11,128,128]{2,1,0:T(8,128)(2,1)S(1)}, u32[]{:S(2)}, u32[]{:S(2)}) %collective-permute-start.13) | collective-permute-done | bytes 360480 | tf_op jit(solution)/shard_map/ppermute | solution.py:23
  77.8 0.0 collective-permute-done.12.refs_0_
  77.9 1.6 %middle.1 = (bf16[3,128,128]{2,1,0:T(8,128)(2,1)}, bf16[8,128,128]{2,1,0:T(8,128)(2,1)}, bf16[19,16,128]{2,1,0:T(8,128)(2,1)S(1)}) custom-call(s32[8]{0:T(128)S(1)} %copy-done.6, s32[3]{0:T(128)S(1)} %bitcast.49, s32[8]{0:T(128)S(1)} %bitcast.51, bf16[8,128,128]{2,1,0:T(8,128)(2,1)S(1)} %copy-done, f32[11,128,128]{2,1,0:T(8,128)S(1)} %slice_bitcast_fusion.keep, ...), custom_call_target="tpu_custom_call" | custom-call | tf_op jit(solution)/shard_map/middle/pallas_call | solution.py:41
  79.5 1.5 %collective-permute-start.23 = (bf16[19,16,128]{2,1,0:T(8,128)(2,1)S(1)}, bf16[19,16,128]{2,1,0:T(8,128)(2,1)S(1)}, u32[]{:S(2)}, u32[]{:S(2)}) collective-permute-start(bf16[19,16,128]{2,1,0:T(8,128)(2,1)S(1)} %get-tuple-element.33), channel_id=1, source_target_pairs={{0,24},{4,28},{8,16},{12,20},{16,8},{20,12},{24,0},{28,4},{1,25},{... | collective-permute-start | bytes 233480 | tf_op jit(solution)/shard_map/ppermute | solution.py:23
  81.0 1.4 %collective-permute-start.22 = (bf16[19,16,128]{2,1,0:T(8,128)(2,1)S(1)}, bf16[19,16,128]{2,1,0:T(8,128)(2,1)S(1)}, u32[]{:S(2)}, u32[]{:S(2)}) collective-permute-start(bf16[19,16,128]{2,1,0:T(8,128)(2,1)S(1)} %get-tuple-element.33), channel_id=1, source_target_pairs={{0,16},{4,20},{8,24},{12,28},{16,0},{20,4},{24,8},{28,12},{1,17},{... | collective-permute-start | bytes 233480 | tf_op jit(solution)/shard_map/ppermute | solution.py:23
  82.5 0.5 collective-permute-start.21
  83.0 2.1 %collective-permute-done.23 = bf16[19,16,128]{2,1,0:T(8,128)(2,1)S(1)} collective-permute-done((bf16[19,16,128]{2,1,0:T(8,128)(2,1)S(1)}, bf16[19,16,128]{2,1,0:T(8,128)(2,1)S(1)}, u32[]{:S(2)}, u32[]{:S(2)}) %collective-permute-start.23) | collective-permute-done | bytes 77856 | tf_op jit(solution)/shard_map/ppermute | solution.py:23
  85.1 1.2 %collective-permute-done.22 = bf16[19,16,128]{2,1,0:T(8,128)(2,1)S(1)} collective-permute-done((bf16[19,16,128]{2,1,0:T(8,128)(2,1)S(1)}, bf16[19,16,128]{2,1,0:T(8,128)(2,1)S(1)}, u32[]{:S(2)}, u32[]{:S(2)}) %collective-permute-start.22) | collective-permute-done | bytes 77856 | tf_op jit(solution)/shard_map/ppermute | solution.py:23
  86.3 0.5 collective-permute-done.21
  86.9 0.1 collective-permute-start.24
  87.0 1.6 %collective-permute-done.24.far = bf16[4,19,16,128]{3,2,1,0:T(8,128)(2,1)S(1)} collective-permute-done((bf16[4,19,16,128]{3,2,1,0:T(8,128)(2,1)S(1)}, bf16[4,19,16,128]{3,2,1,0:T(8,128)(2,1)S(1)}, u32[]{:S(2)}, u32[]{:S(2)}) %collective-permute-start.24) | collective-permute-done | bytes 311328 | tf_op jit(solution)/shard_map/ppermute | solution.py:23
  88.6 3.2 %blocks.1 = (f32[3,128,128]{2,1,0:T(8,128)}, f32[8,128,128]{2,1,0:T(8,128)}, f32[8,128,128]{2,1,0:T(8,128)}) custom-call(s32[8]{0:T(128)S(1)} %copy-done.6, bf16[4,19,16,128]{3,2,1,0:T(8,128)(2,1)S(1)} %pad_maximum_fusion.1.near, bf16[4,19,16,128]{3,2,1,0:T(8,128)(2,1)S(1)} %collective-permute-done.24.far, f32[3,128,128]{2,1,0:T(8,128)S(1)} %copy-done.4, ...), custom_call_target="tpu_custom_call" | custom-call | tf_op jit(solution)/shard_map/blocks/pallas_call | solution.py:41
  (22 shorter events, 0.2 us)
Async XLA Ops:
  0.6 1.0 %copy-start.3 = (bf16[8,1,1,128,128]{4,3,2,1,0:T(8,128)(2,1)S(1)}, bf16[8,1,1,128,128]{4,3,2,1,0:T(8,128)(2,1)}, u32[]{:S(2)}) copy-start(bf16[8,1,1,128,128]{4,3,2,1,0:T(8,128)(2,1)} %param.13) | copy-start | bytes 786436
  1.6 0.9 copy-start.5
  2.5 0.7 copy-start.7
  3.1 0.7 copy-start.9
  4.4 13.3 %collective-permute-start.5 = (bf16[11,128,128]{2,1,0:T(8,128)(2,1)S(1)}, bf16[11,128,128]{2,1,0:T(8,128)(2,1)S(1)}, u32[]{:S(2)}, u32[]{:S(2)}) collective-permute-start(bf16[11,128,128]{2,1,0:T(8,128)(2,1)S(1)} %mask.1.masked.refs_0_), channel_id=1, source_target_pairs={{1,0},{2,1},{3,2},{5,4},{6,5},{7,6},{9,8},{10,9},{11,10},{13,12},{... | collective-permute-start | bytes 1081352 | tf_op jit(solution)/shard_map/ppermute | solution.py:221
  5.7 13.3 %collective-permute-start = (bf16[11,128,128]{2,1,0:T(8,128)(2,1)S(1)}, bf16[11,128,128]{2,1,0:T(8,128)(2,1)S(1)}, u32[]{:S(2)}, u32[]{:S(2)}) collective-permute-start(bf16[11,128,128]{2,1,0:T(8,128)(2,1)S(1)} %mask.1.masked.refs_0_), channel_id=1, source_target_pairs={{0,1},{1,2},{2,3},{4,5},{5,6},{6,7},{8,9},{9,10},{10,11},{12,13},{... | collective-permute-start | bytes 1081352 | tf_op jit(solution)/shard_map/ppermute | solution.py:220
  11.4 12.3 %collective-permute-start.3 = (bf16[11,128,128]{2,1,0:T(8,128)(2,1)S(1)}, bf16[11,128,128]{2,1,0:T(8,128)(2,1)S(1)}, u32[]{:S(2)}, u32[]{:S(2)}) collective-permute-start(bf16[11,128,128]{2,1,0:T(8,128)(2,1)S(1)} %turn.1), channel_id=1, source_target_pairs={{0,24},{4,28},{8,16},{12,20},{16,8},{20,12},{24,0},{28,4},{1,25},{... | collective-permute-start | bytes 1081352 | tf_op jit(solution)/shard_map/ppermute | solution.py:23
  14.4 15.6 %collective-permute-start.2 = (bf16[11,128,128]{2,1,0:T(8,128)(2,1)S(1)}, bf16[11,128,128]{2,1,0:T(8,128)(2,1)S(1)}, u32[]{:S(2)}, u32[]{:S(2)}) collective-permute-start(bf16[11,128,128]{2,1,0:T(8,128)(2,1)S(1)} %turn.1), channel_id=1, source_target_pairs={{0,16},{4,20},{8,24},{12,28},{16,0},{20,4},{24,8},{28,12},{1,17},{... | collective-permute-start | bytes 1081352 | tf_op jit(solution)/shard_map/ppermute | solution.py:23
  14.9 15.4 %collective-permute-start.1 = (bf16[11,128,128]{2,1,0:T(8,128)(2,1)S(1)}, bf16[11,128,128]{2,1,0:T(8,128)(2,1)S(1)}, u32[]{:S(2)}, u32[]{:S(2)}) collective-permute-start(bf16[11,128,128]{2,1,0:T(8,128)(2,1)S(1)} %turn.1), channel_id=1, source_target_pairs={{0,8},{4,12},{8,0},{12,4},{16,24},{20,28},{24,16},{28,20},{1,9},{5... | collective-permute-start | bytes 1081352 | tf_op jit(solution)/shard_map/ppermute | solution.py:23
  17.7 12.7 %collective-permute-start.6 = (bf16[11,128,128]{2,1,0:T(8,128)(2,1)S(1)}, bf16[11,128,128]{2,1,0:T(8,128)(2,1)S(1)}, u32[]{:S(2)}, u32[]{:S(2)}) collective-permute-start(bf16[11,128,128]{2,1,0:T(8,128)(2,1)S(1)} %collective-permute-done.5.refs_4_), channel_id=1, source_target_pairs={{1,0},{2,1},{5,4},{6,5},{9,8},{10,9},{13,12},{14,13},{17,16},{18,1... | collective-permute-start | bytes 1081352 | tf_op jit(solution)/shard_map/ppermute | solution.py:221
  19.0 11.4 %collective-permute-start.4 = (bf16[11,128,128]{2,1,0:T(8,128)(2,1)S(1)}, bf16[11,128,128]{2,1,0:T(8,128)(2,1)S(1)}, u32[]{:S(2)}, u32[]{:S(2)}) collective-permute-start(bf16[11,128,128]{2,1,0:T(8,128)(2,1)S(1)} %collective-permute-done.refs_1_), channel_id=1, source_target_pairs={{1,2},{2,3},{5,6},{6,7},{9,10},{10,11},{13,14},{14,15},{17,18},{18... | collective-permute-start | bytes 1081352 | tf_op jit(solution)/shard_map/ppermute | solution.py:220
  30.3 2.4 %copy-start = (bf16[8,128,128]{2,1,0:T(8,128)(2,1)S(1)}, bf16[8,128,128]{2,1,0:T(8,128)(2,1)}, u32[]{:S(2)}) copy-start(bf16[8,128,128]{2,1,0:T(8,128)(2,1)} %panel.5) | copy-start | bytes 786436
  30.3 2.4 %copy-start.1 = (bf16[1,4,8,1,128,128]{5,4,3,2,1,0:T(8,128)(2,1)S(1)}, bf16[1,4,8,1,128,128]{5,4,3,2,1,0:T(8,128)(2,1)}, u32[]{:S(2)}) copy-start(bf16[1,4,8,1,128,128]{5,4,3,2,1,0:T(8,128)(2,1)} %param.9) | copy-start | bytes 3145732
  30.3 13.0 %copy-start.6 = (s32[8]{0:T(128)S(1)}, s32[8]{0:T(128)}, u32[]{:S(2)}) copy-start(s32[8]{0:T(128)} %parents.5) | copy-start | bytes 100
  30.5 12.8 %collective-permute-start.9 = (bf16[4,11,128,128]{3,2,1,0:T(8,128)(2,1)S(1)}, bf16[4,11,128,128]{3,2,1,0:T(8,128)(2,1)S(1)}, u32[]{:S(2)}, u32[]{:S(2)}) collective-permute-start(bf16[4,11,128,128]{3,2,1,0:T(8,128)(2,1)S(1)} %pad_maximum_fusion.refs_7_), channel_id=1, source_target_pairs={{0,4},{4,0},{8,12},{12,8},{16,20},{20,16},{24,28},{28,24},{1,5},{5... | collective-permute-start | bytes 4325384 | tf_op jit(solution)/shard_map/ppermute | solution.py:23
  30.5 12.7 %collective-permute-start.8 = (bf16[11,128,128]{2,1,0:T(8,128)(2,1)S(1)}, bf16[11,128,128]{2,1,0:T(8,128)(2,1)S(1)}, u32[]{:S(2)}, u32[]{:S(2)}) collective-permute-start(bf16[11,128,128]{2,1,0:T(8,128)(2,1)S(1)} %collective-permute-done.6.refs_5_), channel_id=1, source_target_pairs={{1,0},{5,4},{9,8},{13,12},{17,16},{21,20},{25,24},{29,28}} | collective-permute-start | bytes 1081352 | tf_op jit(solution)/shard_map/ppermute | solution.py:221
  32.0 11.3 %collective-permute-start.7 = (bf16[11,128,128]{2,1,0:T(8,128)(2,1)S(1)}, bf16[11,128,128]{2,1,0:T(8,128)(2,1)S(1)}, u32[]{:S(2)}, u32[]{:S(2)}) collective-permute-start(bf16[11,128,128]{2,1,0:T(8,128)(2,1)S(1)} %collective-permute-done.4.refs_2_), channel_id=1, source_target_pairs={{2,3},{6,7},{10,11},{14,15},{18,19},{22,23},{26,27},{30,31}} | collective-permute-start | bytes 1081352 | tf_op jit(solution)/shard_map/ppermute | solution.py:220
  50.4 2.1 %collective-permute-start.10 = (f32[4,19,16,128]{3,2,1,0:T(8,128)S(1)}, f32[4,19,16,128]{3,2,1,0:T(8,128)S(1)}, u32[]{:S(2)}, u32[]{:S(2)}) collective-permute-start(f32[4,19,16,128]{3,2,1,0:T(8,128)S(1)} %get-tuple-element.27), channel_id=1, source_target_pairs={{0,4},{4,0},{8,12},{12,8},{16,20},{20,16},{24,28},{28,24},{1,5},{5... | collective-permute-start | bytes 1867784 | tf_op jit(solution)/shard_map/ppermute | solution.py:23
  52.5 5.3 %collective-permute-start.11 = (f32[4,11,128,128]{3,2,1,0:T(8,128)S(1)}, f32[4,11,128,128]{3,2,1,0:T(8,128)S(1)}, u32[]{:S(2)}, u32[]{:S(2)}) collective-permute-start(f32[4,11,128,128]{3,2,1,0:T(8,128)S(1)} %get-tuple-element.29), channel_id=1, source_target_pairs={{0,4},{4,0},{8,12},{12,8},{16,20},{20,16},{24,28},{28,24},{1,5},{5... | collective-permute-start | bytes 8650760 | tf_op jit(solution)/shard_map/ppermute | solution.py:23
  52.8 9.0 %collective-permute-start.15 = (bf16[19,16,128]{2,1,0:T(8,128)(2,1)S(1)}, bf16[19,16,128]{2,1,0:T(8,128)(2,1)S(1)}, u32[]{:S(2)}, u32[]{:S(2)}) collective-permute-start(bf16[19,16,128]{2,1,0:T(8,128)(2,1)S(1)} %get-tuple-element.51), channel_id=1, source_target_pairs={{0,8},{4,12},{8,0},{12,4},{16,24},{20,28},{24,16},{28,20},{1,9},{5... | collective-permute-start | bytes 233480 | tf_op jit(solution)/shard_map/ppermute | solution.py:23
  54.4 7.9 %collective-permute-start.17 = (bf16[19,16,128]{2,1,0:T(8,128)(2,1)S(1)}, bf16[19,16,128]{2,1,0:T(8,128)(2,1)S(1)}, u32[]{:S(2)}, u32[]{:S(2)}) collective-permute-start(bf16[19,16,128]{2,1,0:T(8,128)(2,1)S(1)} %get-tuple-element.52), channel_id=1, source_target_pairs={{0,24},{4,28},{8,16},{12,20},{16,8},{20,12},{24,0},{28,4},{1,25},{... | collective-permute-start | bytes 233480 | tf_op jit(solution)/shard_map/ppermute | solution.py:23
  55.8 6.5 %collective-permute-start.16 = (bf16[19,16,128]{2,1,0:T(8,128)(2,1)S(1)}, bf16[19,16,128]{2,1,0:T(8,128)(2,1)S(1)}, u32[]{:S(2)}, u32[]{:S(2)}) collective-permute-start(bf16[19,16,128]{2,1,0:T(8,128)(2,1)S(1)} %get-tuple-element.53), channel_id=1, source_target_pairs={{0,16},{4,20},{8,24},{12,28},{16,0},{20,4},{24,8},{28,12},{1,17},{... | collective-permute-start | bytes 233480 | tf_op jit(solution)/shard_map/ppermute | solution.py:23
  58.7 19.2 %copy-start.8 = (s32[3,1,1]{0,2,1:T(1,128)S(1)}, s32[3,1,1]{0,2,1:T(1,128)}, u32[]{:S(2)}) copy-start(s32[3,1,1]{0,2,1:T(1,128)} %param.11) | copy-start | bytes 40
  58.7 19.2 %copy-start.10 = (s32[8,1,1]{0,2,1:T(1,128)S(1)}, s32[8,1,1]{0,2,1:T(1,128)}, u32[]{:S(2)}) copy-start(s32[8,1,1]{0,2,1:T(1,128)} %param.14) | copy-start | bytes 100
  58.7 15.4 %collective-permute-start.14 = (bf16[11,128,128]{2,1,0:T(8,128)(2,1)S(1)}, bf16[11,128,128]{2,1,0:T(8,128)(2,1)S(1)}, u32[]{:S(2)}, u32[]{:S(2)}) collective-permute-start(bf16[11,128,128]{2,1,0:T(8,128)(2,1)S(1)} %get-tuple-element.48), channel_id=1, source_target_pairs={{0,24},{4,28},{8,16},{12,20},{16,8},{20,12},{24,0},{28,4},{1,25},{... | collective-permute-start | bytes 1081352 | tf_op jit(solution)/shard_map/ppermute | solution.py:23
  60.3 17.5 %collective-permute-start.13 = (bf16[11,128,128]{2,1,0:T(8,128)(2,1)S(1)}, bf16[11,128,128]{2,1,0:T(8,128)(2,1)S(1)}, u32[]{:S(2)}, u32[]{:S(2)}) collective-permute-start(bf16[11,128,128]{2,1,0:T(8,128)(2,1)S(1)} %get-tuple-element.49), channel_id=1, source_target_pairs={{0,16},{4,20},{8,24},{12,28},{16,0},{20,4},{24,8},{28,12},{1,17},{... | collective-permute-start | bytes 1081352 | tf_op jit(solution)/shard_map/ppermute | solution.py:23
  61.7 16.1 %collective-permute-start.12 = (bf16[11,128,128]{2,1,0:T(8,128)(2,1)S(1)}, bf16[11,128,128]{2,1,0:T(8,128)(2,1)S(1)}, u32[]{:S(2)}, u32[]{:S(2)}) collective-permute-start(bf16[11,128,128]{2,1,0:T(8,128)(2,1)S(1)} %get-tuple-element.50), channel_id=1, source_target_pairs={{0,8},{4,12},{8,0},{12,4},{16,24},{20,28},{24,16},{28,20},{1,9},{5... | collective-permute-start | bytes 1081352 | tf_op jit(solution)/shard_map/ppermute | solution.py:23
  62.3 7.4 %collective-permute-start.20 = (bf16[19,16,128]{2,1,0:T(8,128)(2,1)S(1)}, bf16[19,16,128]{2,1,0:T(8,128)(2,1)S(1)}, u32[]{:S(2)}, u32[]{:S(2)}) collective-permute-start(bf16[19,16,128]{2,1,0:T(8,128)(2,1)S(1)} %fusion.3.refs_3_), channel_id=1, source_target_pairs={{0,1},{1,2},{2,3},{3,0},{4,5},{5,6},{6,7},{7,4},{8,9},{9,10},{10,1... | collective-permute-start | bytes 233480 | tf_op jit(solution)/shard_map/ppermute | solution.py:28
  62.4 9.9 %collective-permute-start.19 = (bf16[19,16,128]{2,1,0:T(8,128)(2,1)S(1)}, bf16[19,16,128]{2,1,0:T(8,128)(2,1)S(1)}, u32[]{:S(2)}, u32[]{:S(2)}) collective-permute-start(bf16[19,16,128]{2,1,0:T(8,128)(2,1)S(1)} %fusion.3.refs_3_), channel_id=1, source_target_pairs={{0,2},{1,3},{2,0},{3,1},{4,6},{5,7},{6,4},{7,5},{8,10},{9,11},{10,... | collective-permute-start | bytes 233480 | tf_op jit(solution)/shard_map/ppermute | solution.py:28
  69.7 4.4 %collective-permute-start.18 = (bf16[19,16,128]{2,1,0:T(8,128)(2,1)S(1)}, bf16[19,16,128]{2,1,0:T(8,128)(2,1)S(1)}, u32[]{:S(2)}, u32[]{:S(2)}) collective-permute-start(bf16[19,16,128]{2,1,0:T(8,128)(2,1)S(1)} %fusion.3.refs_3_), channel_id=1, source_target_pairs={{0,3},{1,0},{2,1},{3,2},{4,7},{5,4},{6,5},{7,6},{8,11},{9,8},{10,9... | collective-permute-start | bytes 233480 | tf_op jit(solution)/shard_map/ppermute | solution.py:28
  71.7 16.8 %copy-start.2 = (f32[8,128,128]{2,1,0:T(8,128)S(1)}, f32[8,128,128]{2,1,0:T(8,128)}, u32[]{:S(2)}) copy-start(f32[8,128,128]{2,1,0:T(8,128)} %lower_diagonal.1) | copy-start | bytes 1572868
  71.8 16.8 %copy-start.4 = (f32[3,128,128]{2,1,0:T(8,128)S(1)}, f32[3,128,128]{2,1,0:T(8,128)}, u32[]{:S(2)}) copy-start(f32[3,128,128]{2,1,0:T(8,128)} %upper_diagonal.1) | copy-start | bytes 589828
  79.5 5.6 %collective-permute-start.23 = (bf16[19,16,128]{2,1,0:T(8,128)(2,1)S(1)}, bf16[19,16,128]{2,1,0:T(8,128)(2,1)S(1)}, u32[]{:S(2)}, u32[]{:S(2)}) collective-permute-start(bf16[19,16,128]{2,1,0:T(8,128)(2,1)S(1)} %get-tuple-element.33), channel_id=1, source_target_pairs={{0,24},{4,28},{8,16},{12,20},{16,8},{20,12},{24,0},{28,4},{1,25},{... | collective-permute-start | bytes 233480 | tf_op jit(solution)/shard_map/ppermute | solution.py:23
  81.0 5.3 %collective-permute-start.22 = (bf16[19,16,128]{2,1,0:T(8,128)(2,1)S(1)}, bf16[19,16,128]{2,1,0:T(8,128)(2,1)S(1)}, u32[]{:S(2)}, u32[]{:S(2)}) collective-permute-start(bf16[19,16,128]{2,1,0:T(8,128)(2,1)S(1)} %get-tuple-element.33), channel_id=1, source_target_pairs={{0,16},{4,20},{8,24},{12,28},{16,0},{20,4},{24,8},{28,12},{1,17},{... | collective-permute-start | bytes 233480 | tf_op jit(solution)/shard_map/ppermute | solution.py:23
  82.5 4.4 %collective-permute-start.21 = (bf16[19,16,128]{2,1,0:T(8,128)(2,1)S(1)}, bf16[19,16,128]{2,1,0:T(8,128)(2,1)S(1)}, u32[]{:S(2)}, u32[]{:S(2)}) collective-permute-start(bf16[19,16,128]{2,1,0:T(8,128)(2,1)S(1)} %get-tuple-element.33), channel_id=1, source_target_pairs={{0,8},{4,12},{8,0},{12,4},{16,24},{20,28},{24,16},{28,20},{1,9},{5... | collective-permute-start | bytes 233480 | tf_op jit(solution)/shard_map/ppermute | solution.py:23
  86.9 1.7 %collective-permute-start.24 = (bf16[4,19,16,128]{3,2,1,0:T(8,128)(2,1)S(1)}, bf16[4,19,16,128]{3,2,1,0:T(8,128)(2,1)S(1)}, u32[]{:S(2)}, u32[]{:S(2)}) collective-permute-start(bf16[4,19,16,128]{3,2,1,0:T(8,128)(2,1)S(1)} %pad_maximum_fusion.1.near), channel_id=1, source_target_pairs={{0,4},{4,0},{8,12},{12,8},{16,20},{20,16},{24,28},{28,24},{1,5},{5... | collective-permute-start | bytes 933896 | tf_op jit(solution)/shard_map/ppermute | solution.py:23

commit v4 on v3

v4 whole, which is shorter than its diff:
```python
import functools

import jax
import jax.numpy as jnp
import numpy as np
from jax import lax
from jax.experimental import pallas as pl
from jax.experimental.pallas import tpu as pltpu
from jax.sharding import PartitionSpec as P

F32 = jnp.float32
WIRE = jnp.bfloat16
VMEM = pl.BlockSpec(memory_space=pltpu.VMEM)
SMEM = pl.BlockSpec(memory_space=pltpu.SMEM)


def shape_of(dims, kind):
    return jax.ShapeDtypeStruct(dims, kind)


def flip(value, axis, mask):
    size = lax.axis_size(axis)
    return lax.ppermute(value, axis, [(i, i ^ mask) for i in range(size)])


def shift(value, axis, step):
    size = lax.axis_size(axis)
    return lax.ppermute(value, axis, [(i, (i + step) % size) for i in range(size)])


def ceil_to(value, step):
    return -(-value // step) * step


def params(refs, limit):
    size = sum(int(np.prod(r.shape)) * np.dtype(r.dtype).itemsize for r in refs)
    return pltpu.CompilerParams(vmem_limit_bytes=limit or ceil_to(size * 5 // 4, 1 << 20) + (4 << 20))


def call(kernel, name, scalars, arrays, outs, scratch=(), limit=0):
    return pl.pallas_call(
        kernel,
        out_shape=outs,
        in_specs=[SMEM] * len(scalars) + [VMEM] * len(arrays),
        out_specs=[VMEM] * len(outs),
        scratch_shapes=[pltpu.VMEM(r.shape, r.dtype) for r in scratch],
        compiler_params=params([*arrays, *outs, *scratch], limit),
        name=name,
    )(*scalars, *arrays)


def mask_kernel(upper_pattern, lower_pattern, upper_panel, lower_panel, masked):
    uppers, lowers = upper_panel.shape[0], lower_panel.shape[0]
    for k in range(uppers):
        masked[k] = upper_panel[k] * upper_pattern[k].astype(F32).astype(jnp.bfloat16)
    for m in range(lowers):
        masked[uppers + m] = lower_panel[m] * lower_pattern[m].astype(F32).astype(jnp.bfloat16)


def turn_kernel(*refs):
    pieces, turned = refs[:-1], refs[-1]
    total, block = pieces[0].shape[0], pieces[0].shape[-1]
    for k in range(total):
        for o, piece in enumerate(pieces):
            turned[k, :, o * block : (o + 1) * block] = piece[k].T


def top_kernel(top, panel, out, panel_turned):
    depth, width, block, _ = top.shape
    row, col = lax.axis_index("row"), lax.axis_index("col")
    half = width // 2

    def step(o, carry):
        start = pl.multiple_of(o * block, block)
        for i in range(width):
            m = 2 * (i % half) + i // half
            tile = top[lax.rem(col + o, depth), row ^ m]
            out[i // half, pl.ds(start, block), (i % half) * block : (i % half + 1) * block] = tile
        return carry

    lax.fori_loop(0, depth, step, 0)
    for m in range(panel.shape[0]):
        panel_turned[m] = panel[m].T


def dot_pair(left, pieces, first, second):
    right = [
        jnp.concatenate([pieces[i, first], pieces[i, second]], axis=1)
        for i in range(pieces.shape[0])
    ]
    return jnp.dot(left, jnp.concatenate(right), preferred_element_type=F32)


def first_kernel(top, near, out):
    total = near.shape[1]
    for first in range(0, total, 2):
        out[first // 2] = dot_pair(top[0], near, first, min(first + 1, total - 1))


def second_kernel(uppers, parents, top, far, start, turned, *refs):
    own, returns, (sums_keep, sums_away, both, forms) = refs[0], refs[1:-4], refs[-4:]
    total, block, reach = turned.shape
    lowers = total - uppers
    half, _, chunk, _ = sums_keep.shape
    row = lax.axis_index("row")

    for first in range(0, total, 2):
        second = min(first + 1, total - 1)
        value = start[first // 2] + dot_pair(top[1], far, first, second)
        for lane, k in enumerate(range(first, second + 1)):
            part = value[:, lane * block : (lane + 1) * block]
            own[k] = part[:block]
            for o, out in enumerate(returns):
                out[k] = part[(o + 1) * block : (o + 2) * block].astype(WIRE)
            part = jnp.concatenate([0.5 * part[:block], part[block:reach]])
            high = part.astype(jnp.bfloat16)
            both[k, :, :block] = high
            both[k, :, block:] = (part - high.astype(F32)).astype(jnp.bfloat16)

    def fold(rows, k):
        value = jnp.dot(rows, both[k], preferred_element_type=F32)
        return value[:, :block] + value[:, block:]

    def spread(slot, index):
        for m in range(2 * half):
            place = pl.multiple_of((row ^ m) * chunk, chunk)
            (sums_away if m & 1 else sums_keep)[m // 2, index] = forms[slot, pl.ds(place, chunk)]

    for k in range(uppers):
        forms[k] = fold(turned[k], k)
        spread(k, k)
    for m in range(lowers):
        own_row, parent = turned[uppers + m], parents[m]
        value = fold(jnp.concatenate([own_row, turned[parent]], axis=0), uppers + m)
        slot = uppers + 2 * m
        forms[slot] = value[:block]
        forms[slot + 1] = value[block:] + fold(own_row, parent).T
        spread(slot, total + m)
        spread(slot + 1, uppers + m)


def line_kernel(*refs):
    parts, (total_out, order) = refs[:-2], refs[-2:]
    depth, col = len(parts), lax.axis_index("col")
    for o in range(depth):
        order[lax.rem(col + o, depth)] = parts[o][...].astype(F32)
    total = order[0]
    for c in range(1, depth):
        total = total + order[c]
    total_out[...] = total.astype(total_out.dtype)


def columns_kernel(parents, upper_pattern, lower_pattern, panel, own, *refs):
    got, (upper_out, lower_out) = refs[:-2], refs[-2:]
    uppers, lowers = upper_out.shape[0], lower_out.shape[0]

    def product(k):
        value = own[k]
        for piece in got:
            value = value + piece[k].astype(F32)
        return value

    for k in range(uppers):
        upper_out[k] = (-product(k) * upper_pattern[k].astype(F32)).astype(jnp.bfloat16)
    for m in range(lowers):
        extension = jnp.dot(upper_out[parents[m]], panel[m], preferred_element_type=F32)
        value = -(product(uppers + m) + extension) * lower_pattern[m].astype(F32)
        lower_out[m] = value.astype(jnp.bfloat16)


def split(wide):
    high = wide.astype(jnp.bfloat16)
    return high, (wide - high.astype(F32)).astype(jnp.bfloat16)


def blocks_kernel(
    width,
    parents,
    near,
    far,
    upper_diagonal,
    lower_diagonal,
    panel,
    panel_turned,
    upper_out,
    cross_out,
    lower_out,
    sums,
    halves,
):
    uppers, lowers = upper_out.shape[0], lower_out.shape[0]
    block = panel.shape[-1]
    chunk = block // width
    row = lax.axis_index("row")
    for m in range(width):
        start = pl.multiple_of((row ^ m) * chunk, chunk)
        sums[:, pl.ds(start, chunk)] = (far if m & 1 else near)[m // 2].astype(F32)
    for k in range(uppers):
        value = upper_diagonal[k] + (sums[k] + sums[k].T)
        upper_out[k] = value
        halves[k, :block], halves[k, block:] = split(value)
    for m in range(lowers):
        forms = sums[uppers + m]
        value = jnp.dot(halves[parents[m]], panel[m], preferred_element_type=F32)
        cross = forms - (value[:block] + value[block:])
        cross_out[m] = cross
        right = jnp.concatenate([forms.astype(jnp.bfloat16), *split(cross)], axis=1)
        value = jnp.dot(panel_turned[m], right, preferred_element_type=F32)
        back = value[:, :block].T + value[:, block : 2 * block] + value[:, 2 * block :]
        square = sums[uppers + lowers + m]
        lower_out[m] = lower_diagonal[m] + (square + square.T) - back


def gather_shifts(value, axis):
    size = lax.axis_size(axis)
    return [value] + [shift(value, axis, -o) for o in range(1, size)]


def gather_pairs(value, axis):
    size = lax.axis_size(axis)
    pieces = [value]
    for o in range(1, size // 2 + 1):
        takers = range(size)
        if 2 * o == size:
            takers = [c if c % 2 == 0 else c + o for c in range(o)]
        pieces.append(lax.ppermute(value, axis, [((c + o) % size, c) for c in takers]))
    return pieces


def gather_near(value, axis):
    masks = range(2, lax.axis_size(axis), 2)
    return jnp.stack([value] + [flip(value, axis, m) for m in masks])


def scatter_flips(value, axis):
    masks = range(2, lax.axis_size(axis), 2)
    return [flip(value[m // 2].astype(WIRE), axis, m) for m in masks]


def tie(*values):
    return lax.optimization_barrier(values)


def per_device(
    top_inverse,
    upper_panel,
    upper_pattern,
    upper_diagonal,
    lower_panel,
    lower_pattern,
    parents,
    parent_panel,
    lower_diagonal,
):
    uppers, block = upper_panel.shape[0], upper_panel.shape[-1]
    lowers = lower_panel.shape[0]
    total = uppers + lowers
    sums_n = total + lowers
    width, depth = lax.axis_size("row"), lax.axis_size("col")
    half, chunk = width // 2, block // width
    bf16 = jnp.bfloat16
    upper_pattern, lower_pattern = upper_pattern.reshape(-1), lower_pattern.reshape(-1)

    (masked,) = call(
        mask_kernel,
        "mask",
        (upper_pattern, lower_pattern),
        (upper_panel.reshape(-1, block, block), lower_panel.reshape(-1, block, block)),
        [shape_of((total, block, block), bf16)],
        limit=60 << 20,
    )
    near, *pieces = tie(gather_near(masked, "row"), *gather_pairs(masked, "col"))
    far = flip(near, "row", 1)
    top, panel_turned = call(
        top_kernel,
        "top",
        (),
        (top_inverse[0, :, :, 0], parent_panel),
        [shape_of((2, depth * block, half * block), bf16), shape_of(parent_panel.shape, bf16)],
    )
    reach = len(pieces) * block
    (turned,) = call(turn_kernel, "turn", (), pieces, [shape_of((total, block, reach), bf16)])
    pairs = ceil_to(total, 2) // 2
    (start,) = call(
        first_kernel, "first", (), (top, near), [shape_of((pairs, depth * block, 2 * block), F32)]
    )
    own, *rest = call(
        functools.partial(second_kernel, uppers),
        "second",
        (parents,),
        (top, far, start, turned),
        [shape_of((total, block, block), F32)]
        + [shape_of((total, block, block), WIRE)] * (depth - 1)
        + [shape_of((half, sums_n, chunk, block), F32)] * 2,
        [shape_of((total, reach, 2 * block), bf16), shape_of((sums_n, block, block), F32)],
    )
    returns, (sums_keep, sums_away) = rest[:-2], rest[-2:]

    other, *returns = tie(flip(sums_away, "row", 1), *returns)
    sums = sums_keep + other
    middle = depth // 2
    part = sums[0]
    for piece in scatter_flips(sums, "row"):
        part = part + piece.astype(F32)
    parts = gather_shifts(part.astype(WIRE), "col")
    got = [shift(returns[o - 1], "col", o) for o in range(1, depth) if o == middle]
    tied = tie(*parts, *got)
    parts, got = tied[:depth], tied[depth:]
    (part,) = call(
        line_kernel,
        "line",
        (),
        parts,
        [shape_of((sums_n, chunk, block), WIRE)],
        [shape_of((depth, sums_n, chunk, block), F32)],
    )
    near = gather_near(part, "row")
    near, *more = tie(near, *[shift(returns[o - 1], "col", o) for o in range(1, middle)])
    part, *returns = tie(part, *returns)
    got = [*got, *more, *[shift(returns[o - 1], "col", o) for o in range(middle + 1, depth)]]
    far = flip(near, "row", 1)

    upper_columns, lower_columns = call(
        columns_kernel,
        "columns",
        (parents, upper_pattern, lower_pattern),
        (parent_panel, own, *got),
        [
            shape_of((uppers, block, block), bf16),
            shape_of((lowers, block, block), bf16),
        ],
    )
    upper_blocks, lower_cross, lower_blocks = call(
        functools.partial(blocks_kernel, width),
        "blocks",
        (parents,),
        (near, far, upper_diagonal, lower_diagonal, parent_panel, panel_turned),
        [
            shape_of((uppers, block, block), F32),
            shape_of((lowers, block, block), F32),
            shape_of((lowers, block, block), F32),
        ],
        [shape_of((sums_n, block, block), F32), shape_of((uppers, 2 * block, block), bf16)],
    )
    return (
        upper_columns[:, None, None],
        upper_blocks,
        lower_columns[:, None, None],
        lower_cross,
        lower_blocks,
    )


def solution(mesh):
    return jax.shard_map(
        per_device,
        mesh=mesh,
        in_specs=(
            P("row", None, None, "col", None, None),
            P(None, "row", "col", None, None),
            P(None, "row", "col"),
            P(),
            P(None, "row", "col", None, None),
            P(None, "row", "col"),
            P(),
            P(),
            P(),
        ),
        out_specs=(
            P(None, "row", "col", None, None),
            P(),
            P(None, "row", "col", None, None),
            P(),
            P(),
        ),
        check_vma=False,
    )
```

time: 92.1 us -> 88.6 us (0.962)
  waiting for transfers between devices: 40.2 us -> 47.2 us
  starting transfers between devices: 32.7 us -> 27.9 us
  local copies, waits for them, and re-layouts: 3.33 us -> 0.06 us
  Pallas kernels: 13.6 us -> 11.1 us
    ppermute x3 -> x6, waiting for transfers between devices: 4.52 us -> 27.5 us  [shift(): lax.ppermute(value, axis, [(i, (i + step) % size) for i in range(size)])]
    ppermute x6 -> x2, waiting for transfers between devices: 12.4 us -> 2.95 us  [gather_pairs(): lax.ppermute(value, axis, [((c + o) % size, c) for c in takers])]
    ppermute x16 -> x12, waiting for transfers between devices: 23.3 us -> 16.7 us  [flip(): return lax.ppermute(value, axis, [(i, i ^ mask) for i in range(size)])]
    ppermute x6 -> x2, starting transfers between devices: 10.9 us -> 5.41 us  [gather_pairs(): lax.ppermute(value, axis, [((c + o) % size, c) for c in takers])]
    ppermute x3 -> x6, starting transfers between devices: 7.18 us -> 10.6 us  [shift(): lax.ppermute(value, axis, [(i, (i + step) % size) for i in range(size)])]
    unnamed x22 -> x16, local copies, waits for them, and re-layouts: 3.18 us -> 0.05 us
    ppermute x16 -> x12, starting transfers between devices: 14.6 us -> 11.9 us  [flip(): return lax.ppermute(value, axis, [(i, i ^ mask) for i in range(size)])]
    pallas_call x6 -> x8, Pallas kernels: 13.6 us -> 11.1 us  [call(): pl.pallas_call(kernel, out_shape=outs, in_specs=[SMEM] * len(scalars) + [...]
  transfers between devices with their start and end apart: 25 -> 20, of which waited for: 15 -> 13; matrix products, arithmetic and copies ran while one was open for 1% -> 2% of each run, Pallas kernels for 1% -> 4%
where the time goes in v4:
time: 88.6 us; the launch traced here: 88.4 us
  waiting for transfers between devices  47.2 us (53%)
  starting transfers between devices  27.9 us (31%)
  Pallas kernels  11.1 us (13%)
  other arithmetic  1.45 us (2%)
    ppermute x6, waiting for transfers between devices, shift(): lax.ppermute(value, axis, [(i, (i + step) % size) for i in range(size)])  27.5 us
    ppermute x12, waiting for transfers between devices, flip(): return lax.ppermute(value, axis, [(i, i ^ mask) for i in range(size)])  16.7 us
    ppermute x12, starting transfers between devices, flip(): return lax.ppermute(value, axis, [(i, i ^ mask) for i in range(size)])  11.9 us
    pallas_call x8, Pallas kernels, call(): pl.pallas_call(kernel, out_shape=outs, in_specs=[SMEM] * len(scalars) + [...  11.1 us
    ppermute x6, starting transfers between devices, shift(): lax.ppermute(value, axis, [(i, (i + step) % size) for i in range(size)])  10.6 us
    ppermute x2, starting transfers between devices, gather_pairs(): lax.ppermute(value, axis, [((c + o) % size, c) for c in takers])  5.41 us
    ppermute x2, waiting for transfers between devices, gather_pairs(): lax.ppermute(value, axis, [((c + o) % size, c) for c in takers])  2.95 us
  transfers between devices with their start and end apart: 20, of which 13 were waited for; matrix products, arithmetic and copies ran while one was open for 2% of the time, Pallas kernels for 4%

profile of v4, /device:TPU:0, one launch (start us, length us, event | category | flops | bytes accessed | tf_op | source)
XLA Modules:
  0.0 88.4 jit_solution(17801703176105910470)
XLA Ops:
  0.6 1.8 %mask.1.refs_0_ = bf16[11,128,128]{2,1,0:T(8,128)(2,1)} custom-call(s32[3]{0:T(128)} %bitcast.38, s32[8]{0:T(128)} %bitcast.40, bf16[3,128,128]{2,1,0:T(8,128)(2,1)} %bitcast.46, bf16[8,128,128]{2,1,0:T(8,128)(2,1)} %bitcast.45), custom_call_target="tpu_custom_call" | custom-call | tf_op jit(solution)/shard_map/mask/pallas_call | solution.py:41
  2.4 3.9 %collective-permute-start.2 = (bf16[11,128,128]{2,1,0:T(8,128)(2,1)}, bf16[11,128,128]{2,1,0:T(8,128)(2,1)S(1)}, u32[]{:S(2)}, u32[]{:S(2)}) collective-permute-start(bf16[11,128,128]{2,1,0:T(8,128)(2,1)} %mask.1.refs_0_), channel_id=1, source_target_pairs={{0,24},{4,28},{8,16},{12,20},{16,8},{20,12},{24,0},{28,4},{1,25},{... | collective-permute-start | bytes 1081352 | tf_op jit(solution)/shard_map/ppermute | solution.py:23
  6.3 0.5 collective-permute-start.1
  6.8 0.1 collective-permute-start
  6.9 1.3 %collective-permute-start.4 = (bf16[11,128,128]{2,1,0:T(8,128)(2,1)}, bf16[11,128,128]{2,1,0:T(8,128)(2,1)S(1)}, u32[]{:S(2)}, u32[]{:S(2)}) collective-permute-start(bf16[11,128,128]{2,1,0:T(8,128)(2,1)} %mask.1.refs_0_), channel_id=1, source_target_pairs={{2,0},{1,3},{6,4},{5,7},{10,8},{9,11},{14,12},{13,15},{18,16},{17,... | collective-permute-start | bytes 1081352 | tf_op jit(solution)/shard_map/ppermute | solution.py:226
  8.2 4.1 %collective-permute-start.3 = (bf16[11,128,128]{2,1,0:T(8,128)(2,1)}, bf16[11,128,128]{2,1,0:T(8,128)(2,1)S(1)}, u32[]{:S(2)}, u32[]{:S(2)}) collective-permute-start(bf16[11,128,128]{2,1,0:T(8,128)(2,1)} %mask.1.refs_0_), channel_id=1, source_target_pairs={{1,0},{2,1},{3,2},{0,3},{5,4},{6,5},{7,6},{4,7},{9,8},{10,9},{11,1... | collective-permute-start | bytes 1081352 | tf_op jit(solution)/shard_map/ppermute | solution.py:226
  12.3 3.5 %collective-permute-done.2 = bf16[11,128,128]{2,1,0:T(8,128)(2,1)S(1)} collective-permute-done((bf16[11,128,128]{2,1,0:T(8,128)(2,1)}, bf16[11,128,128]{2,1,0:T(8,128)(2,1)S(1)}, u32[]{:S(2)}, u32[]{:S(2)}) %collective-permute-start.2) | collective-permute-done | bytes 360480 | tf_op jit(solution)/shard_map/ppermute | solution.py:23
  15.8 6.9 %collective-permute-done.1 = bf16[11,128,128]{2,1,0:T(8,128)(2,1)S(1)} collective-permute-done((bf16[11,128,128]{2,1,0:T(8,128)(2,1)}, bf16[11,128,128]{2,1,0:T(8,128)(2,1)S(1)}, u32[]{:S(2)}, u32[]{:S(2)}) %collective-permute-start.1) | collective-permute-done | bytes 360480 | tf_op jit(solution)/shard_map/ppermute | solution.py:23
  22.7 0.3 collective-permute-done
  23.0 1.3 %pad_maximum_fusion.near = bf16[4,11,128,128]{3,2,1,0:T(8,128)(2,1)S(1)} fusion(bf16[1,11,128,128]{3,2,1,0:T(8,128)(2,1)S(1)} %bitcast.42, bf16[1,11,128,128]{3,2,1,0:T(8,128)(2,1)S(1)} %bitcast.43, bf16[1,11,128,128]{3,2,1,0:T(8,128)(2,1)S(1)} %bitcast.44, bf16[1,11,128,128]{3,2,1,0:T(8,128)(2,1)} %bitcast.35), kind=kLoop, calls=%fused_computation | loop fusion | flops 2162688 | bytes 2883584 | tf_op jit(solution)/shard_map/stack | solution.py:232
  24.2 0.0 collective-permute-done.4.refs_2_
  24.3 2.9 %collective-permute-done.3.refs_1_ = bf16[11,128,128]{2,1,0:T(8,128)(2,1)S(1)} collective-permute-done((bf16[11,128,128]{2,1,0:T(8,128)(2,1)}, bf16[11,128,128]{2,1,0:T(8,128)(2,1)S(1)}, u32[]{:S(2)}, u32[]{:S(2)}) %collective-permute-start.3) | collective-permute-done | bytes 360480 | tf_op jit(solution)/shard_map/ppermute | solution.py:226
  27.2 0.0 collective-permute-start.5
  27.2 0.0 copy-done.1
  27.2 0.0 copy-done.2
  27.2 0.3 top.1
  27.6 0.0 copy-start
  27.6 1.0 %first.1.start = f32[6,512,256]{2,1,0:T(8,128)S(1)} custom-call(bf16[2,512,512]{2,1,0:T(8,128)(2,1)S(1)} %get-tuple-element.34.top, bf16[4,11,128,128]{3,2,1,0:T(8,128)(2,1)S(1)} %pad_maximum_fusion.near), custom_call_target="tpu_custom_call" | custom-call | tf_op jit(solution)/shard_map/first/pallas_call | solution.py:41
  28.6 0.0 copy-done
  28.6 0.0 copy-start.5
  28.6 0.3 turn.1.turned
  29.0 1.5 %collective-permute-done.5.far = bf16[4,11,128,128]{3,2,1,0:T(8,128)(2,1)S(1)} collective-permute-done((bf16[4,11,128,128]{3,2,1,0:T(8,128)(2,1)S(1)}, bf16[4,11,128,128]{3,2,1,0:T(8,128)(2,1)S(1)}, u32[]{:S(2)}, u32[]{:S(2)}) %collective-permute-start.5) | collective-permute-done | bytes 1441824 | tf_op jit(solution)/shard_map/ppermute | solution.py:23
  30.4 0.0 copy-done.5
  30.4 2.6 %second.1 = (f32[11,128,128]{2,1,0:T(8,128)S(1)}, bf16[11,128,128]{2,1,0:T(8,128)(2,1)S(1)}, bf16[11,128,128]{2,1,0:T(8,128)(2,1)S(1)}, bf16[11,128,128]{2,1,0:T...) custom-call(s32[8]{0:T(128)S(1)} %copy-done.5, ...), custom_call_target="tpu_custom_call" | custom-call | tf_op jit(solution)/shard_map/second/pallas_call | solution.py:41
  33.0 0.2 collective-permute-start.6
  33.2 1.9 %collective-permute-done.6 = f32[4,19,16,128]{3,2,1,0:T(8,128)S(1)} collective-permute-done((f32[4,19,16,128]{3,2,1,0:T(8,128)S(1)}, f32[4,19,16,128]{3,2,1,0:T(8,128)S(1)}, u32[]{:S(2)}, u32[]{:S(2)}) %collective-permute-start.6) | collective-permute-done | bytes 622624 | tf_op jit(solution)/shard_map/ppermute | solution.py:23
  35.2 0.1 fusion.4
  35.3 0.0 copy-start.6
  35.3 0.0 copy-start.7
  35.3 1.8 %collective-permute-start.7 = (bf16[19,16,128]{2,1,0:T(8,128)(2,1)S(1)}, bf16[19,16,128]{2,1,0:T(8,128)(2,1)S(1)}, u32[]{:S(2)}, u32[]{:S(2)}) collective-permute-start(bf16[19,16,128]{2,1,0:T(8,128)(2,1)S(1)} %get-tuple-element.70), channel_id=1, source_target_pairs={{0,8},{4,12},{8,0},{12,4},{16,24},{20,28},{24,16},{28,20},{1,9},{5... | collective-permute-start | bytes 233480 | tf_op jit(solution)/shard_map/ppermute | solution.py:23
  37.1 1.5 %collective-permute-start.9 = (bf16[19,16,128]{2,1,0:T(8,128)(2,1)S(1)}, bf16[19,16,128]{2,1,0:T(8,128)(2,1)S(1)}, u32[]{:S(2)}, u32[]{:S(2)}) collective-permute-start(bf16[19,16,128]{2,1,0:T(8,128)(2,1)S(1)} %get-tuple-element.71), channel_id=1, source_target_pairs={{0,24},{4,28},{8,16},{12,20},{16,8},{20,12},{24,0},{28,4},{1,25},{... | collective-permute-start | bytes 233480 | tf_op jit(solution)/shard_map/ppermute | solution.py:23
  38.6 0.3 collective-permute-start.8
  38.9 0.0 collective-permute-start.13
  38.9 4.4 %collective-permute-start.17 = (bf16[11,128,128]{2,1,0:T(8,128)(2,1)S(1)}, bf16[11,128,128]{2,1,0:T(8,128)(2,1)S(1)}, u32[]{:S(2)}, u32[]{:S(2)}) collective-permute-start(bf16[11,128,128]{2,1,0:T(8,128)(2,1)S(1)} %get-tuple-element.52), channel_id=1, source_target_pairs={{0,1},{1,2},{2,3},{3,0},{4,5},{5,6},{6,7},{7,4},{8,9},{9,10},{10,1... | collective-permute-start | bytes 1081352 | tf_op jit(solution)/shard_map/ppermute | solution.py:28
  43.2 0.0 collective-permute-done.7
  43.2 0.0 collective-permute-done.9
  43.2 0.7 collective-permute-done.8
  44.0 0.9 %collective-permute-start.12 = (bf16[19,16,128]{2,1,0:T(8,128)(2,1)S(1)}, bf16[19,16,128]{2,1,0:T(8,128)(2,1)S(1)}, u32[]{:S(2)}, u32[]{:S(2)}) collective-permute-start(bf16[19,16,128]{2,1,0:T(8,128)(2,1)S(1)} %fusion.3.refs_0_), channel_id=1, source_target_pairs={{0,1},{1,2},{2,3},{3,0},{4,5},{5,6},{6,7},{7,4},{8,9},{9,10},{10,1... | collective-permute-start | bytes 233480 | tf_op jit(solution)/shard_map/ppermute | solution.py:28
  44.9 3.3 %collective-permute-start.11 = (bf16[19,16,128]{2,1,0:T(8,128)(2,1)S(1)}, bf16[19,16,128]{2,1,0:T(8,128)(2,1)S(1)}, u32[]{:S(2)}, u32[]{:S(2)}) collective-permute-start(bf16[19,16,128]{2,1,0:T(8,128)(2,1)S(1)} %fusion.3.refs_0_), channel_id=1, source_target_pairs={{0,2},{1,3},{2,0},{3,1},{4,6},{5,7},{6,4},{7,5},{8,10},{9,11},{10,... | collective-permute-start | bytes 233480 | tf_op jit(solution)/shard_map/ppermute | solution.py:28
  48.2 0.0 collective-permute-start.10
  48.2 13.2 %collective-permute-done.12.refs_3_ = bf16[19,16,128]{2,1,0:T(8,128)(2,1)S(1)} collective-permute-done((bf16[19,16,128]{2,1,0:T(8,128)(2,1)S(1)}, bf16[19,16,128]{2,1,0:T(8,128)(2,1)S(1)}, u32[]{:S(2)}, u32[]{:S(2)}) %collective-permute-start.12) | collective-permute-done | bytes 77856 | tf_op jit(solution)/shard_map/ppermute | solution.py:28
  61.4 9.3 %collective-permute-done.11.refs_2_ = bf16[19,16,128]{2,1,0:T(8,128)(2,1)S(1)} collective-permute-done((bf16[19,16,128]{2,1,0:T(8,128)(2,1)S(1)}, bf16[19,16,128]{2,1,0:T(8,128)(2,1)S(1)}, u32[]{:S(2)}, u32[]{:S(2)}) %collective-permute-start.11) | collective-permute-done | bytes 77856 | tf_op jit(solution)/shard_map/ppermute | solution.py:28
  70.7 0.0 collective-permute-done.10.refs_1_
  70.7 0.0 collective-permute-done.13.refs_0_
  70.7 0.1 line.1
  70.8 0.0 copy-start.3
  70.8 0.0 copy-start.4
  70.9 2.7 %collective-permute-start.16 = (bf16[19,16,128]{2,1,0:T(8,128)(2,1)S(1)}, bf16[19,16,128]{2,1,0:T(8,128)(2,1)S(1)}, u32[]{:S(2)}, u32[]{:S(2)}) collective-permute-start(bf16[19,16,128]{2,1,0:T(8,128)(2,1)S(1)} %line.1), channel_id=1, source_target_pairs={{0,24},{4,28},{8,16},{12,20},{16,8},{20,12},{24,0},{28,4},{1,25},{... | collective-permute-start | bytes 233480 | tf_op jit(solution)/shard_map/ppermute | solution.py:23
  73.5 0.5 collective-permute-start.15
  74.0 0.4 collective-permute-start.14
  74.4 2.0 %collective-permute-start.18 = (bf16[11,128,128]{2,1,0:T(8,128)(2,1)S(1)}, bf16[11,128,128]{2,1,0:T(8,128)(2,1)S(1)}, u32[]{:S(2)}, u32[]{:S(2)}) collective-permute-start(bf16[11,128,128]{2,1,0:T(8,128)(2,1)S(1)} %get-tuple-element.55), channel_id=1, source_target_pairs={{0,3},{1,0},{2,1},{3,2},{4,7},{5,4},{6,5},{7,6},{8,11},{9,8},{10,9... | collective-permute-start | bytes 1081352 | tf_op jit(solution)/shard_map/ppermute | solution.py:28
  76.4 0.4 collective-permute-done.16
  76.9 1.1 %collective-permute-done.15 = bf16[19,16,128]{2,1,0:T(8,128)(2,1)S(1)} collective-permute-done((bf16[19,16,128]{2,1,0:T(8,128)(2,1)S(1)}, bf16[19,16,128]{2,1,0:T(8,128)(2,1)S(1)}, u32[]{:S(2)}, u32[]{:S(2)}) %collective-permute-start.15) | collective-permute-done | bytes 77856 | tf_op jit(solution)/shard_map/ppermute | solution.py:23
  77.9 0.5 collective-permute-done.14
  78.5 0.0 collective-permute-done.17.refs_1_
  78.5 0.1 collective-permute-start.19
  78.6 4.9 %collective-permute-done.18.refs_2_ = bf16[11,128,128]{2,1,0:T(8,128)(2,1)S(1)} collective-permute-done((bf16[11,128,128]{2,1,0:T(8,128)(2,1)S(1)}, bf16[11,128,128]{2,1,0:T(8,128)(2,1)S(1)}, u32[]{:S(2)}, u32[]{:S(2)}) %collective-permute-start.18) | collective-permute-done | bytes 360480 | tf_op jit(solution)/shard_map/ppermute | solution.py:28
  83.5 0.0 copy-done.6
  83.5 0.0 copy-done.7
  83.5 1.6 %columns.1 = (bf16[3,128,128]{2,1,0:T(8,128)(2,1)}, bf16[8,128,128]{2,1,0:T(8,128)(2,1)}) custom-call(s32[8]{0:T(128)S(1)} %copy-done.5, s32[3]{0:T(128)S(1)} %bitcast.39, s32[8]{0:T(128)S(1)} %bitcast.41, bf16[8,128,128]{2,1,0:T(8,128)(2,1)S(1)} %copy-done.1, f32[11,128,128]{2,1,0:T(8,128)S(1)} %get-tuple-element.39.own, ...), custom_call_target="tpu_custom_call" | custom-call | tf_op jit(solution)/shard_map/columns/pallas_call | solution.py:41
  85.1 0.0 collective-permute-done.19.far
  85.1 0.0 copy-done.3
  85.1 0.0 copy-done.4
  85.1 3.3 %blocks.1 = (f32[3,128,128]{2,1,0:T(8,128)}, f32[8,128,128]{2,1,0:T(8,128)}, f32[8,128,128]{2,1,0:T(8,128)}) custom-call(s32[8]{0:T(128)S(1)} %copy-done.5, bf16[4,19,16,128]{3,2,1,0:T(8,128)(2,1)S(1)} %pad_maximum_fusion.1.near, bf16[4,19,16,128]{3,2,1,0:T(8,128)(2,1)S(1)} %collective-permute-done.19.far, f32[3,128,128]{2,1,0:T(8,128)S(1)} %copy-done.4, ...), custom_call_target="tpu_custom_call" | custom-call | tf_op jit(solution)/shard_map/blocks/pallas_call | solution.py:41
  (5 shorter events, 0.1 us)
Async XLA Ops:
  2.4 13.4 %collective-permute-start.2 = (bf16[11,128,128]{2,1,0:T(8,128)(2,1)}, bf16[11,128,128]{2,1,0:T(8,128)(2,1)S(1)}, u32[]{:S(2)}, u32[]{:S(2)}) collective-permute-start(bf16[11,128,128]{2,1,0:T(8,128)(2,1)} %mask.1.refs_0_), channel_id=1, source_target_pairs={{0,24},{4,28},{8,16},{12,20},{16,8},{20,12},{24,0},{28,4},{1,25},{... | collective-permute-start | bytes 1081352 | tf_op jit(solution)/shard_map/ppermute | solution.py:23
  6.3 16.3 %collective-permute-start.1 = (bf16[11,128,128]{2,1,0:T(8,128)(2,1)}, bf16[11,128,128]{2,1,0:T(8,128)(2,1)S(1)}, u32[]{:S(2)}, u32[]{:S(2)}) collective-permute-start(bf16[11,128,128]{2,1,0:T(8,128)(2,1)} %mask.1.refs_0_), channel_id=1, source_target_pairs={{0,16},{4,20},{8,24},{12,28},{16,0},{20,4},{24,8},{28,12},{1,17},{... | collective-permute-start | bytes 1081352 | tf_op jit(solution)/shard_map/ppermute | solution.py:23
  6.8 16.1 %collective-permute-start = (bf16[11,128,128]{2,1,0:T(8,128)(2,1)}, bf16[11,128,128]{2,1,0:T(8,128)(2,1)S(1)}, u32[]{:S(2)}, u32[]{:S(2)}) collective-permute-start(bf16[11,128,128]{2,1,0:T(8,128)(2,1)} %mask.1.refs_0_), channel_id=1, source_target_pairs={{0,8},{4,12},{8,0},{12,4},{16,24},{20,28},{24,16},{28,20},{1,9},{5... | collective-permute-start | bytes 1081352 | tf_op jit(solution)/shard_map/ppermute | solution.py:23
  6.9 17.4 %collective-permute-start.4 = (bf16[11,128,128]{2,1,0:T(8,128)(2,1)}, bf16[11,128,128]{2,1,0:T(8,128)(2,1)S(1)}, u32[]{:S(2)}, u32[]{:S(2)}) collective-permute-start(bf16[11,128,128]{2,1,0:T(8,128)(2,1)} %mask.1.refs_0_), channel_id=1, source_target_pairs={{2,0},{1,3},{6,4},{5,7},{10,8},{9,11},{14,12},{13,15},{18,16},{17,... | collective-permute-start | bytes 1081352 | tf_op jit(solution)/shard_map/ppermute | solution.py:226
  8.2 19.0 %collective-permute-start.3 = (bf16[11,128,128]{2,1,0:T(8,128)(2,1)}, bf16[11,128,128]{2,1,0:T(8,128)(2,1)S(1)}, u32[]{:S(2)}, u32[]{:S(2)}) collective-permute-start(bf16[11,128,128]{2,1,0:T(8,128)(2,1)} %mask.1.refs_0_), channel_id=1, source_target_pairs={{1,0},{2,1},{3,2},{0,3},{5,4},{6,5},{7,6},{4,7},{9,8},{10,9},{11,1... | collective-permute-start | bytes 1081352 | tf_op jit(solution)/shard_map/ppermute | solution.py:226
  23.0 4.3 %copy-start.1 = (bf16[8,128,128]{2,1,0:T(8,128)(2,1)S(1)}, bf16[8,128,128]{2,1,0:T(8,128)(2,1)}, u32[]{:S(2)}) copy-start(bf16[8,128,128]{2,1,0:T(8,128)(2,1)} %panel.5) | copy-start | bytes 786436
  23.0 4.3 %copy-start.2 = (bf16[1,4,8,1,128,128]{5,4,3,2,1,0:T(8,128)(2,1)S(1)}, bf16[1,4,8,1,128,128]{5,4,3,2,1,0:T(8,128)(2,1)}, u32[]{:S(2)}) copy-start(bf16[1,4,8,1,128,128]{5,4,3,2,1,0:T(8,128)(2,1)} %param.9) | copy-start | bytes 3145732
  27.2 3.2 %collective-permute-start.5 = (bf16[4,11,128,128]{3,2,1,0:T(8,128)(2,1)S(1)}, bf16[4,11,128,128]{3,2,1,0:T(8,128)(2,1)S(1)}, u32[]{:S(2)}, u32[]{:S(2)}) collective-permute-start(bf16[4,11,128,128]{3,2,1,0:T(8,128)(2,1)S(1)} %pad_maximum_fusion.near), channel_id=1, source_target_pairs={{0,4},{4,0},{8,12},{12,8},{16,20},{20,16},{24,28},{28,24},{1,5},{5... | collective-permute-start | bytes 4325384 | tf_op jit(solution)/shard_map/ppermute | solution.py:23
  27.6 1.0 %copy-start = (bf16[11,128,128]{2,1,0:T(8,128)(2,1)S(1)}, bf16[11,128,128]{2,1,0:T(8,128)(2,1)}, u32[]{:S(2)}) copy-start(bf16[11,128,128]{2,1,0:T(8,128)(2,1)} %mask.1.refs_0_) | copy-start | bytes 1081348
  28.6 1.8 %copy-start.5 = (s32[8]{0:T(128)S(1)}, s32[8]{0:T(128)}, u32[]{:S(2)}) copy-start(s32[8]{0:T(128)} %parents.5) | copy-start | bytes 100
  33.0 2.1 %collective-permute-start.6 = (f32[4,19,16,128]{3,2,1,0:T(8,128)S(1)}, f32[4,19,16,128]{3,2,1,0:T(8,128)S(1)}, u32[]{:S(2)}, u32[]{:S(2)}) collective-permute-start(f32[4,19,16,128]{3,2,1,0:T(8,128)S(1)} %get-tuple-element.41), channel_id=1, source_target_pairs={{0,4},{4,0},{8,12},{12,8},{16,20},{20,16},{24,28},{28,24},{1,5},{5... | collective-permute-start | bytes 1867784 | tf_op jit(solution)/shard_map/ppermute | solution.py:23
  35.3 48.2 %copy-start.6 = (s32[3,1,1]{0,2,1:T(1,128)S(1)}, s32[3,1,1]{0,2,1:T(1,128)}, u32[]{:S(2)}) copy-start(s32[3,1,1]{0,2,1:T(1,128)} %param.11) | copy-start | bytes 40
  35.3 48.2 %copy-start.7 = (s32[8,1,1]{0,2,1:T(1,128)S(1)}, s32[8,1,1]{0,2,1:T(1,128)}, u32[]{:S(2)}) copy-start(s32[8,1,1]{0,2,1:T(1,128)} %param.14) | copy-start | bytes 100
  35.3 7.9 %collective-permute-start.7 = (bf16[19,16,128]{2,1,0:T(8,128)(2,1)S(1)}, bf16[19,16,128]{2,1,0:T(8,128)(2,1)S(1)}, u32[]{:S(2)}, u32[]{:S(2)}) collective-permute-start(bf16[19,16,128]{2,1,0:T(8,128)(2,1)S(1)} %get-tuple-element.70), channel_id=1, source_target_pairs={{0,8},{4,12},{8,0},{12,4},{16,24},{20,28},{24,16},{28,20},{1,9},{5... | collective-permute-start | bytes 233480 | tf_op jit(solution)/shard_map/ppermute | solution.py:23
  37.1 6.2 %collective-permute-start.9 = (bf16[19,16,128]{2,1,0:T(8,128)(2,1)S(1)}, bf16[19,16,128]{2,1,0:T(8,128)(2,1)S(1)}, u32[]{:S(2)}, u32[]{:S(2)}) collective-permute-start(bf16[19,16,128]{2,1,0:T(8,128)(2,1)S(1)} %get-tuple-element.71), channel_id=1, source_target_pairs={{0,24},{4,28},{8,16},{12,20},{16,8},{20,12},{24,0},{28,4},{1,25},{... | collective-permute-start | bytes 233480 | tf_op jit(solution)/shard_map/ppermute | solution.py:23
  38.6 5.3 %collective-permute-start.8 = (bf16[19,16,128]{2,1,0:T(8,128)(2,1)S(1)}, bf16[19,16,128]{2,1,0:T(8,128)(2,1)S(1)}, u32[]{:S(2)}, u32[]{:S(2)}) collective-permute-start(bf16[19,16,128]{2,1,0:T(8,128)(2,1)S(1)} %get-tuple-element.72), channel_id=1, source_target_pairs={{0,16},{4,20},{8,24},{12,28},{16,0},{20,4},{24,8},{28,12},{1,17},{... | collective-permute-start | bytes 233480 | tf_op jit(solution)/shard_map/ppermute | solution.py:23
  38.9 31.9 %collective-permute-start.13 = (bf16[11,128,128]{2,1,0:T(8,128)(2,1)S(1)}, bf16[11,128,128]{2,1,0:T(8,128)(2,1)S(1)}, u32[]{:S(2)}, u32[]{:S(2)}) collective-permute-start(bf16[11,128,128]{2,1,0:T(8,128)(2,1)S(1)} %get-tuple-element.46), channel_id=1, source_target_pairs={{0,2},{1,3},{2,0},{3,1},{4,6},{5,7},{6,4},{7,5},{8,10},{9,11},{10,... | collective-permute-start | bytes 1081352 | tf_op jit(solution)/shard_map/ppermute | solution.py:28
  38.9 39.6 %collective-permute-start.17 = (bf16[11,128,128]{2,1,0:T(8,128)(2,1)S(1)}, bf16[11,128,128]{2,1,0:T(8,128)(2,1)S(1)}, u32[]{:S(2)}, u32[]{:S(2)}) collective-permute-start(bf16[11,128,128]{2,1,0:T(8,128)(2,1)S(1)} %get-tuple-element.52), channel_id=1, source_target_pairs={{0,1},{1,2},{2,3},{3,0},{4,5},{5,6},{6,7},{7,4},{8,9},{9,10},{10,1... | collective-permute-start | bytes 1081352 | tf_op jit(solution)/shard_map/ppermute | solution.py:28
  44.0 17.5 %collective-permute-start.12 = (bf16[19,16,128]{2,1,0:T(8,128)(2,1)S(1)}, bf16[19,16,128]{2,1,0:T(8,128)(2,1)S(1)}, u32[]{:S(2)}, u32[]{:S(2)}) collective-permute-start(bf16[19,16,128]{2,1,0:T(8,128)(2,1)S(1)} %fusion.3.refs_0_), channel_id=1, source_target_pairs={{0,1},{1,2},{2,3},{3,0},{4,5},{5,6},{6,7},{7,4},{8,9},{9,10},{10,1... | collective-permute-start | bytes 233480 | tf_op jit(solution)/shard_map/ppermute | solution.py:28
  44.9 25.8 %collective-permute-start.11 = (bf16[19,16,128]{2,1,0:T(8,128)(2,1)S(1)}, bf16[19,16,128]{2,1,0:T(8,128)(2,1)S(1)}, u32[]{:S(2)}, u32[]{:S(2)}) collective-permute-start(bf16[19,16,128]{2,1,0:T(8,128)(2,1)S(1)} %fusion.3.refs_0_), channel_id=1, source_target_pairs={{0,2},{1,3},{2,0},{3,1},{4,6},{5,7},{6,4},{7,5},{8,10},{9,11},{10,... | collective-permute-start | bytes 233480 | tf_op jit(solution)/shard_map/ppermute | solution.py:28
  48.2 22.6 %collective-permute-start.10 = (bf16[19,16,128]{2,1,0:T(8,128)(2,1)S(1)}, bf16[19,16,128]{2,1,0:T(8,128)(2,1)S(1)}, u32[]{:S(2)}, u32[]{:S(2)}) collective-permute-start(bf16[19,16,128]{2,1,0:T(8,128)(2,1)S(1)} %fusion.3.refs_0_), channel_id=1, source_target_pairs={{0,3},{1,0},{2,1},{3,2},{4,7},{5,4},{6,5},{7,6},{8,11},{9,8},{10,9... | collective-permute-start | bytes 233480 | tf_op jit(solution)/shard_map/ppermute | solution.py:28
  70.8 14.2 %copy-start.3 = (f32[8,128,128]{2,1,0:T(8,128)S(1)}, f32[8,128,128]{2,1,0:T(8,128)}, u32[]{:S(2)}) copy-start(f32[8,128,128]{2,1,0:T(8,128)} %lower_diagonal.1) | copy-start | bytes 1572868
  70.8 14.2 %copy-start.4 = (f32[3,128,128]{2,1,0:T(8,128)S(1)}, f32[3,128,128]{2,1,0:T(8,128)}, u32[]{:S(2)}) copy-start(f32[3,128,128]{2,1,0:T(8,128)} %upper_diagonal.1) | copy-start | bytes 589828
  70.9 6.0 %collective-permute-start.16 = (bf16[19,16,128]{2,1,0:T(8,128)(2,1)S(1)}, bf16[19,16,128]{2,1,0:T(8,128)(2,1)S(1)}, u32[]{:S(2)}, u32[]{:S(2)}) collective-permute-start(bf16[19,16,128]{2,1,0:T(8,128)(2,1)S(1)} %line.1), channel_id=1, source_target_pairs={{0,24},{4,28},{8,16},{12,20},{16,8},{20,12},{24,0},{28,4},{1,25},{... | collective-permute-start | bytes 233480 | tf_op jit(solution)/shard_map/ppermute | solution.py:23
  73.5 4.4 %collective-permute-start.15 = (bf16[19,16,128]{2,1,0:T(8,128)(2,1)S(1)}, bf16[19,16,128]{2,1,0:T(8,128)(2,1)S(1)}, u32[]{:S(2)}, u32[]{:S(2)}) collective-permute-start(bf16[19,16,128]{2,1,0:T(8,128)(2,1)S(1)} %line.1), channel_id=1, source_target_pairs={{0,16},{4,20},{8,24},{12,28},{16,0},{20,4},{24,8},{28,12},{1,17},{... | collective-permute-start | bytes 233480 | tf_op jit(solution)/shard_map/ppermute | solution.py:23
  74.0 4.4 %collective-permute-start.14 = (bf16[19,16,128]{2,1,0:T(8,128)(2,1)S(1)}, bf16[19,16,128]{2,1,0:T(8,128)(2,1)S(1)}, u32[]{:S(2)}, u32[]{:S(2)}) collective-permute-start(bf16[19,16,128]{2,1,0:T(8,128)(2,1)S(1)} %line.1), channel_id=1, source_target_pairs={{0,8},{4,12},{8,0},{12,4},{16,24},{20,28},{24,16},{28,20},{1,9},{5... | collective-permute-start | bytes 233480 | tf_op jit(solution)/shard_map/ppermute | solution.py:23
  74.4 9.1 %collective-permute-start.18 = (bf16[11,128,128]{2,1,0:T(8,128)(2,1)S(1)}, bf16[11,128,128]{2,1,0:T(8,128)(2,1)S(1)}, u32[]{:S(2)}, u32[]{:S(2)}) collective-permute-start(bf16[11,128,128]{2,1,0:T(8,128)(2,1)S(1)} %get-tuple-element.55), channel_id=1, source_target_pairs={{0,3},{1,0},{2,1},{3,2},{4,7},{5,4},{6,5},{7,6},{8,11},{9,8},{10,9... | collective-permute-start | bytes 1081352 | tf_op jit(solution)/shard_map/ppermute | solution.py:28
  78.5 6.6 %collective-permute-start.19 = (bf16[4,19,16,128]{3,2,1,0:T(8,128)(2,1)S(1)}, bf16[4,19,16,128]{3,2,1,0:T(8,128)(2,1)S(1)}, u32[]{:S(2)}, u32[]{:S(2)}) collective-permute-start(bf16[4,19,16,128]{3,2,1,0:T(8,128)(2,1)S(1)} %pad_maximum_fusion.1.near), channel_id=1, source_target_pairs={{0,4},{4,0},{8,12},{12,8},{16,20},{20,16},{24,28},{28,24},{1,5},{5... | collective-permute-start | bytes 933896 | tf_op jit(solution)/shard_map/ppermute | solution.py:23

commit v5 on v4

--- a/solution.py
+++ b/solution.py
@@ -37,7 +37,7 @@
     return pltpu.CompilerParams(vmem_limit_bytes=limit or ceil_to(size * 5 // 4, 1 << 20) + (4 << 20))
 
 
-def call(kernel, name, scalars, arrays, outs, scratch=(), limit=0):
+def call(kernel, name, scalars, arrays, outs, scratch=(), limit=0, cost=0):
     return pl.pallas_call(
         kernel,
         out_shape=outs,
@@ -45,16 +45,49 @@
         out_specs=[VMEM] * len(outs),
         scratch_shapes=[pltpu.VMEM(r.shape, r.dtype) for r in scratch],
         compiler_params=params([*arrays, *outs, *scratch], limit),
+        cost_estimate=pl.CostEstimate(flops=cost, bytes_accessed=cost, transcendentals=0) if cost else None,
         name=name,
     )(*scalars, *arrays)
 
 
-def mask_kernel(upper_pattern, lower_pattern, upper_panel, lower_panel, masked):
+def stack_kernel(*refs):
+    for i, piece in enumerate(refs[:-2]):
+        refs[-1][i] = piece[...]
+
+
+def mask_kernel(*refs):
+    sources, masked, stages, sems = refs[:4], refs[4], refs[5:9], refs[9]
+    copies = [
+        pltpu.make_async_copy(source, stage, sems.at[i])
+        for i, (source, stage) in enumerate(zip(sources, stages))
+    ]
+    for copy in copies:
+        copy.start()
+    for copy in copies:
+        copy.wait()
+    upper_pattern, lower_pattern, upper_panel, lower_panel = stages
     uppers, lowers = upper_panel.shape[0], lower_panel.shape[0]
     for k in range(uppers):
         masked[k] = upper_panel[k] * upper_pattern[k].astype(F32).astype(jnp.bfloat16)
     for m in range(lowers):
         masked[uppers + m] = lower_panel[m] * lower_pattern[m].astype(F32).astype(jnp.bfloat16)
+
+
+def mask(*arrays):
+    total, block = arrays[2].shape[0] + arrays[3].shape[0], arrays[2].shape[-1]
+    return pl.pallas_call(
+        mask_kernel,
+        out_shape=shape_of((total, block, block), jnp.bfloat16),
+        in_specs=[pl.BlockSpec(memory_space=pltpu.HBM)] * 4,
+        out_specs=VMEM,
+        scratch_shapes=[
+            *[pltpu.SMEM(a.shape, a.dtype) for a in arrays[:2]],
+            *[pltpu.VMEM(a.shape, a.dtype) for a in arrays[2:]],
+            pltpu.SemaphoreType.DMA((4,)),
+        ],
+        compiler_params=params(arrays, 0),
+        name="mask",
+    )(*arrays)
 
 
 def turn_kernel(*refs):
@@ -229,7 +262,7 @@
 
 def gather_near(value, axis):
     masks = range(2, lax.axis_size(axis), 2)
-    return jnp.stack([value] + [flip(value, axis, m) for m in masks])
+    return [value] + [flip(value, axis, m) for m in masks]
 
 
 def scatter_flips(value, axis):
@@ -261,15 +294,28 @@
     bf16 = jnp.bfloat16
     upper_pattern, lower_pattern = upper_pattern.reshape(-1), lower_pattern.reshape(-1)
 
-    (masked,) = call(
-        mask_kernel,
-        "mask",
-        (upper_pattern, lower_pattern),
-        (upper_panel.reshape(-1, block, block), lower_panel.reshape(-1, block, block)),
-        [shape_of((total, block, block), bf16)],
-        limit=60 << 20,
-    )
-    near, *pieces = tie(gather_near(masked, "row"), *gather_pairs(masked, "col"))
+    masked = mask(
+        upper_pattern,
+        lower_pattern,
+        upper_panel.reshape(-1, block, block),
+        lower_panel.reshape(-1, block, block),
+    )
+    reach = (depth // 2 + 1) * block
+    (turned,) = call(
+        turn_kernel,
+        "turn",
+        (),
+        gather_pairs(masked, "col"),
+        [shape_of((total, block, reach), bf16)],
+        cost=0,
+    )
+    (near,) = call(
+        stack_kernel,
+        "stack",
+        (),
+        (*gather_near(masked, "row"), turned),
+        [shape_of((half, total, block, block), bf16)],
+    )
     far = flip(near, "row", 1)
     top, panel_turned = call(
         top_kernel,
@@ -278,8 +324,6 @@
         (top_inverse[0, :, :, 0], parent_panel),
         [shape_of((2, depth * block, half * block), bf16), shape_of(parent_panel.shape, bf16)],
     )
-    reach = len(pieces) * block
-    (turned,) = call(turn_kernel, "turn", (), pieces, [shape_of((total, block, reach), bf16)])
     pairs = ceil_to(total, 2) // 2
     (start,) = call(
         first_kernel, "first", (), (top, near), [shape_of((pairs, depth * block, 2 * block), F32)]
@@ -298,13 +342,13 @@
 
     other, *returns = tie(flip(sums_away, "row", 1), *returns)
     sums = sums_keep + other
-    middle = depth // 2
     part = sums[0]
     for piece in scatter_flips(sums, "row"):
         part = part + piece.astype(F32)
     parts = gather_shifts(part.astype(WIRE), "col")
-    got = [shift(returns[o - 1], "col", o) for o in range(1, depth) if o == middle]
-    tied = tie(*parts, *got)
+    early = [o for o in range(1, depth) if min(o, depth - o) <= depth // 4]
+    late = [o for o in range(1, depth) if o not in early]
+    tied = tie(*parts, *[shift(returns[o - 1], "col", o) for o in early])
     parts, got = tied[:depth], tied[depth:]
     (part,) = call(
         line_kernel,
@@ -314,10 +358,9 @@
         [shape_of((sums_n, chunk, block), WIRE)],
         [shape_of((depth, sums_n, chunk, block), F32)],
     )
-    near = gather_near(part, "row")
-    near, *more = tie(near, *[shift(returns[o - 1], "col", o) for o in range(1, middle)])
     part, *returns = tie(part, *returns)
-    got = [*got, *more, *[shift(returns[o - 1], "col", o) for o in range(middle + 1, depth)]]
+    got = [*got, *[shift(returns[o - 1], "col", o) for o in late]]
+    near = jnp.stack(gather_near(part, "row"))
     far = flip(near, "row", 1)
 
     upper_columns, lower_columns = call(

time: 88.6 us -> 92.4 us (1.043)
  local copies, waits for them, and re-layouts: 0.06 us -> 3.21 us
  waiting for transfers between devices: 47.2 us -> 50.1 us
  other arithmetic: 1.45 us -> 0.17 us
  Pallas kernels: 11.1 us -> 10 us
    ppermute x2, waiting for transfers between devices: 2.95 us -> 11.6 us  [gather_pairs(): lax.ppermute(value, axis, [((c + o) % size, c) for c in takers])]
    ppermute x12, waiting for transfers between devices: 16.7 us -> 10.4 us  [flip(): return lax.ppermute(value, axis, [(i, i ^ mask) for i in range(size)])]
    unnamed x16 -> x22, local copies, waits for them, and re-layouts: 0.05 us -> 3.19 us
    pallas_call x8, Pallas kernels: 11.1 us -> 9.41 us  [call(): pl.pallas_call(kernel, out_shape=outs, in_specs=[SMEM] * len(scalars) + [...]
    another operation x3 -> x2, other arithmetic: 1.41 us -> 0.13 us  [the longest x2 1.31 us: gather_near(): return jnp.stack([value] + [flip(value, axis, m) for m in masks])]
    ppermute x2, starting transfers between devices: 5.41 us -> 6.39 us  [gather_pairs(): lax.ppermute(value, axis, [((c + o) % size, c) for c in takers])]
  transfers between devices with their start and end apart: 20 -> 20, of which waited for: 13 -> 13; matrix products, arithmetic and copies ran while one was open for 2% -> 0% of each run, Pallas kernels for 4% -> 4%
where the time goes in v5:
time: 92.4 us; the launch traced here: 92.2 us
  waiting for transfers between devices  50.1 us (54%)
  starting transfers between devices  27.9 us (30%)
  Pallas kernels  10 us (11%)
  local copies, waits for them, and re-layouts  3.21 us (3%)
    ppermute x6, waiting for transfers between devices, shift(): lax.ppermute(value, axis, [(i, (i + step) % size) for i in range(size)])  28.1 us
    ppermute x2, waiting for transfers between devices, gather_pairs(): lax.ppermute(value, axis, [((c + o) % size, c) for c in takers])  11.6 us
    ppermute x12, starting transfers between devices, flip(): return lax.ppermute(value, axis, [(i, i ^ mask) for i in range(size)])  10.9 us
    ppermute x6, starting transfers between devices, shift(): lax.ppermute(value, axis, [(i, (i + step) % size) for i in range(size)])  10.5 us
    ppermute x12, waiting for transfers between devices, flip(): return lax.ppermute(value, axis, [(i, i ^ mask) for i in range(size)])  10.4 us
    pallas_call x8, Pallas kernels, call(): pl.pallas_call(kernel, out_shape=outs, in_specs=[SMEM] * len(scalars) + [...  9.41 us
    ppermute x2, starting transfers between devices, gather_pairs(): lax.ppermute(value, axis, [((c + o) % size, c) for c in takers])  6.39 us
    unnamed x22, local copies, waits for them, and re-layouts  3.19 us
  transfers between devices with their start and end apart: 20, of which 13 were waited for; matrix products, arithmetic and copies ran while one was open for 0% of the time, Pallas kernels for 4%

profile of v5, /device:TPU:0, one launch (start us, length us, event | category | flops | bytes accessed | tf_op | source)
XLA Modules:
  0.0 92.2 jit_solution(2928797456237650411)
XLA Ops:
  0.6 0.0 copy-start.3
  0.6 0.9 %copy-done.3 = bf16[8,1,1,128,128]{4,3,2,1,0:T(8,128)(2,1)S(1)} copy-done((bf16[8,1,1,128,128]{4,3,2,1,0:T(8,128)(2,1)S(1)}, bf16[8,1,1,128,128]{4,3,2,1,0:T(8,128)(2,1)}, u32[]{:S(2)}) %copy-start.3) | copy-done | bytes 262168
  1.6 0.9 copy-done.5
  2.5 0.7 copy-done.7
  3.1 0.7 copy-done.9
  3.8 0.6 mask.1.refs_0_
  4.4 1.3 %collective-permute-start.4 = (bf16[11,128,128]{2,1,0:T(8,128)(2,1)S(1)}, bf16[11,128,128]{2,1,0:T(8,128)(2,1)S(1)}, u32[]{:S(2)}, u32[]{:S(2)}) collective-permute-start(bf16[11,128,128]{2,1,0:T(8,128)(2,1)S(1)} %mask.1.refs_0_), channel_id=1, source_target_pairs={{2,0},{1,3},{6,4},{5,7},{10,8},{9,11},{14,12},{13,15},{18,16},{17,... | collective-permute-start | bytes 1081352 | tf_op jit(solution)/shard_map/ppermute | solution.py:259
  5.7 5.1 %collective-permute-start.3 = (bf16[11,128,128]{2,1,0:T(8,128)(2,1)S(1)}, bf16[11,128,128]{2,1,0:T(8,128)(2,1)S(1)}, u32[]{:S(2)}, u32[]{:S(2)}) collective-permute-start(bf16[11,128,128]{2,1,0:T(8,128)(2,1)S(1)} %mask.1.refs_0_), channel_id=1, source_target_pairs={{1,0},{2,1},{3,2},{0,3},{5,4},{6,5},{7,6},{4,7},{9,8},{10,9},{11,1... | collective-permute-start | bytes 1081352 | tf_op jit(solution)/shard_map/ppermute | solution.py:259
  10.8 2.4 %collective-permute-start.2 = (bf16[11,128,128]{2,1,0:T(8,128)(2,1)S(1)}, bf16[11,128,128]{2,1,0:T(8,128)(2,1)S(1)}, u32[]{:S(2)}, u32[]{:S(2)}) collective-permute-start(bf16[11,128,128]{2,1,0:T(8,128)(2,1)S(1)} %mask.1.refs_0_), channel_id=1, source_target_pairs={{0,24},{4,28},{8,16},{12,20},{16,8},{20,12},{24,0},{28,4},{1,25},{... | collective-permute-start | bytes 1081352 | tf_op jit(solution)/shard_map/ppermute | solution.py:23
  13.3 0.5 collective-permute-start.1
  13.8 0.5 collective-permute-start
  14.3 4.7 %collective-permute-done.4.refs_2_ = bf16[11,128,128]{2,1,0:T(8,128)(2,1)S(1)} collective-permute-done((bf16[11,128,128]{2,1,0:T(8,128)(2,1)S(1)}, bf16[11,128,128]{2,1,0:T(8,128)(2,1)S(1)}, u32[]{:S(2)}, u32[]{:S(2)}) %collective-permute-start.4) | collective-permute-done | bytes 360480 | tf_op jit(solution)/shard_map/ppermute | solution.py:259
  19.0 6.9 %collective-permute-done.3.refs_1_ = bf16[11,128,128]{2,1,0:T(8,128)(2,1)S(1)} collective-permute-done((bf16[11,128,128]{2,1,0:T(8,128)(2,1)S(1)}, bf16[11,128,128]{2,1,0:T(8,128)(2,1)S(1)}, u32[]{:S(2)}, u32[]{:S(2)}) %collective-permute-start.3) | collective-permute-done | bytes 360480 | tf_op jit(solution)/shard_map/ppermute | solution.py:259
  25.9 0.3 turn.1.refs_4_.turned
  26.2 0.0 copy-start
  26.2 0.0 copy-start.1
  26.2 0.0 collective-permute-done.2.refs_3_
  26.3 3.1 %collective-permute-done.1.refs_2_ = bf16[11,128,128]{2,1,0:T(8,128)(2,1)S(1)} collective-permute-done((bf16[11,128,128]{2,1,0:T(8,128)(2,1)S(1)}, bf16[11,128,128]{2,1,0:T(8,128)(2,1)S(1)}, u32[]{:S(2)}, u32[]{:S(2)}) %collective-permute-start.1) | collective-permute-done | bytes 360480 | tf_op jit(solution)/shard_map/ppermute | solution.py:23
  29.3 0.1 collective-permute-done.refs_1_
  29.4 0.1 stack.21.near
  29.5 0.1 collective-permute-start.5
  29.6 0.0 copy-done
  29.6 0.0 copy-done.1
  29.6 0.4 top.1
  30.0 0.0 copy-start.6
  30.0 1.0 %first.1.start = f32[6,512,256]{2,1,0:T(8,128)S(1)} custom-call(bf16[2,512,512]{2,1,0:T(8,128)(2,1)S(1)} %get-tuple-element.30.top, bf16[4,11,128,128]{3,2,1,0:T(8,128)(2,1)S(1)} %stack.21.near), custom_call_target="tpu_custom_call" | custom-call | tf_op jit(solution)/shard_map/first/pallas_call | solution.py:41
  31.0 1.8 %collective-permute-done.5.far = bf16[4,11,128,128]{3,2,1,0:T(8,128)(2,1)S(1)} collective-permute-done((bf16[4,11,128,128]{3,2,1,0:T(8,128)(2,1)S(1)}, bf16[4,11,128,128]{3,2,1,0:T(8,128)(2,1)S(1)}, u32[]{:S(2)}, u32[]{:S(2)}) %collective-permute-start.5) | collective-permute-done | bytes 1441824 | tf_op jit(solution)/shard_map/ppermute | solution.py:23
  32.8 2.6 %second.1 = (f32[11,128,128]{2,1,0:T(8,128)S(1)}, bf16[11,128,128]{2,1,0:T(8,128)(2,1)S(1)}, bf16[11,128,128]{2,1,0:T(8,128)(2,1)S(1)}, bf16[11,128,128]{2,1,0:T...) custom-call(s32[8]{0:T(128)S(1)} %copy-done.6, ...), custom_call_target="tpu_custom_call" | custom-call | tf_op jit(solution)/shard_map/second/pallas_call | solution.py:41
  35.5 0.2 collective-permute-start.6
  35.7 1.9 %collective-permute-done.6 = f32[4,19,16,128]{3,2,1,0:T(8,128)S(1)} collective-permute-done((f32[4,19,16,128]{3,2,1,0:T(8,128)S(1)}, f32[4,19,16,128]{3,2,1,0:T(8,128)S(1)}, u32[]{:S(2)}, u32[]{:S(2)}) %collective-permute-start.6) | collective-permute-done | bytes 622624 | tf_op jit(solution)/shard_map/ppermute | solution.py:23
  37.6 0.1 fusion.4
  37.7 0.0 copy-start.8
  37.7 0.0 copy-start.10
  37.7 1.6 %collective-permute-start.7 = (bf16[19,16,128]{2,1,0:T(8,128)(2,1)S(1)}, bf16[19,16,128]{2,1,0:T(8,128)(2,1)S(1)}, u32[]{:S(2)}, u32[]{:S(2)}) collective-permute-start(bf16[19,16,128]{2,1,0:T(8,128)(2,1)S(1)} %get-tuple-element.62), channel_id=1, source_target_pairs={{0,8},{4,12},{8,0},{12,4},{16,24},{20,28},{24,16},{28,20},{1,9},{5... | collective-permute-start | bytes 233480 | tf_op jit(solution)/shard_map/ppermute | solution.py:23
  39.3 1.4 %collective-permute-start.9 = (bf16[19,16,128]{2,1,0:T(8,128)(2,1)S(1)}, bf16[19,16,128]{2,1,0:T(8,128)(2,1)S(1)}, u32[]{:S(2)}, u32[]{:S(2)}) collective-permute-start(bf16[19,16,128]{2,1,0:T(8,128)(2,1)S(1)} %get-tuple-element.63), channel_id=1, source_target_pairs={{0,24},{4,28},{8,16},{12,20},{16,8},{20,12},{24,0},{28,4},{1,25},{... | collective-permute-start | bytes 233480 | tf_op jit(solution)/shard_map/ppermute | solution.py:23
  40.7 0.6 collective-permute-start.8
  41.3 1.3 %collective-permute-start.13 = (bf16[11,128,128]{2,1,0:T(8,128)(2,1)S(1)}, bf16[11,128,128]{2,1,0:T(8,128)(2,1)S(1)}, u32[]{:S(2)}, u32[]{:S(2)}) collective-permute-start(bf16[11,128,128]{2,1,0:T(8,128)(2,1)S(1)} %get-tuple-element.38), channel_id=1, source_target_pairs={{0,1},{1,2},{2,3},{3,0},{4,5},{5,6},{6,7},{7,4},{8,9},{9,10},{10,1... | collective-permute-start | bytes 1081352 | tf_op jit(solution)/shard_map/ppermute | solution.py:28
  42.6 2.5 %collective-permute-start.14 = (bf16[11,128,128]{2,1,0:T(8,128)(2,1)S(1)}, bf16[11,128,128]{2,1,0:T(8,128)(2,1)S(1)}, u32[]{:S(2)}, u32[]{:S(2)}) collective-permute-start(bf16[11,128,128]{2,1,0:T(8,128)(2,1)S(1)} %get-tuple-element.39), channel_id=1, source_target_pairs={{0,3},{1,0},{2,1},{3,2},{4,7},{5,4},{6,5},{7,6},{8,11},{9,8},{10,9... | collective-permute-start | bytes 1081352 | tf_op jit(solution)/shard_map/ppermute | solution.py:28
  45.1 0.0 collective-permute-done.7
  45.1 0.0 collective-permute-done.9
  45.1 0.9 %collective-permute-done.8 = bf16[19,16,128]{2,1,0:T(8,128)(2,1)S(1)} collective-permute-done((bf16[19,16,128]{2,1,0:T(8,128)(2,1)S(1)}, bf16[19,16,128]{2,1,0:T(8,128)(2,1)S(1)}, u32[]{:S(2)}, u32[]{:S(2)}) %collective-permute-start.8) | collective-permute-done | bytes 77856 | tf_op jit(solution)/shard_map/ppermute | solution.py:23
  46.1 1.3 %collective-permute-start.12 = (bf16[19,16,128]{2,1,0:T(8,128)(2,1)S(1)}, bf16[19,16,128]{2,1,0:T(8,128)(2,1)S(1)}, u32[]{:S(2)}, u32[]{:S(2)}) collective-permute-start(bf16[19,16,128]{2,1,0:T(8,128)(2,1)S(1)} %fusion.3.refs_0_), channel_id=1, source_target_pairs={{0,1},{1,2},{2,3},{3,0},{4,5},{5,6},{6,7},{7,4},{8,9},{9,10},{10,1... | collective-permute-start | bytes 233480 | tf_op jit(solution)/shard_map/ppermute | solution.py:28
  47.4 1.2 %collective-permute-start.11 = (bf16[19,16,128]{2,1,0:T(8,128)(2,1)S(1)}, bf16[19,16,128]{2,1,0:T(8,128)(2,1)S(1)}, u32[]{:S(2)}, u32[]{:S(2)}) collective-permute-start(bf16[19,16,128]{2,1,0:T(8,128)(2,1)S(1)} %fusion.3.refs_0_), channel_id=1, source_target_pairs={{0,2},{1,3},{2,0},{3,1},{4,6},{5,7},{6,4},{7,5},{8,10},{9,11},{10,... | collective-permute-start | bytes 233480 | tf_op jit(solution)/shard_map/ppermute | solution.py:28
  48.6 2.8 %collective-permute-start.10 = (bf16[19,16,128]{2,1,0:T(8,128)(2,1)S(1)}, bf16[19,16,128]{2,1,0:T(8,128)(2,1)S(1)}, u32[]{:S(2)}, u32[]{:S(2)}) collective-permute-start(bf16[19,16,128]{2,1,0:T(8,128)(2,1)S(1)} %fusion.3.refs_0_), channel_id=1, source_target_pairs={{0,3},{1,0},{2,1},{3,2},{4,7},{5,4},{6,5},{7,6},{8,11},{9,8},{10,9... | collective-permute-start | bytes 233480 | tf_op jit(solution)/shard_map/ppermute | solution.py:28
  51.4 12.5 %collective-permute-done.12.refs_3_ = bf16[19,16,128]{2,1,0:T(8,128)(2,1)S(1)} collective-permute-done((bf16[19,16,128]{2,1,0:T(8,128)(2,1)S(1)}, bf16[19,16,128]{2,1,0:T(8,128)(2,1)S(1)}, u32[]{:S(2)}, u32[]{:S(2)}) %collective-permute-start.12) | collective-permute-done | bytes 77856 | tf_op jit(solution)/shard_map/ppermute | solution.py:28
  63.9 1.6 %collective-permute-done.11.refs_2_ = bf16[19,16,128]{2,1,0:T(8,128)(2,1)S(1)} collective-permute-done((bf16[19,16,128]{2,1,0:T(8,128)(2,1)S(1)}, bf16[19,16,128]{2,1,0:T(8,128)(2,1)S(1)}, u32[]{:S(2)}, u32[]{:S(2)}) %collective-permute-start.11) | collective-permute-done | bytes 77856 | tf_op jit(solution)/shard_map/ppermute | solution.py:28
  65.5 0.0 collective-permute-done.10.refs_1_
  65.5 0.0 collective-permute-done.13.refs_0_
  65.5 0.0 collective-permute-done.14.refs_1_
  65.5 0.1 line.1
  65.6 0.0 copy-start.2
  65.6 0.0 copy-start.4
  65.6 1.7 %collective-permute-start.18 = (bf16[19,16,128]{2,1,0:T(8,128)(2,1)S(1)}, bf16[19,16,128]{2,1,0:T(8,128)(2,1)S(1)}, u32[]{:S(2)}, u32[]{:S(2)}) collective-permute-start(bf16[19,16,128]{2,1,0:T(8,128)(2,1)S(1)} %line.1), channel_id=1, source_target_pairs={{0,24},{4,28},{8,16},{12,20},{16,8},{20,12},{24,0},{28,4},{1,25},{... | collective-permute-start | bytes 233480 | tf_op jit(solution)/shard_map/ppermute | solution.py:23
  67.4 1.3 %collective-permute-start.17 = (bf16[19,16,128]{2,1,0:T(8,128)(2,1)S(1)}, bf16[19,16,128]{2,1,0:T(8,128)(2,1)S(1)}, u32[]{:S(2)}, u32[]{:S(2)}) collective-permute-start(bf16[19,16,128]{2,1,0:T(8,128)(2,1)S(1)} %line.1), channel_id=1, source_target_pairs={{0,16},{4,20},{8,24},{12,28},{16,0},{20,4},{24,8},{28,12},{1,17},{... | collective-permute-start | bytes 233480 | tf_op jit(solution)/shard_map/ppermute | solution.py:23
  68.7 0.5 collective-permute-start.16
  69.2 1.3 %collective-permute-start.15 = (bf16[11,128,128]{2,1,0:T(8,128)(2,1)S(1)}, bf16[11,128,128]{2,1,0:T(8,128)(2,1)S(1)}, u32[]{:S(2)}, u32[]{:S(2)}) collective-permute-start(bf16[11,128,128]{2,1,0:T(8,128)(2,1)S(1)} %get-tuple-element.47), channel_id=1, source_target_pairs={{0,2},{1,3},{2,0},{3,1},{4,6},{5,7},{6,4},{7,5},{8,10},{9,11},{10,... | collective-permute-start | bytes 1081352 | tf_op jit(solution)/shard_map/ppermute | solution.py:28
  70.5 0.7 collective-permute-done.18
  71.3 1.2 %collective-permute-done.17 = bf16[19,16,128]{2,1,0:T(8,128)(2,1)S(1)} collective-permute-done((bf16[19,16,128]{2,1,0:T(8,128)(2,1)S(1)}, bf16[19,16,128]{2,1,0:T(8,128)(2,1)S(1)}, u32[]{:S(2)}, u32[]{:S(2)}) %collective-permute-start.17) | collective-permute-done | bytes 77856 | tf_op jit(solution)/shard_map/ppermute | solution.py:23
  72.5 0.6 collective-permute-done.16
  73.1 0.1 collective-permute-start.19
  73.2 14.0 %collective-permute-done.15.refs_2_ = bf16[11,128,128]{2,1,0:T(8,128)(2,1)S(1)} collective-permute-done((bf16[11,128,128]{2,1,0:T(8,128)(2,1)S(1)}, bf16[11,128,128]{2,1,0:T(8,128)(2,1)S(1)}, u32[]{:S(2)}, u32[]{:S(2)}) %collective-permute-start.15) | collective-permute-done | bytes 360480 | tf_op jit(solution)/shard_map/ppermute | solution.py:28
  87.2 1.6 %columns.1 = (bf16[3,128,128]{2,1,0:T(8,128)(2,1)}, bf16[8,128,128]{2,1,0:T(8,128)(2,1)}) custom-call(s32[8]{0:T(128)S(1)} %copy-done.6, s32[3]{0:T(128)S(1)} %bitcast.36, s32[8]{0:T(128)S(1)} %bitcast.38, bf16[8,128,128]{2,1,0:T(8,128)(2,1)S(1)} %copy-done, f32[11,128,128]{2,1,0:T(8,128)S(1)} %get-tuple-element.31.own, ...), custom_call_target="tpu_custom_call" | custom-call | tf_op jit(solution)/shard_map/columns/pallas_call | solution.py:41
  88.8 0.0 collective-permute-done.19.far
  88.8 3.3 %blocks.1 = (f32[3,128,128]{2,1,0:T(8,128)}, f32[8,128,128]{2,1,0:T(8,128)}, f32[8,128,128]{2,1,0:T(8,128)}) custom-call(s32[8]{0:T(128)S(1)} %copy-done.6, bf16[4,19,16,128]{3,2,1,0:T(8,128)(2,1)S(1)} %pad_maximum_fusion.near, bf16[4,19,16,128]{3,2,1,0:T(8,128)(2,1)S(1)} %collective-permute-done.19.far, f32[3,128,128]{2,1,0:T(8,128)S(1)} %copy-done.4, ...), custom_call_target="tpu_custom_call" | custom-call | tf_op jit(solution)/shard_map/blocks/pallas_call | solution.py:41
  (11 shorter events, 0.1 us)
Async XLA Ops:
  0.6 1.0 %copy-start.3 = (bf16[8,1,1,128,128]{4,3,2,1,0:T(8,128)(2,1)S(1)}, bf16[8,1,1,128,128]{4,3,2,1,0:T(8,128)(2,1)}, u32[]{:S(2)}) copy-start(bf16[8,1,1,128,128]{4,3,2,1,0:T(8,128)(2,1)} %param.13) | copy-start | bytes 786436
  1.6 0.9 copy-start.5
  2.5 0.7 copy-start.7
  3.1 0.7 copy-start.9
  4.4 14.6 %collective-permute-start.4 = (bf16[11,128,128]{2,1,0:T(8,128)(2,1)S(1)}, bf16[11,128,128]{2,1,0:T(8,128)(2,1)S(1)}, u32[]{:S(2)}, u32[]{:S(2)}) collective-permute-start(bf16[11,128,128]{2,1,0:T(8,128)(2,1)S(1)} %mask.1.refs_0_), channel_id=1, source_target_pairs={{2,0},{1,3},{6,4},{5,7},{10,8},{9,11},{14,12},{13,15},{18,16},{17,... | collective-permute-start | bytes 1081352 | tf_op jit(solution)/shard_map/ppermute | solution.py:259
  5.7 20.1 %collective-permute-start.3 = (bf16[11,128,128]{2,1,0:T(8,128)(2,1)S(1)}, bf16[11,128,128]{2,1,0:T(8,128)(2,1)S(1)}, u32[]{:S(2)}, u32[]{:S(2)}) collective-permute-start(bf16[11,128,128]{2,1,0:T(8,128)(2,1)S(1)} %mask.1.refs_0_), channel_id=1, source_target_pairs={{1,0},{2,1},{3,2},{0,3},{5,4},{6,5},{7,6},{4,7},{9,8},{10,9},{11,1... | collective-permute-start | bytes 1081352 | tf_op jit(solution)/shard_map/ppermute | solution.py:259
  10.8 15.4 %collective-permute-start.2 = (bf16[11,128,128]{2,1,0:T(8,128)(2,1)S(1)}, bf16[11,128,128]{2,1,0:T(8,128)(2,1)S(1)}, u32[]{:S(2)}, u32[]{:S(2)}) collective-permute-start(bf16[11,128,128]{2,1,0:T(8,128)(2,1)S(1)} %mask.1.refs_0_), channel_id=1, source_target_pairs={{0,24},{4,28},{8,16},{12,20},{16,8},{20,12},{24,0},{28,4},{1,25},{... | collective-permute-start | bytes 1081352 | tf_op jit(solution)/shard_map/ppermute | solution.py:23
  13.3 16.0 %collective-permute-start.1 = (bf16[11,128,128]{2,1,0:T(8,128)(2,1)S(1)}, bf16[11,128,128]{2,1,0:T(8,128)(2,1)S(1)}, u32[]{:S(2)}, u32[]{:S(2)}) collective-permute-start(bf16[11,128,128]{2,1,0:T(8,128)(2,1)S(1)} %mask.1.refs_0_), channel_id=1, source_target_pairs={{0,16},{4,20},{8,24},{12,28},{16,0},{20,4},{24,8},{28,12},{1,17},{... | collective-permute-start | bytes 1081352 | tf_op jit(solution)/shard_map/ppermute | solution.py:23
  13.8 15.6 %collective-permute-start = (bf16[11,128,128]{2,1,0:T(8,128)(2,1)S(1)}, bf16[11,128,128]{2,1,0:T(8,128)(2,1)S(1)}, u32[]{:S(2)}, u32[]{:S(2)}) collective-permute-start(bf16[11,128,128]{2,1,0:T(8,128)(2,1)S(1)} %mask.1.refs_0_), channel_id=1, source_target_pairs={{0,8},{4,12},{8,0},{12,4},{16,24},{20,28},{24,16},{28,20},{1,9},{5... | collective-permute-start | bytes 1081352 | tf_op jit(solution)/shard_map/ppermute | solution.py:23
  26.2 3.4 %copy-start = (bf16[8,128,128]{2,1,0:T(8,128)(2,1)S(1)}, bf16[8,128,128]{2,1,0:T(8,128)(2,1)}, u32[]{:S(2)}) copy-start(bf16[8,128,128]{2,1,0:T(8,128)(2,1)} %panel.5) | copy-start | bytes 786436
  26.2 3.4 %copy-start.1 = (bf16[1,4,8,1,128,128]{5,4,3,2,1,0:T(8,128)(2,1)S(1)}, bf16[1,4,8,1,128,128]{5,4,3,2,1,0:T(8,128)(2,1)}, u32[]{:S(2)}) copy-start(bf16[1,4,8,1,128,128]{5,4,3,2,1,0:T(8,128)(2,1)} %param.9) | copy-start | bytes 3145732
  29.5 3.3 %collective-permute-start.5 = (bf16[4,11,128,128]{3,2,1,0:T(8,128)(2,1)S(1)}, bf16[4,11,128,128]{3,2,1,0:T(8,128)(2,1)S(1)}, u32[]{:S(2)}, u32[]{:S(2)}) collective-permute-start(bf16[4,11,128,128]{3,2,1,0:T(8,128)(2,1)S(1)} %stack.21.near), channel_id=1, source_target_pairs={{0,4},{4,0},{8,12},{12,8},{16,20},{20,16},{24,28},{28,24},{1,5},{5... | collective-permute-start | bytes 4325384 | tf_op jit(solution)/shard_map/ppermute | solution.py:23
  30.0 2.8 %copy-start.6 = (s32[8]{0:T(128)S(1)}, s32[8]{0:T(128)}, u32[]{:S(2)}) copy-start(s32[8]{0:T(128)} %parents.5) | copy-start | bytes 100
  35.5 2.1 %collective-permute-start.6 = (f32[4,19,16,128]{3,2,1,0:T(8,128)S(1)}, f32[4,19,16,128]{3,2,1,0:T(8,128)S(1)}, u32[]{:S(2)}, u32[]{:S(2)}) collective-permute-start(f32[4,19,16,128]{3,2,1,0:T(8,128)S(1)} %get-tuple-element.33), channel_id=1, source_target_pairs={{0,4},{4,0},{8,12},{12,8},{16,20},{20,16},{24,28},{28,24},{1,5},{5... | collective-permute-start | bytes 1867784 | tf_op jit(solution)/shard_map/ppermute | solution.py:23
  37.7 49.6 %copy-start.8 = (s32[3,1,1]{0,2,1:T(1,128)S(1)}, s32[3,1,1]{0,2,1:T(1,128)}, u32[]{:S(2)}) copy-start(s32[3,1,1]{0,2,1:T(1,128)} %param.11) | copy-start | bytes 40
  37.7 49.5 %copy-start.10 = (s32[8,1,1]{0,2,1:T(1,128)S(1)}, s32[8,1,1]{0,2,1:T(1,128)}, u32[]{:S(2)}) copy-start(s32[8,1,1]{0,2,1:T(1,128)} %param.14) | copy-start | bytes 100
  37.7 7.4 %collective-permute-start.7 = (bf16[19,16,128]{2,1,0:T(8,128)(2,1)S(1)}, bf16[19,16,128]{2,1,0:T(8,128)(2,1)S(1)}, u32[]{:S(2)}, u32[]{:S(2)}) collective-permute-start(bf16[19,16,128]{2,1,0:T(8,128)(2,1)S(1)} %get-tuple-element.62), channel_id=1, source_target_pairs={{0,8},{4,12},{8,0},{12,4},{16,24},{20,28},{24,16},{28,20},{1,9},{5... | collective-permute-start | bytes 233480 | tf_op jit(solution)/shard_map/ppermute | solution.py:23
  39.3 5.8 %collective-permute-start.9 = (bf16[19,16,128]{2,1,0:T(8,128)(2,1)S(1)}, bf16[19,16,128]{2,1,0:T(8,128)(2,1)S(1)}, u32[]{:S(2)}, u32[]{:S(2)}) collective-permute-start(bf16[19,16,128]{2,1,0:T(8,128)(2,1)S(1)} %get-tuple-element.63), channel_id=1, source_target_pairs={{0,24},{4,28},{8,16},{12,20},{16,8},{20,12},{24,0},{28,4},{1,25},{... | collective-permute-start | bytes 233480 | tf_op jit(solution)/shard_map/ppermute | solution.py:23
  40.7 5.4 %collective-permute-start.8 = (bf16[19,16,128]{2,1,0:T(8,128)(2,1)S(1)}, bf16[19,16,128]{2,1,0:T(8,128)(2,1)S(1)}, u32[]{:S(2)}, u32[]{:S(2)}) collective-permute-start(bf16[19,16,128]{2,1,0:T(8,128)(2,1)S(1)} %get-tuple-element.64), channel_id=1, source_target_pairs={{0,16},{4,20},{8,24},{12,28},{16,0},{20,4},{24,8},{28,12},{1,17},{... | collective-permute-start | bytes 233480 | tf_op jit(solution)/shard_map/ppermute | solution.py:23
  41.3 24.2 %collective-permute-start.13 = (bf16[11,128,128]{2,1,0:T(8,128)(2,1)S(1)}, bf16[11,128,128]{2,1,0:T(8,128)(2,1)S(1)}, u32[]{:S(2)}, u32[]{:S(2)}) collective-permute-start(bf16[11,128,128]{2,1,0:T(8,128)(2,1)S(1)} %get-tuple-element.38), channel_id=1, source_target_pairs={{0,1},{1,2},{2,3},{3,0},{4,5},{5,6},{6,7},{7,4},{8,9},{9,10},{10,1... | collective-permute-start | bytes 1081352 | tf_op jit(solution)/shard_map/ppermute | solution.py:28
  42.6 23.0 %collective-permute-start.14 = (bf16[11,128,128]{2,1,0:T(8,128)(2,1)S(1)}, bf16[11,128,128]{2,1,0:T(8,128)(2,1)S(1)}, u32[]{:S(2)}, u32[]{:S(2)}) collective-permute-start(bf16[11,128,128]{2,1,0:T(8,128)(2,1)S(1)} %get-tuple-element.39), channel_id=1, source_target_pairs={{0,3},{1,0},{2,1},{3,2},{4,7},{5,4},{6,5},{7,6},{8,11},{9,8},{10,9... | collective-permute-start | bytes 1081352 | tf_op jit(solution)/shard_map/ppermute | solution.py:28
  46.1 17.8 %collective-permute-start.12 = (bf16[19,16,128]{2,1,0:T(8,128)(2,1)S(1)}, bf16[19,16,128]{2,1,0:T(8,128)(2,1)S(1)}, u32[]{:S(2)}, u32[]{:S(2)}) collective-permute-start(bf16[19,16,128]{2,1,0:T(8,128)(2,1)S(1)} %fusion.3.refs_0_), channel_id=1, source_target_pairs={{0,1},{1,2},{2,3},{3,0},{4,5},{5,6},{6,7},{7,4},{8,9},{9,10},{10,1... | collective-permute-start | bytes 233480 | tf_op jit(solution)/shard_map/ppermute | solution.py:28
  47.4 18.1 %collective-permute-start.11 = (bf16[19,16,128]{2,1,0:T(8,128)(2,1)S(1)}, bf16[19,16,128]{2,1,0:T(8,128)(2,1)S(1)}, u32[]{:S(2)}, u32[]{:S(2)}) collective-permute-start(bf16[19,16,128]{2,1,0:T(8,128)(2,1)S(1)} %fusion.3.refs_0_), channel_id=1, source_target_pairs={{0,2},{1,3},{2,0},{3,1},{4,6},{5,7},{6,4},{7,5},{8,10},{9,11},{10,... | collective-permute-start | bytes 233480 | tf_op jit(solution)/shard_map/ppermute | solution.py:28
  48.6 16.9 %collective-permute-start.10 = (bf16[19,16,128]{2,1,0:T(8,128)(2,1)S(1)}, bf16[19,16,128]{2,1,0:T(8,128)(2,1)S(1)}, u32[]{:S(2)}, u32[]{:S(2)}) collective-permute-start(bf16[19,16,128]{2,1,0:T(8,128)(2,1)S(1)} %fusion.3.refs_0_), channel_id=1, source_target_pairs={{0,3},{1,0},{2,1},{3,2},{4,7},{5,4},{6,5},{7,6},{8,11},{9,8},{10,9... | collective-permute-start | bytes 233480 | tf_op jit(solution)/shard_map/ppermute | solution.py:28
  65.6 23.2 %copy-start.2 = (f32[8,128,128]{2,1,0:T(8,128)S(1)}, f32[8,128,128]{2,1,0:T(8,128)}, u32[]{:S(2)}) copy-start(f32[8,128,128]{2,1,0:T(8,128)} %lower_diagonal.1) | copy-start | bytes 1572868
  65.6 23.2 %copy-start.4 = (f32[3,128,128]{2,1,0:T(8,128)S(1)}, f32[3,128,128]{2,1,0:T(8,128)}, u32[]{:S(2)}) copy-start(f32[3,128,128]{2,1,0:T(8,128)} %upper_diagonal.1) | copy-start | bytes 589828
  65.6 5.6 %collective-permute-start.18 = (bf16[19,16,128]{2,1,0:T(8,128)(2,1)S(1)}, bf16[19,16,128]{2,1,0:T(8,128)(2,1)S(1)}, u32[]{:S(2)}, u32[]{:S(2)}) collective-permute-start(bf16[19,16,128]{2,1,0:T(8,128)(2,1)S(1)} %line.1), channel_id=1, source_target_pairs={{0,24},{4,28},{8,16},{12,20},{16,8},{20,12},{24,0},{28,4},{1,25},{... | collective-permute-start | bytes 233480 | tf_op jit(solution)/shard_map/ppermute | solution.py:23
  67.4 5.1 %collective-permute-start.17 = (bf16[19,16,128]{2,1,0:T(8,128)(2,1)S(1)}, bf16[19,16,128]{2,1,0:T(8,128)(2,1)S(1)}, u32[]{:S(2)}, u32[]{:S(2)}) collective-permute-start(bf16[19,16,128]{2,1,0:T(8,128)(2,1)S(1)} %line.1), channel_id=1, source_target_pairs={{0,16},{4,20},{8,24},{12,28},{16,0},{20,4},{24,8},{28,12},{1,17},{... | collective-permute-start | bytes 233480 | tf_op jit(solution)/shard_map/ppermute | solution.py:23
  68.7 4.4 %collective-permute-start.16 = (bf16[19,16,128]{2,1,0:T(8,128)(2,1)S(1)}, bf16[19,16,128]{2,1,0:T(8,128)(2,1)S(1)}, u32[]{:S(2)}, u32[]{:S(2)}) collective-permute-start(bf16[19,16,128]{2,1,0:T(8,128)(2,1)S(1)} %line.1), channel_id=1, source_target_pairs={{0,8},{4,12},{8,0},{12,4},{16,24},{20,28},{24,16},{28,20},{1,9},{5... | collective-permute-start | bytes 233480 | tf_op jit(solution)/shard_map/ppermute | solution.py:23
  69.2 18.0 %collective-permute-start.15 = (bf16[11,128,128]{2,1,0:T(8,128)(2,1)S(1)}, bf16[11,128,128]{2,1,0:T(8,128)(2,1)S(1)}, u32[]{:S(2)}, u32[]{:S(2)}) collective-permute-start(bf16[11,128,128]{2,1,0:T(8,128)(2,1)S(1)} %get-tuple-element.47), channel_id=1, source_target_pairs={{0,2},{1,3},{2,0},{3,1},{4,6},{5,7},{6,4},{7,5},{8,10},{9,11},{10,... | collective-permute-start | bytes 1081352 | tf_op jit(solution)/shard_map/ppermute | solution.py:28
  73.1 15.7 %collective-permute-start.19 = (bf16[4,19,16,128]{3,2,1,0:T(8,128)(2,1)S(1)}, bf16[4,19,16,128]{3,2,1,0:T(8,128)(2,1)S(1)}, u32[]{:S(2)}, u32[]{:S(2)}) collective-permute-start(bf16[4,19,16,128]{3,2,1,0:T(8,128)(2,1)S(1)} %pad_maximum_fusion.near), channel_id=1, source_target_pairs={{0,4},{4,0},{8,12},{12,8},{16,20},{20,16},{24,28},{28,24},{1,5},{5... | collective-permute-start | bytes 933896 | tf_op jit(solution)/shard_map/ppermute | solution.py:23
